TPU v7x, 32 devices: a whole 2x2x4 slice. The times are simulated.
32 devices in a mesh: img: 2 (over x), ty: 4 (over y, core), tx: 4 (over z).
Axes of the slice: x: 2, y: 2, z: 4, core: 2. Of those that a mesh axis runs over, the one named last changes fastest.
Arguments:
- tokens: bfloat16 [2, 2048, 1152], P('img', ('ty', 'tx')), may hold values from -6 to 6
- cotangent: bfloat16 [2, 2048, 1152], P('img', ('ty', 'tx')), may hold values from -6 to 6
- class_embed: float32 [2, 1152], P('img'), may hold values from -6 to 6
- timestep: int32 [2], P('img'), may hold values from 0 to 999
- grid_height: int32 [2], P('img'), may hold values from 16 to 32, as said below
- grid_width: int32 [2], P('img'), may hold values from 32 to 64, as said below
- qkv_weight: bfloat16 [1152, 3456], P('img'), may hold values from -0.1875 to 0.1875
- out_weight: bfloat16 [1152, 1152], P('img'), may hold values from -3 to 3
- up_weight: bfloat16 [1152, 6144], P('img'), may hold values from -0.1875 to 0.1875
- down_weight: bfloat16 [3072, 1152], P('img'), may hold values from -0.109375 to 0.109375
- ada_weight: bfloat16 [6912, 1152], P(('img', 'ty', 'tx')), may hold values from -0.1875 to 0.1875
- q_gain: float32 [72], replicated, may hold values from 0.1 to 1.9
- k_gain: float32 [72], replicated, may hold values from 0.1 to 1.9
Outputs:
- mixed: bfloat16 [2, 2048, 1152], P('img', ('ty', 'tx'))
- tokens_grad: bfloat16 [2, 2048, 1152], P('img', ('ty', 'tx'))
- qkv_grad: float32 [1152, 3456], P('img', ('ty', 'tx'))
- out_grad: float32 [1152, 1152], P('img', ('ty', 'tx'))
- up_grad: float32 [1152, 6144], P('img', ('ty', 'tx'))
- down_grad: float32 [3072, 1152], P('img', ('ty', 'tx'))
- ada_grad: float32 [6912, 1152], P(('img', 'ty', 'tx'))
- q_gain_grad: float32 [72], replicated
- k_gain_grad: float32 [72], replicated
Inputs may be any that keep to these rules, and one draw needn't show every extreme that they name: `grid_height`: one image, drawn from the seed, has the full grid of 32 by 64 patches; the others are shorter. `grid_width`: as for grid_height; the full image is the same one, and the others are narrower.
All inputs are finite; a program needn't handle non-finite values.
Results may differ from a plain program's by a relative error of at most 0.02.
Values may be sent and summed in bfloat16 or wider, within the bound.
A program may use at most 192 MiB of HBM per device.

v0:
```python
import jax
import jax.numpy as jnp
from jax import lax
from jax.sharding import PartitionSpec as P

HEADS = 16
HEAD = 72


EPS = 1e-06
HIGH = lax.Precision.HIGHEST


def layout(slot, height, width, cap, rows_tiles, cols_tiles):
    tile = slot // cap
    row_tile = tile // cols_tiles
    col_tile = tile % cols_tiles
    local = slot % cap
    top = row_tile * height // rows_tiles
    bottom = (row_tile + 1) * height // rows_tiles
    left = col_tile * width // cols_tiles
    right = (col_tile + 1) * width // cols_tiles
    span = right - left
    valid = local < (bottom - top) * span
    row = jnp.where(valid, top + local // span, 0)
    col = jnp.where(valid, left + local % span, 0)
    return (valid, row, col)


def time_embed(step, dim):
    half = dim // 2
    freq = jnp.exp(-jnp.log(10000.0) * jnp.arange(half, dtype=jnp.float32) / half)
    angle = step.astype(jnp.float32)[:, None] * freq
    return jnp.concatenate([jnp.cos(angle), jnp.sin(angle)], axis=-1)


def rotate(part, position):
    quarter = part.shape[-1] // 2
    freq = jnp.exp(-jnp.log(10000.0) * jnp.arange(quarter, dtype=jnp.float32) / quarter)
    angle = position.astype(jnp.float32)[..., None, None] * freq
    first, second = (part[..., :quarter], part[..., quarter:])
    cosine, sine = (jnp.cos(angle), jnp.sin(angle))
    return jnp.concatenate(
        [first * cosine - second * sine, second * cosine + first * sine], axis=-1
    )


def rope(heads, row, col):
    half = heads.shape[-1] // 2
    return jnp.concatenate(
        [rotate(heads[..., :half], row), rotate(heads[..., half:], col)], axis=-1
    )


def head_norm(value, gain):
    return value * lax.rsqrt(jnp.mean(value * value, axis=-1, keepdims=True) + EPS) * gain


def rms(value):
    return value * lax.rsqrt(jnp.mean(value * value, axis=-1, keepdims=True) + EPS)


def flat_rows(value):
    return value.reshape(-1, value.shape[-1])


def outer_sum(left, right):
    return lax.dot_general(
        flat_rows(left),
        flat_rows(right),
        (((0,), (0,)), ((), ())),
        preferred_element_type=jnp.float32,
    )


def times_transposed(left, weight):
    return lax.dot_general(
        left, weight, (((left.ndim - 1,), (1,)), ((), ())), preferred_element_type=jnp.float32
    )


def masked_scores(query, keys_all, key_valid):
    scores = jnp.einsum("qhd,khd->hqk", query, keys_all, preferred_element_type=jnp.float32)
    return jnp.where(key_valid[None, None, :], scores, -1e30)


def body(
    tokens,
    cotangent,
    class_embed,
    timestep,
    grid_height,
    grid_width,
    qkv_weight,
    out_weight,
    up_weight,
    down_weight,
    ada_weight,
    q_gain,
    k_gain,
):
    images, slots_dev, width = tokens.shape
    rows_tiles = lax.axis_size("ty")
    cols_tiles = lax.axis_size("tx")
    slots_all = slots_dev * rows_tiles * cols_tiles
    own_slot = lax.axis_index(("ty", "tx")) * slots_dev + jnp.arange(slots_dev, dtype=jnp.int32)
    all_slot = jnp.arange(slots_all, dtype=jnp.int32)
    valid_q, row_q, col_q = jax.vmap(
        lambda h, w: layout(own_slot, h, w, slots_dev, rows_tiles, cols_tiles)
    )(grid_height, grid_width)
    valid_k = jax.vmap(lambda h, w: layout(all_slot, h, w, slots_dev, rows_tiles, cols_tiles)[0])(
        grid_height, grid_width
    )
    keep = valid_q.astype(jnp.float32)[..., None]
    act = jax.nn.silu(class_embed + time_embed(timestep, width)).astype(jnp.bfloat16)
    mod = lax.dot_general(
        act,
        lax.all_gather(ada_weight, ("img", "ty", "tx"), axis=0, tiled=True),
        (((1,), (1,)), ((), ())),
        preferred_element_type=jnp.float32,
    )
    shift1, scale1, gate1, shift2, scale2, gate2 = [
        part[:, None, :] for part in jnp.split(mod, 6, axis=1)
    ]
    wqkv, wout, w12, w3 = (
        lax.all_gather(qkv_weight, "img", axis=0, tiled=True),
        lax.all_gather(out_weight, "img", axis=0, tiled=True),
        lax.all_gather(up_weight, "img", axis=0, tiled=True),
        lax.all_gather(down_weight, "img", axis=0, tiled=True),
    )
    xf = tokens.astype(jnp.float32)
    norm1, pull_norm1 = jax.vjp(rms, xf)
    h1 = (norm1 * (1.0 + scale1) + shift1).astype(jnp.bfloat16)
    qkv = jnp.dot(h1, wqkv, preferred_element_type=jnp.float32).reshape(
        images, slots_dev, 3, HEADS, HEAD
    )

    def finish(query_raw, key_raw, query_gain, key_gain):
        query = rope(head_norm(query_raw, query_gain), row_q, col_q) * HEAD ** (-0.5)
        return (query, rope(head_norm(key_raw, key_gain), row_q, col_q))

    (query_f, key_f), pull_heads = jax.vjp(finish, qkv[:, :, 0], qkv[:, :, 1], q_gain, k_gain)
    query_b = query_f.astype(jnp.bfloat16)
    key_b = key_f.astype(jnp.bfloat16)
    value_b = qkv[:, :, 2].astype(jnp.bfloat16)
    keys_all, values_all = (
        lax.all_gather(key_b, ("ty", "tx"), axis=1, tiled=True),
        lax.all_gather(value_b, ("ty", "tx"), axis=1, tiled=True),
    )
    index = 0
    scores = masked_scores(query_b[index], keys_all[index], valid_k[index])
    top = jnp.max(scores, axis=-1, keepdims=True)
    lse = top + jnp.log(jnp.sum(jnp.exp(scores - top), axis=-1, keepdims=True))
    prob = jnp.exp(scores - lse).astype(jnp.bfloat16)
    attn_list = [
        jnp.einsum("hqk,khd->qhd", prob, values_all[index], preferred_element_type=jnp.float32)
    ]
    lse_list = [lse]
    attn = jnp.stack(attn_list).reshape(images, slots_dev, width).astype(jnp.bfloat16)
    branch = jnp.dot(attn, wout, preferred_element_type=jnp.float32)
    x1 = xf + keep * gate1 * branch
    norm2, pull_norm2 = jax.vjp(rms, x1)
    h2 = (norm2 * (1.0 + scale2) + shift2).astype(jnp.bfloat16)
    gate_up = jnp.dot(h2, w12, preferred_element_type=jnp.float32)
    hidden = gate_up.shape[-1] // 2
    gate_part, up_part = (gate_up[..., :hidden], gate_up[..., hidden:])
    sig = jax.nn.sigmoid(gate_part)
    silu_gate = gate_part * sig
    mid = (silu_gate * up_part).astype(jnp.bfloat16)
    ffn = jnp.dot(mid, w3, preferred_element_type=jnp.float32)
    mixed = (x1 + keep * gate2 * ffn).astype(jnp.bfloat16)
    grad_out = cotangent.astype(jnp.float32)
    d_gate2 = jnp.sum(grad_out * keep * ffn, axis=1)
    d_ffn = (grad_out * keep * gate2).astype(jnp.bfloat16)
    term_down = outer_sum(mid, d_ffn)
    d_mid = times_transposed(d_ffn, w3)
    d_gate = d_mid * up_part * (sig + gate_part * sig * (1.0 - sig))
    d_up = d_mid * silu_gate
    d_gate_up = jnp.concatenate([d_gate, d_up], axis=-1).astype(jnp.bfloat16)
    term_up = outer_sum(h2, d_gate_up)
    d_h2 = times_transposed(d_gate_up, w12)
    d_scale2 = jnp.sum(d_h2 * norm2, axis=1)
    d_shift2 = jnp.sum(d_h2, axis=1)
    d_x1 = grad_out + pull_norm2(d_h2 * (1.0 + scale2))[0]
    d_gate1 = jnp.sum(d_x1 * keep * branch, axis=1)
    d_branch = (d_x1 * keep * gate1).astype(jnp.bfloat16)
    term_out = outer_sum(attn, d_branch)
    d_attn = (
        times_transposed(d_branch, wout)
        .astype(jnp.bfloat16)
        .reshape(images, slots_dev, HEADS, HEAD)
    )
    keys_back, values_back = (
        lax.all_gather(key_b, ("ty", "tx"), axis=1, tiled=True),
        lax.all_gather(value_b, ("ty", "tx"), axis=1, tiled=True),
    )
    index = 0
    scores = masked_scores(query_b[index], keys_back[index], valid_k[index])
    prob = jnp.exp(scores - lse_list[index])
    d_prob = jnp.einsum(
        "qhd,khd->hqk", d_attn[index], values_back[index], preferred_element_type=jnp.float32
    )
    delta = jnp.sum(prob * d_prob, axis=-1, keepdims=True)
    d_scores = (prob * (d_prob - delta)).astype(jnp.bfloat16)
    dq_list = [
        jnp.einsum("hqk,khd->qhd", d_scores, keys_back[index], preferred_element_type=jnp.float32)
    ]
    dk_list = [
        jnp.einsum("hqk,qhd->khd", d_scores, query_b[index], preferred_element_type=jnp.float32)
    ]
    dv_list = [
        jnp.einsum(
            "hqk,qhd->khd",
            prob.astype(jnp.bfloat16),
            d_attn[index],
            preferred_element_type=jnp.float32,
        )
    ]
    d_key, d_value = (
        lax.psum_scatter(
            jnp.stack(dk_list).astype(jnp.bfloat16), ("ty", "tx"), scatter_dimension=1, tiled=True
        ).astype(jnp.float32),
        lax.psum_scatter(
            jnp.stack(dv_list).astype(jnp.bfloat16), ("ty", "tx"), scatter_dimension=1, tiled=True
        ).astype(jnp.float32),
    )
    d_query_raw, d_key_raw, d_q_gain, d_k_gain = pull_heads((jnp.stack(dq_list), d_key))
    d_qkv = (
        jnp.stack([d_query_raw, d_key_raw, d_value], axis=2)
        .reshape(images, slots_dev, 3 * width)
        .astype(jnp.bfloat16)
    )
    term_qkv = outer_sum(h1, d_qkv)
    d_h1 = times_transposed(d_qkv, wqkv)
    d_scale1 = jnp.sum(d_h1 * norm1, axis=1)
    d_shift1 = jnp.sum(d_h1, axis=1)
    tokens_grad = (d_x1 + pull_norm1(d_h1 * (1.0 + scale1))[0]).astype(jnp.bfloat16)
    d_mod = jnp.concatenate([d_shift1, d_scale1, d_gate1, d_shift2, d_scale2, d_gate2], axis=1)
    act_f = act.astype(jnp.float32)
    ada_grad = lax.psum_scatter(
        lax.dot_general(
            d_mod,
            act_f,
            (((0,), (0,)), ((), ())),
            precision=HIGH,
            preferred_element_type=jnp.float32,
        ),
        ("img", "ty", "tx"),
        scatter_dimension=0,
        tiled=True,
    )
    q_gain_grad, k_gain_grad = lax.psum((d_q_gain, d_k_gain), ("img", "ty", "tx"))
    parts = (
        lax.psum_scatter(
            term_qkv.astype(jnp.bfloat16), ("ty", "tx"), scatter_dimension=1, tiled=True
        ).astype(jnp.float32),
        lax.psum_scatter(
            term_out.astype(jnp.bfloat16), ("ty", "tx"), scatter_dimension=1, tiled=True
        ).astype(jnp.float32),
        lax.psum_scatter(
            term_up.astype(jnp.bfloat16), ("ty", "tx"), scatter_dimension=1, tiled=True
        ).astype(jnp.float32),
        lax.psum_scatter(
            term_down.astype(jnp.bfloat16), ("ty", "tx"), scatter_dimension=1, tiled=True
        ).astype(jnp.float32),
    )
    grads = (
        lax.psum_scatter(
            parts[0].astype(jnp.bfloat16), "img", scatter_dimension=0, tiled=True
        ).astype(jnp.float32),
        lax.psum_scatter(
            parts[1].astype(jnp.bfloat16), "img", scatter_dimension=0, tiled=True
        ).astype(jnp.float32),
        lax.psum_scatter(
            parts[2].astype(jnp.bfloat16), "img", scatter_dimension=0, tiled=True
        ).astype(jnp.float32),
        lax.psum_scatter(
            parts[3].astype(jnp.bfloat16), "img", scatter_dimension=0, tiled=True
        ).astype(jnp.float32),
    )
    return (
        mixed,
        tokens_grad,
        grads[0],
        grads[1],
        grads[2],
        grads[3],
        ada_grad,
        q_gain_grad,
        k_gain_grad,
    )


def solution(mesh):
    in_specs = (
        P("img", ("ty", "tx"), None),
        P("img", ("ty", "tx"), None),
        P("img", None),
        P("img"),
        P("img"),
        P("img"),
        P("img", None),
        P("img", None),
        P("img", None),
        P("img", None),
        P(("img", "ty", "tx"), None),
        P(),
        P(),
    )
    out_specs = (
        P("img", ("ty", "tx"), None),
        P("img", ("ty", "tx"), None),
        P("img", ("ty", "tx")),
        P("img", ("ty", "tx")),
        P("img", ("ty", "tx")),
        P("img", ("ty", "tx")),
        P(("img", "ty", "tx"), None),
        P(),
        P(),
    )
    return jax.shard_map(body, mesh=mesh, in_specs=in_specs, out_specs=out_specs, check_vma=False)
```

profile of v0, /device:TPU:0, one launch (start us, length us, event | category | flops | bytes accessed | tf_op | source)
XLA Modules:
  0.0 1685.4 jit_solution(16327587392667890537)
XLA Ops:
  14.1 97.3 %all-gather.11.cloned.1.call-done = bf16[1152,3456]{1,0:T(8,128)(2,1)} async-done(((bf16[576,3456]{1,0:T(8,128)(2,1)}), bf16[1152,3456]{1,0:T(8,128)(2,1)}) %all-gather.11.cloned.1.call-update) | async-done | bytes 7962640 | tf_op jit(solution)/shard_map/all_gather | solution.py:126
  111.5 11.4 copy.27
  122.9 102.4 %all-gather.9.cloned.1.call-done = bf16[6912,1152]{1,0:T(8,128)(2,1)} async-done(((bf16[216,1152]{1,0:T(8,128)(2,1)}), bf16[6912,1152]{1,0:T(8,128)(2,1)}) %all-gather.9.cloned.1.call-update) | async-done | bytes 15925264 | tf_op jit(solution)/shard_map/all_gather | solution.py:118
  247.7 50.2 %all-gather.13.cloned.1.call-done = bf16[1,2048,16,72]{1,3,2,0:T(8,128)(2,1)} async-done(((bf16[1,128,16,72]{1,3,2,0:T(8,128)(2,1)}), bf16[1,2048,16,72]{1,3,2,0:T(8,128)(2,1)}) %all-gather.13.cloned.1.call-update) | async-done | bytes 4718608 | tf_op jit(solution)/shard_map/all_gather | solution.py:147
  308.4 46.3 %all-gather.21.cloned.1.call-done = bf16[1,2048,1,16,72]{1,4,3,2,0:T(8,128)(2,1)} async-done(((bf16[1,128,1,16,72]{1,4,3,2,0:T(8,128)(2,1)}), bf16[1,2048,1,16,72]{1,4,3,2,0:T(8,128)(2,1)}) %all-gather.21.cloned.1.call-update) | async-done | bytes 4718608 | tf_op jit(solution)/shard_map/all_gather | solution.py:148
  365.8 27.8 %all-gather.15.cloned.1.call-done = bf16[1152,1152]{1,0:T(8,128)(2,1)} async-done(((bf16[576,1152]{1,0:T(8,128)(2,1)}), bf16[1152,1152]{1,0:T(8,128)(2,1)}) %all-gather.15.cloned.1.call-update) | async-done | bytes 2654224 | tf_op jit(solution)/shard_map/all_gather | solution.py:127
  396.9 168.0 %all-gather.17.cloned.1.call-done = bf16[1152,6144]{1,0:T(8,128)(2,1)} async-done(((bf16[576,6144]{1,0:T(8,128)(2,1)}), bf16[1152,6144]{1,0:T(8,128)(2,1)}) %all-gather.17.cloned.1.call-update) | async-done | bytes 14155792 | tf_op jit(solution)/shard_map/all_gather | solution.py:128
  573.9 81.8 %all-gather.19.cloned.1.call-done = bf16[3072,1152]{1,0:T(8,128)(2,1)} async-done(((bf16[1536,1152]{1,0:T(8,128)(2,1)}), bf16[3072,1152]{1,0:T(8,128)(2,1)}) %all-gather.19.cloned.1.call-update) | async-done | bytes 7077904 | tf_op jit(solution)/shard_map/all_gather | solution.py:129
  663.5 11.7 fusion.40
  682.5 11.5 convert_bitcast_fusion
  693.9 11.6 copy.32
  705.6 13.8 reshape.1293
  719.4 13.2 multiply_reduce_fusion
  732.7 13.3 multiply_convert_fusion
  752.9 11.6 copy.30
  764.5 13.9 reshape.1291
  799.5 74.6 %reduce-scatter.34.cloned.1.call-done = bf16[128,1152]{1,0:T(8,128)(2,1)} async-done(((bf16[2048,1152]{1,0:T(8,128)(2,1)}), bf16[128,1152]{1,0:T(8,128)(2,1)}) %reduce-scatter.34.cloned.1.call-update) | async-done | bytes 294928
  899.8 17.9 %copy.38 = bf16[1152,6144]{0,1:T(8,128)(2,1)} copy(bf16[1152,6144]{1,0:T(8,128)(2,1)} %convolution_convert_fusion) | data formatting | bytes 28311552
  917.8 23.0 %reduce-scatter.46.cloned.1.call-done = bf16[1152,72]{0,1:T(8,128)(2,1)} async-done(((bf16[1152,1152]{0,1:T(8,128)(2,1)}), bf16[1152,72]{0,1:T(8,128)(2,1)}) %reduce-scatter.46.cloned.1.call-update) | async-done | bytes 165904
  942.7 91.6 %reduce-scatter.30.cloned.1.call-done = bf16[3072,72]{0,1:T(8,128)(2,1)} async-done(((bf16[3072,1152]{0,1:T(8,128)(2,1)}), bf16[3072,72]{0,1:T(8,128)(2,1)}) %reduce-scatter.30.cloned.1.call-update) | async-done | bytes 442384 | tf_op jit(solution)/shard_map/reduce_scatter | solution.py:263
  1040.4 98.2 %reduce-scatter.44.cloned.1.call-done = bf16[1152,216]{0,1:T(8,128)(2,1)} async-done(((bf16[1152,3456]{0,1:T(8,128)(2,1)}), bf16[1152,216]{0,1:T(8,128)(2,1)}) %reduce-scatter.44.cloned.1.call-update) | async-done | bytes 497680
  1140.9 147.9 %reduce-scatter.42.cloned.1.call-done = bf16[384,1152]{1,0:T(8,128)(2,1)} async-done(((bf16[6144,1152]{1,0:T(8,128)(2,1)}), bf16[384,1152]{1,0:T(8,128)(2,1)}) %reduce-scatter.42.cloned.1.call-update) | async-done | bytes 884752
  1304.4 39.4 %all-reduce.15 = (f32[72]{0:T(128)}, f32[72]{0:T(128)}) all-reduce(f32[72]{0:T(128)S(1)} %get-tuple-element.14, f32[72]{0:T(128)S(1)} %get-tuple-element.9), channel_id=1, replica_groups=mesh['img'=2,'ty'=4,'tx'=4] {'img','ty','tx'}, use_global_device_ids=true, to_apply=%region_29.30 | all-reduce | flops 144 | bytes 1152 | tf_op jit(solution)/shard_map/psum | solution.py:252
  1359.5 318.6 %reduce-scatter.48.cloned.1.call-done = f32[216,1152]{1,0:T(8,128)} async-done(((f32[6912,1152]{1,0:T(8,128)}), f32[216,1152]{1,0:T(8,128)}) %reduce-scatter.48.cloned.1.call-update) | async-done | bytes 995344
  (242 shorter events, 170.9 us)
Async XLA Ops:
  7.2 104.3 %all-gather.11.cloned.1.call-start = ((), (), s32[]{:S(2)}) async-start(), calls=%async_computation.12 | async-start | bytes 11943936 | tf_op jit(solution)/shard_map/all_gather | solution.py:126
  7.9 217.5 %all-gather.9.cloned.1.call-start = ((), (), s32[]{:S(2)}) async-start(), calls=%async_computation.11 | async-start | bytes 16422912 | tf_op jit(solution)/shard_map/all_gather | solution.py:118
  8.7 289.2 %all-gather.13.cloned.1.call-start = ((), (), s32[]{:S(2)}) async-start(), calls=%async_computation.13 | async-start | bytes 5013504 | tf_op jit(solution)/shard_map/all_gather | solution.py:147
  243.6 111.1 %all-gather.21.cloned.1.call-start = ((), (), s32[]{:S(2)}) async-start(), calls=%async_computation.20 | async-start | bytes 5013504 | tf_op jit(solution)/shard_map/all_gather | solution.py:148
  245.5 148.2 %all-gather.15.cloned.1.call-start = ((), (), s32[]{:S(2)}) async-start(), calls=%async_computation.14 | async-start | bytes 3981312 | tf_op jit(solution)/shard_map/all_gather | solution.py:127
  246.1 318.8 %all-gather.17.cloned.1.call-start = ((), (), s32[]{:S(2)}) async-start(), calls=%async_computation.15 | async-start | bytes 21233664 | tf_op jit(solution)/shard_map/all_gather | solution.py:128
  246.6 409.1 %all-gather.19.cloned.1.call-start = ((), (), s32[]{:S(2)}) async-start(), calls=%async_computation.16 | async-start | bytes 10616832 | tf_op jit(solution)/shard_map/all_gather | solution.py:129
  247.4 548.0 %reduce-scatter.36.cloned.1.call-start = ((), (), s32[]{:S(2)}) async-start(), calls=%async_computation.22 | async-start | bytes 5013504
  247.5 408.2 %copy-start.50 = (f32[128]{0:T(128)}, f32[128]{0:T(128)S(1)}, u32[]{:S(2)}) copy-start(f32[128]{0:T(128)S(1)} %fusion.88) | copy-start | bytes 1540
  308.3 256.5 %copy-start.29 = (f32[1152]{0:T(1024)S(1)}, f32[1152]{0:T(1024)}, u32[]{:S(2)}) copy-start(f32[1152]{0:T(1024)} %get-tuple-element.26) | copy-start | bytes 13828
  365.8 208.1 %copy-start.22 = (bf16[16,72,128]{2,1,0:T(8,128)(2,1)}, bf16[16,72,128]{2,1,0:T(8,128)(2,1)S(1)}, u32[]{:S(2)}) copy-start(bf16[16,72,128]{2,1,0:T(8,128)(2,1)S(1)} %fusion.15) | copy-start | bytes 884740
  719.4 154.7 %reduce-scatter.34.cloned.1.call-start = ((), (), s32[]{:S(2)}) async-start(), calls=%async_computation.21 | async-start | bytes 5013504
  778.5 162.3 %reduce-scatter.46.cloned.1.call-start = ((), (), s32[]{:S(2)}) async-start(), calls=%async_computation.27 | async-start | bytes 2820096
  781.3 252.9 %reduce-scatter.30.cloned.1.call-start = ((), (), s32[]{:S(2)}) async-start(), calls=%async_computation.18 | async-start | bytes 7520256 | tf_op jit(solution)/shard_map/reduce_scatter | solution.py:263
  786.4 352.2 %reduce-scatter.44.cloned.1.call-start = ((), (), s32[]{:S(2)}) async-start(), calls=%async_computation.26 | async-start | bytes 8460288
  890.9 397.8 %reduce-scatter.42.cloned.1.call-start = ((), (), s32[]{:S(2)}) async-start(), calls=%async_computation.25 | async-start | bytes 15040512
  917.8 223.0 %copy-start.49 = (f32[1152]{0:T(1024)S(1)}, f32[1152]{0:T(1024)}, u32[]{:S(2)}) copy-start(f32[1152]{0:T(1024)} %get-tuple-element.28) | copy-start | bytes 13828
  917.8 223.0 %copy-start.47 = (f32[1152]{0:T(1024)S(1)}, f32[1152]{0:T(1024)}, u32[]{:S(2)}) copy-start(f32[1152]{0:T(1024)} %get-tuple-element.17) | copy-start | bytes 13828
  917.8 223.0 %copy-start.48 = (f32[1152]{0:T(1024)S(1)}, f32[1152]{0:T(1024)}, u32[]{:S(2)}) copy-start(f32[1152]{0:T(1024)} %get-tuple-element.27) | copy-start | bytes 13828
  917.8 384.8 %reduce-scatter.40.cloned.1.call-start = ((), (), s32[]{:S(2)}) async-start(), calls=%async_computation.24 | async-start | bytes 442368
  942.6 402.1 %reduce-scatter.32.cloned.1.call-start = ((), (), s32[]{:S(2)}) async-start(), calls=%async_computation.19 | async-start | bytes 663552 | tf_op jit(solution)/shard_map/reduce_scatter | solution.py:277
  1034.3 312.2 %reduce-scatter.38.cloned.1.call-start = ((), (), s32[]{:S(2)}) async-start(), calls=%async_computation.23 | async-start | bytes 884736
  1140.7 216.9 %reduce-scatter.28.cloned.1.call-start = ((), (), s32[]{:S(2)}) async-start(), calls=%async_computation.17 | async-start | bytes 1327104 | tf_op jit(solution)/shard_map/reduce_scatter | solution.py:274
  1291.0 387.1 %reduce-scatter.48.cloned.1.call-start = ((), (), s32[]{:S(2)}) async-start(), calls=%async_computation.28 | async-start | bytes 32845824
  (56 other events, 2053.8 us)
Sparse Core Ops, SparseCore 0:
  9.5 101.8 all-gather.10
  114.3 110.9 all-gather.8
  243.7 54.1 all-gather.12
  300.4 54.1 all-gather.20
  356.0 37.5 all-gather.14
  395.0 169.8 all-gather.16
  566.4 89.2 all-gather.18
  719.5 75.5 reduce-scatter.35
  799.4 74.5 reduce-scatter.33
  877.8 62.9 reduce-scatter.45
  945.3 88.8 reduce-scatter.29
  1038.2 100.3 reduce-scatter.43
  1143.3 145.4 reduce-scatter.41
  1291.5 11.0 reduce-scatter.39
  1304.8 13.8 reduce-scatter.31
  1320.8 15.3 reduce-scatter.37
  1339.0 18.5 reduce-scatter.27
  1365.5 312.5 reduce-scatter.47
where the time goes:
time: 1690 us
  waiting for transfers between devices  1340 us (79%)
  matrix products  131 us (8%)
  local copies, waits for them, and re-layouts  108 us (6%)
  other arithmetic  48 us (3%)
  blocking collectives  39.4 us (2%)
  between operations  17.5 us (1%)
    unnamed x26, waiting for transfers between devices  666 us
    all_gather x1, waiting for transfers between devices, body(): lax.all_gather(up_weight, 'img', axis=0, tiled=True)  168 us
    all_gather x1, waiting for transfers between devices, body(): lax.all_gather(ada_weight, ('img', 'ty', 'tx'), axis=0, tiled=True)  102 us
    all_gather x1, waiting for transfers between devices, body(): lax.all_gather(qkv_weight, 'img', axis=0, tiled=True)  97.3 us
    unnamed x143, local copies, waits for them, and re-layouts  94.2 us
    reduce_scatter x1, waiting for transfers between devices, body(): lax.psum_scatter(term_down.astype(jnp.bfloat16), ('ty', 'tx'), scatter_di...  91.6 us
    all_gather x1, waiting for transfers between devices, body(): lax.all_gather(down_weight, 'img', axis=0, tiled=True)  81.8 us
    all_gather x1, waiting for transfers between devices, body(): lax.all_gather(key_b, ('ty', 'tx'), axis=1, tiled=True)  50.2 us
  transfers between devices with their start and end apart: 18, of which 15 were waited for; matrix products, arithmetic and copies ran while one was open for 12% of the time, Pallas kernels for 0%

commit v1 on v0

--- a/solution.py
+++ b/solution.py
@@ -1,6 +1,11 @@
+import functools
+
 import jax
 import jax.numpy as jnp
+import numpy as np
 from jax import lax
+from jax.experimental import pallas as pl
+from jax.experimental.pallas import tpu as pltpu
 from jax.sharding import PartitionSpec as P
 
 HEADS = 16
@@ -84,7 +89,7 @@
     return jnp.where(key_valid[None, None, :], scores, -1e30)
 
 
-def body(
+def general_body(
     tokens,
     cotangent,
     class_embed,
@@ -291,6 +296,856 @@
     )
 
 
+VMEM_LIMIT = 63 << 20
+MESH = pl.DeviceIdType.MESH
+PAD = 128
+TILE = 128
+F32 = jnp.float32
+BF16 = jnp.bfloat16
+
+
+def dot(a, b):
+    return lax.dot_general(a, b, (((1,), (0,)), ((), ())), preferred_element_type=F32)
+
+
+def dot_nt(a, b):
+    return lax.dot_general(a, b, (((1,), (1,)), ((), ())), preferred_element_type=F32)
+
+
+def dot_tn(a, b, precision=None):
+    return lax.dot_general(
+        a, b, (((0,), (0,)), ((), ())), preferred_element_type=F32, precision=precision
+    )
+
+
+def lanes(shape):
+    return lax.broadcasted_iota(jnp.int32, shape, len(shape) - 1)
+
+
+def split3(value):
+    high = value.astype(BF16)
+    rest = value - high.astype(F32)
+    mid = rest.astype(BF16)
+    low = (rest - mid.astype(F32)).astype(BF16)
+    return (high, mid, low)
+
+
+def put_split3(tile, value, lane0):
+    at = lanes(tile.shape)
+    for k, term in enumerate(split3(value)):
+        tile = jnp.where(at == lane0 + k, jnp.broadcast_to(term.astype(F32), tile.shape), tile)
+    return tile
+
+
+OUT, UP, DOWN, QKV = range(4)
+
+
+def weight_chunks(width, hidden):
+    up = []
+    step = hidden // 4
+    for k in range(4):
+        up += [(UP, k * step, step), (UP, hidden + k * step, step)]
+    return [(OUT, 0, width)] + up + [(DOWN, 0, width), (QKV, 0, 3 * width)]
+
+
+def block_kernel(
+    tok, cot, act, ada, wh, wout, wup, wdown, wqkv, q_gain, k_gain, tab, hw,
+    mixed, tgrad, l_attn, l_h2, l_mid, r_ffn, r_branch, r_gu, qkv_grad, ada_grad, gain_grad, qkv_hbm,
+    tok_all, whv, woutv, wupv, wdownv, actbuf, modsend, modbuf, modv,
+    cosv, sinv, qraw, kraw, qa, ka, va, kt, qt, onorm, attn_send, attn_in,
+    do_in, dot_t, dqt, dkv, dvv, dqkv_send, dqkv_in, dw_send, dw_in, pc_send, pc_in,
+    x1v, branchv, ffnv, dh2v, dx1v, dwv, dmod, dsend, dbuf,
+    tok_send, tok_recv, tok_loc, w_send, w_recv, w_loc, wh_sem, act_sem, mod_s, mod_r,
+    at_s, at_r, do_s, do_r, dq_s, dq_r, dw_sem, pc_s, pc_r, dm_s, dm_r, loc,
+):
+    img, ty, z = lax.axis_index("img"), lax.axis_index("ty"), lax.axis_index("tx")
+    b = ty * 4 + z
+    me = img * 16 + b
+    width = tok.shape[1]
+    half = width // 2
+    hidden = wup.shape[1] // 2
+    part = ada.shape[0]
+    other = 1 - img
+
+    def dev(i=img, t=ty, k=z):
+        return {"img": i, "ty": t, "tx": k}
+
+    def dev_flat(p):
+        return dev(p // 16, lax.rem(p // 4, 4), lax.rem(p, 4))
+
+    def dev_tile(t):
+        return dev(img, t // 4, lax.rem(t, 4))
+
+    def rcopy(src, dst, s, r, d):
+        return pltpu.make_async_remote_copy(
+            src_ref=src, dst_ref=dst, send_sem=s, recv_sem=r, device_id=d, device_id_type=MESH
+        )
+
+    def loop(lo, hi, f):
+        def step(k, c):
+            f(k)
+            return c
+
+        lax.fori_loop(lo, hi, step, 0)
+
+    bar = pltpu.get_barrier_semaphore()
+    loop(
+        1, 32,
+        lambda k: pl.semaphore_signal(
+            bar, inc=1, device_id=dev_flat(lax.rem(me + k, 32)), device_id_type=MESH
+        ),
+    )
+    pl.semaphore_wait(bar, 31)
+
+    hbm = (wout, wup, wdown, wqkv)
+    vm = (woutv, wupv, wdownv, qkv_hbm)
+    chunks = weight_chunks(width, hidden)
+
+    def wregion(i, owner, p):
+        m, c0, cn = chunks[i]
+        rows = hbm[m].shape[0]
+        return vm[m].at[pl.ds(owner * rows + p * (rows // 4), rows // 4), pl.ds(c0, cn)]
+
+    def w_x(i):
+        m, c0, cn = chunks[i]
+        piece = hbm[m].shape[0] // 4
+        return rcopy(
+            hbm[m].at[pl.ds(ty * piece, piece), pl.ds(c0, cn)],
+            wregion(i, img, ty), w_send.at[i, 0], w_recv.at[i, ty], dev(i=other),
+        )
+
+    def w_y(i):
+        ref = wregion(i, other, ty)
+        return rcopy(ref, ref, w_send.at[i, 1], w_recv.at[i, ty], dev(t=ty ^ 2))
+
+    def w_c(i, p, slot):
+        ref = wregion(i, other, p)
+        return rcopy(ref, ref, w_send.at[i, slot], w_recv.at[i, p], dev(t=ty ^ 1))
+
+    def w_wait(i, p):
+        ref = wregion(i, other, p)
+        rcopy(ref, ref, w_send.at[i, 0], w_recv.at[i, p], dev(t=ty ^ 1)).wait_recv()
+
+    def x_arrived(i):
+        w_wait(i, ty)
+        w_y(i).start()
+        w_c(i, ty, 2).start()
+
+    def y_arrived(i):
+        w_wait(i, ty ^ 2)
+        w_c(i, ty ^ 2, 3).start()
+
+    def w_done(i):
+        w_wait(i, ty ^ 1)
+        w_wait(i, ty ^ 3)
+
+    def w_drain(i):
+        w_x(i).wait_send()
+        w_y(i).wait_send()
+        w_c(i, ty, 2).wait_send()
+        w_c(i, ty ^ 2, 3).wait_send()
+
+    def own(m):
+        rows = hbm[m].shape[0]
+        return pltpu.make_async_copy(hbm[m], vm[m].at[pl.ds(img * rows, rows)], w_loc.at[m])
+
+    act_copy = rcopy(act, actbuf.at[img], act_sem.at[0], act_sem.at[1], dev(i=other))
+    act_copy.start()
+    actbuf[img] = act[...]
+    wh_copy = rcopy(wh, whv.at[pl.ds(img * half, half)], wh_sem.at[0], wh_sem.at[1], dev(i=other))
+    wh_copy.start()
+    whv[pl.ds(pl.multiple_of(img * half, 64), half), :] = wh[...]
+
+    def t_send(src, chunk, way, d):
+        return rcopy(src, tok_all.at[chunk], tok_send.at[chunk, way], tok_recv.at[chunk], d)
+
+    def t_wait(chunk):
+        t_send(tok, chunk, 0, dev(t=ty ^ 1)).wait_recv()
+
+    tok_own = pltpu.make_async_copy(tok, tok_all.at[b], tok_loc)
+    tok_own.start()
+
+    def t_forward(src, chunk, up, down):
+        if up:
+
+            @pl.when(z < 3)
+            def _():
+                t_send(src, chunk, 0, dev(k=z + 1)).start()
+
+        if down:
+
+            @pl.when(z > 0)
+            def _():
+                t_send(src, chunk, 1, dev(k=z - 1)).start()
+
+        t_send(src, chunk, 2, dev(t=ty ^ 2)).start()
+        t_send(src, chunk, 3, dev(t=ty ^ 1)).start()
+
+    t_forward(tok, b, True, True)
+    for m in range(4):
+        own(m).start()
+    for i in range(9):
+        w_x(i).start()
+
+    act_copy.wait_recv()
+    for i in range(2):
+        modsend[i, :, 0:part] = dot_nt(actbuf[i].astype(BF16), ada[...])
+
+    def mod_copy(p):
+        return rcopy(modsend.at[p // 16], modbuf.at[me], mod_s.at[p], mod_r.at[me], dev_flat(p))
+
+    loop(1, 32, lambda k: mod_copy(lax.rem(me + k, 32)).start())
+    modbuf[me] = modsend[img]
+
+    for s in (1, 2, 3):
+
+        @pl.when(z - s >= 0)
+        def _():
+            t_wait(b - s)
+            t_forward(tok_all.at[b - s], b - s, True, False)
+
+        @pl.when(z + s <= 3)
+        def _():
+            t_wait(b + s)
+            t_forward(tok_all.at[b + s], b + s, False, True)
+
+    def t_y(zz):
+        chunk = (ty ^ 2) * 4 + zz
+        t_wait(chunk)
+        t_send(tok_all.at[chunk], chunk, 3, dev(t=ty ^ 1)).start()
+
+    loop(0, 4, t_y)
+    x_arrived(0)
+    for i in range(1, 5):
+        x_arrived(i)
+    w_x(9).start()
+    loop(0, 4, lambda zz: t_wait((ty ^ 1) * 4 + zz))
+    loop(0, 4, lambda zz: t_wait((ty ^ 3) * 4 + zz))
+
+    def t_drain(zz):
+        chunk = ty * 4 + zz
+        ref = tok_all.at[chunk]
+
+        @pl.when((zz <= z) & (z < 3))
+        def _():
+            t_send(ref, chunk, 0, dev(t=ty ^ 1)).wait_send()
+
+        @pl.when((zz >= z) & (z > 0))
+        def _():
+            t_send(ref, chunk, 1, dev(t=ty ^ 1)).wait_send()
+
+        t_send(ref, chunk, 2, dev(t=ty ^ 1)).wait_send()
+        t_send(ref, chunk, 3, dev(t=ty ^ 1)).wait_send()
+        away = (ty ^ 2) * 4 + zz
+        t_send(tok_all.at[away], away, 3, dev(t=ty ^ 1)).wait_send()
+
+    loop(0, 4, t_drain)
+    tok_own.wait()
+
+    def mod_wait(k):
+        p = lax.rem(me + k, 32)
+        rcopy(
+            modsend.at[0], modbuf.at[p], mod_s.at[p], mod_r.at[p], dev_flat(p)
+        ).wait()
+
+    loop(1, 32, mod_wait)
+    for s in range(32):
+        modv[:, s * part : (s + 1) * part] = modbuf[s, :, 0:part]
+    shift1, scale1, gate1, shift2, scale2, gate2 = [
+        functools.partial(lambda k: modv[0:1, k * width : (k + 1) * width], k) for k in range(6)
+    ]
+    wh_copy.wait()
+
+    height, wide = hw[0], hw[1]
+    local = lax.broadcasted_iota(jnp.int32, (TILE, PAD), 0)
+    lane = lax.broadcasted_iota(jnp.int32, (TILE, PAD), 1)
+
+    def tile_layout(t):
+        row_tile, col_tile = t // 4, lax.rem(t, 4)
+        top = row_tile * height // 4
+        rows = (row_tile + 1) * height // 4 - top
+        left = col_tile * wide // 4
+        span = (col_tile + 1) * wide // 4 - left
+        spans = jnp.full((TILE, PAD), span, jnp.int32)
+        quot = jnp.floor((local.astype(F32) + 0.5) / spans.astype(F32)).astype(jnp.int32)
+        valid = local < jnp.full((TILE, PAD), rows * span, jnp.int32)
+        row = jnp.where(valid, top + quot, 0)
+        col = jnp.where(valid, left + local - quot * spans, 0)
+        return valid, row, col
+
+    def rope(n, c, s1, s2):
+        return n * c + pltpu.roll(n, PAD - 18, 1) * s1 + pltpu.roll(n, 18, 1) * s2
+
+    def unrope(d, c, s1, s2):
+        return d * c + pltpu.roll(d * s1, 18, 1) + pltpu.roll(d * s2, PAD - 18, 1)
+
+    def split_sin(sine):
+        first = (lane < 18) | ((lane >= 36) & (lane < 54))
+        return jnp.where(first, -sine, 0.0), jnp.where(first, 0.0, sine)
+
+    def head_rows(t):
+        valid, row, col = tile_layout(t)
+        hot = jnp.where((lane == row) | (lane - 64 == col), 1.0, 0.0)
+        angles = lax.dot_general(
+            hot, tab[...], (((1,), (0,)), ((), ())),
+            precision=HIGH, preferred_element_type=F32,
+        )
+        c, sine = angles[:, 0:PAD], angles[:, PAD : 2 * PAD]
+        cosv[t] = c
+        sinv[t] = sine
+        s1, s2 = split_sin(sine)
+        x = tok_all[t].astype(F32)
+        r = lax.rsqrt(jnp.mean(x * x, axis=1, keepdims=True) + EPS)
+        h1 = ((x * r) * (1.0 + scale1()) + shift1()).astype(BF16)
+        tok_all[t] = h1
+        qkv = dot(h1, whv[...])
+        q_r, k_r, v_r = qkv[:, 0:PAD], qkv[:, PAD : 2 * PAD], qkv[:, 2 * PAD : 3 * PAD]
+        qraw[t] = q_r
+        kraw[t] = k_r
+
+        def normed(v, gain):
+            rr = lax.rsqrt(jnp.sum(v * v, axis=1, keepdims=True) * (1.0 / HEAD) + EPS)
+            return v * rr * gain[0:1, :]
+
+        q_f = rope(normed(q_r, q_gain), c, s1, s2) * HEAD ** (-0.5)
+        k_f = rope(normed(k_r, k_gain), c, s1, s2)
+        qa[t] = jnp.where(lane == HEAD, 1.0, q_f).astype(BF16)
+        k_f = jnp.where(lane == HEAD, jnp.where(valid, 0.0, -30000.0), k_f)
+        k_f = jnp.where((lane > HEAD) & (lane < HEAD + 4), 1.0, k_f)
+        ka[t] = k_f.astype(BF16)
+        kt[:, pl.ds(pl.multiple_of(t * TILE, TILE), TILE)] = k_f.T.astype(BF16)
+        va[t] = jnp.where((lane >= HEAD) & (lane < HEAD + 3), 1.0, v_r).astype(BF16)
+
+    loop(0, 16, head_rows)
+    for i in range(5, 9):
+        x_arrived(i)
+    y_arrived(0)
+
+    def at_copy(t):
+        return rcopy(attn_send.at[t], attn_in.at[b], at_s.at[t], at_r.at[b], dev_tile(t))
+
+    def attend(k):
+        q2 = qa[pl.ds(2 * k, 2)].reshape(2 * TILE, PAD)
+        p = jnp.exp(dot(q2, kt[...])).astype(BF16)
+        o = dot(p, va[...].reshape(16 * TILE, PAD))
+        total = o[:, HEAD : HEAD + 1]
+        o = o / total
+        lse = jnp.log(total)
+        q3 = put_split3(q2.astype(F32), -lse, HEAD + 1)
+        o16 = o.astype(BF16)
+        for u in range(2):
+            t = 2 * k + u
+            rows = slice(u * TILE, (u + 1) * TILE)
+            onorm[t] = o[rows]
+            qa[t] = q3[rows].astype(BF16)
+            qt[:, pl.ds(pl.multiple_of(t * TILE, TILE), TILE)] = q3[rows].T.astype(BF16)
+            attn_send[t] = o16[rows]
+
+            @pl.when(t != b)
+            def _():
+                at_copy(t).start()
+
+    loop(0, 8, attend)
+    attn_in[b] = attn_send[b]
+    for i in range(1, 5):
+        y_arrived(i)
+    x_arrived(9)
+    w_x(10).start()
+    for i in range(5, 9):
+        y_arrived(i)
+
+    def at_wait(k):
+        p = lax.rem(b + k, 16)
+        rcopy(attn_send.at[p], attn_in.at[p], at_s.at[p], at_r.at[p], dev_tile(p)).wait()
+
+    loop(1, 16, at_wait)
+
+    attn = jnp.concatenate(
+        [attn_in[h].astype(F32)[:, 0:HEAD] for h in range(16)], axis=1
+    ).astype(BF16)
+    l_attn[...] = attn
+    own(OUT).wait()
+    w_done(0)
+    own_valid = tile_layout(b)[0]
+    keep = jnp.where(own_valid, 1.0, 0.0)[:, 0:1]
+    cols = width // 3
+
+    def project(k):
+        at = pl.ds(pl.multiple_of(k * cols, PAD), cols)
+        branchv[:, at] = dot(l_attn[...], woutv[:, at])
+
+    loop(0, 3, project)
+    x = tok[...].astype(F32)
+    x1 = x + keep * gate1() * branchv[...]
+    x1v[...] = x1
+    r = lax.rsqrt(jnp.mean(x1 * x1, axis=1, keepdims=True) + EPS)
+    l_h2[...] = ((x1 * r) * (1.0 + scale2()) + shift2()).astype(BF16)
+    r_ffn[...] = (cot[...].astype(F32) * keep * gate2()).astype(BF16)
+    ffnv[...] = jnp.zeros_like(ffnv)
+    dh2v[...] = jnp.zeros_like(dh2v)
+    y_arrived(9)
+    for i in range(1, 10):
+        w_done(i)
+    own(UP).wait()
+    own(DOWN).wait()
+    step = 256
+
+    def mlp(j):
+        g_at = pl.ds(pl.multiple_of(j * step, step), step)
+        u_at = pl.ds(pl.multiple_of(hidden + j * step, step), step)
+        h2 = l_h2[...]
+        gate = dot(h2, wupv[:, g_at])
+        up = dot(h2, wupv[:, u_at])
+        sig = 1.0 / (1.0 + jnp.exp(-gate))
+        act_g = gate * sig
+        mid = (act_g * up).astype(BF16)
+        l_mid[:, g_at] = mid
+        w3 = wdownv[g_at, :]
+        ffnv[...] += dot(mid, w3)
+        d_mid = dot_nt(r_ffn[...], w3)
+        d_gate = (d_mid * up * (sig + gate * sig * (1.0 - sig))).astype(BF16)
+        d_up = (d_mid * act_g).astype(BF16)
+        r_gu[:, g_at] = d_gate
+        r_gu[:, u_at] = d_up
+        dh2v[...] += dot_nt(d_gate, wupv[:, g_at]) + dot_nt(d_up, wupv[:, u_at])
+
+    loop(0, hidden // step, mlp)
+    x_arrived(10)
+    ffn = ffnv[...]
+    g = cot[...].astype(F32)
+    x1 = x1v[...]
+    mixed[...] = (x1 + keep * gate2() * ffn).astype(BF16)
+
+    def dmod_put(k, row):
+        dmod[0:1, k * width : (k + 1) * width] = row
+
+    def colsum(v):
+        return jnp.sum(v, axis=0, keepdims=True)
+
+    dmod_put(5, colsum(g * keep * ffn))
+    d_h2 = dh2v[...]
+    norm2 = x1 * r
+    dmod_put(4, colsum(d_h2 * norm2))
+    dmod_put(3, colsum(d_h2))
+    d_n2 = d_h2 * (1.0 + scale2())
+    d_x1 = g + r * (d_n2 - norm2 * jnp.mean(d_n2 * norm2, axis=1, keepdims=True))
+    dx1v[...] = d_x1
+    dmod_put(2, colsum(d_x1 * keep * branchv[...]))
+    r_branch[...] = (d_x1 * keep * gate1()).astype(BF16)
+
+    def unproject(k):
+        at = pl.ds(pl.multiple_of(k * cols, PAD), cols)
+        branchv[:, at] = dot_nt(r_branch[...], woutv[at, :])
+
+    loop(0, 3, unproject)
+
+    zeros = jnp.zeros((TILE, PAD - HEAD), F32)
+    d_attn = branchv[...]
+    for h in range(16):
+        attn_send[h] = jnp.concatenate(
+            [d_attn[:, h * HEAD : (h + 1) * HEAD], zeros], axis=1
+        ).astype(BF16)
+
+    def do_copy(t):
+        return rcopy(attn_send.at[t], do_in.at[b], do_s.at[t], do_r.at[b], dev_tile(t))
+
+    loop(1, 16, lambda k: do_copy(lax.rem(b + k, 16)).start())
+    do_in[b] = attn_send[b]
+    y_arrived(10)
+    own(QKV).wait()
+
+    def do_wait(k):
+        p = lax.rem(b + k, 16)
+        rcopy(attn_send.at[p], do_in.at[p], do_s.at[p], do_r.at[p], dev_tile(p)).wait()
+
+    loop(1, 16, do_wait)
+
+    def delta(t):
+        d = do_in[t].astype(F32)
+        dsum = jnp.sum(jnp.where(lane < HEAD, d * onorm[t], 0.0), axis=1, keepdims=True)
+        d = put_split3(d, -dsum, HEAD)
+        do_in[t] = d.astype(BF16)
+        dot_t[:, pl.ds(pl.multiple_of(t * TILE, TILE), TILE)] = d.T.astype(BF16)
+
+    loop(0, 16, delta)
+    dqt[...] = jnp.zeros_like(dqt)
+
+    def attend_back(k):
+        two = pl.ds(2 * k, 2)
+        p = jnp.exp(dot(ka[two].reshape(2 * TILE, PAD), qt[...]))
+        ds = (p * dot(va[two].reshape(2 * TILE, PAD), dot_t[...])).astype(BF16)
+        dkv[two] = dot(ds, qa[...].reshape(16 * TILE, PAD)).reshape(2, TILE, PAD)
+        dvv[two] = dot(p.astype(BF16), do_in[...].reshape(16 * TILE, PAD)).reshape(2, TILE, PAD)
+        at = pl.ds(pl.multiple_of(k * 2 * TILE, 2 * TILE), 2 * TILE)
+        dqt[...] += dot(kt[:, at], ds)
+
+    loop(0, 8, attend_back)
+
+    for i in range(11):
+        w_drain(i)
+    gain_grad[...] = jnp.zeros_like(gain_grad)
+
+    def dq_copy(t):
+        return rcopy(dqkv_send.at[t], dqkv_in.at[b], dq_s.at[t], dq_r.at[b], dev_tile(t))
+
+    def heads_back(t):
+        c = cosv[t]
+        s1, s2 = split_sin(sinv[t])
+
+        def norm_back(d, v, gain, row):
+            rr = lax.rsqrt(jnp.sum(v * v, axis=1, keepdims=True) * (1.0 / HEAD) + EPS)
+            n = v * rr
+            gain_grad[row : row + 1, :] += colsum(d * n)
+            dn = d * gain[0:1, :]
+            return rr * (dn - n * (jnp.sum(dn * n, axis=1, keepdims=True) * (1.0 / HEAD)))
+
+        d_q = dqt[:, pl.ds(pl.multiple_of(t * TILE, TILE), TILE)].T * HEAD ** (-0.5)
+        d_q = norm_back(unrope(d_q, c, s1, s2), qraw[t], q_gain, 0)
+        d_k = norm_back(unrope(dkv[t], c, s1, s2), kraw[t], k_gain, 1)
+        d_v = jnp.where(lane < HEAD, dvv[t], 0.0)
+        at = pl.ds(pl.multiple_of(t * TILE, TILE), TILE)
+        wdownv[at, 0 : 3 * PAD] = jnp.concatenate([d_q, d_k, d_v], axis=1).astype(BF16)
+        dqkv_send[t] = jnp.concatenate(
+            [d_q[:, 0:HEAD], d_k[:, 0:HEAD], d_v[:, 0:HEAD], zeros[:, 0:40]], axis=1
+        ).astype(BF16)
+
+        @pl.when(t != b)
+        def _():
+            dq_copy(t).start()
+
+    loop(0, 16, heads_back)
+    dqkv_in[b] = dqkv_send[b]
+
+    dwv[...] = jnp.zeros_like(dwv)
+
+    def dw_rows(k):
+        two = pl.ds(2 * k, 2)
+        at = pl.ds(pl.multiple_of(k * 2 * TILE, TILE), 2 * TILE)
+        dwv[...] += dot_tn(wdownv[at, 0 : 3 * PAD], tok_all[two].reshape(2 * TILE, width))
+
+    loop(0, 8, dw_rows)
+    dw = dwv[...].T
+    dw_send[0] = dw[0:half].astype(BF16)
+    dw_send[1] = dw[half : 2 * half].astype(BF16)
+    dw_copy = rcopy(dw_send.at[other], dw_in, dw_sem.at[0], dw_sem.at[1], dev(i=other))
+    dw_copy.start()
+    w_done(10)
+
+    load = pltpu.make_async_copy(qkv_hbm, wupv.at[:, pl.ds(0, 3 * width)], loc)
+    load.start()
+
+    def dq_wait(k):
+        p = lax.rem(b + k, 16)
+        rcopy(dqkv_send.at[p], dqkv_in.at[p], dq_s.at[p], dq_r.at[p], dev_tile(p)).wait()
+
+    loop(1, 16, dq_wait)
+    dw_copy.wait()
+    dw_sum = dw_send[img].astype(F32) + dw_in[...].astype(F32)
+    for p in range(3):
+        pc_send[p] = dw_sum[:, p * PAD : (p + 1) * PAD].astype(BF16)
+
+    def pc_copy(p):
+        group = 16 * p + b
+        to, slot = group // 3, lax.rem(group, 3)
+        return to, rcopy(
+            pc_send.at[p], pc_in.at[slot], pc_s.at[p], pc_r.at[slot], dev_tile(to)
+        )
+
+    for p in range(3):
+        to, copy = pc_copy(p)
+
+        @pl.when(to != b)
+        def _():
+            copy.start()
+
+        @pl.when(to == b)
+        def _():
+            pc_in[lax.rem(16 * p + b, 3)] = pc_send[p]
+
+    load.wait()
+    dqkv = [dqkv_in[h].astype(F32) for h in range(16)]
+    def own_part(p):
+        return slice(16 * TILE + p * TILE, 16 * TILE + (p + 1) * TILE)
+
+    for p in range(3):
+        wdownv[own_part(p), :] = jnp.concatenate(
+            [dqkv[h][:, p * HEAD : (p + 1) * HEAD] for h in range(16)], axis=1
+        ).astype(BF16)
+
+    def h1_back(k):
+        at = pl.ds(pl.multiple_of(k * cols, PAD), cols)
+        dh2v[:, at] = sum(
+            dot_nt(wdownv[own_part(p), :], wupv[at, p * width : (p + 1) * width])
+            for p in range(3)
+        )
+
+    loop(0, 3, h1_back)
+    d_h1 = dh2v[...]
+    x = tok[...].astype(F32)
+    r1 = lax.rsqrt(jnp.mean(x * x, axis=1, keepdims=True) + EPS)
+    norm1 = x * r1
+    dmod_put(1, colsum(d_h1 * norm1))
+    dmod_put(0, colsum(d_h1))
+    d_n1 = d_h1 * (1.0 + scale1())
+    back = r1 * (d_n1 - norm1 * jnp.mean(d_n1 * norm1, axis=1, keepdims=True))
+    tgrad[...] = (dx1v[...] + back).astype(BF16)
+
+    dsend[...] = jnp.zeros_like(dsend)
+    for s in range(32):
+        dsend[s, 0:1, 0:part] = dmod[0:1, s * part : (s + 1) * part]
+        dsend[s, 1:3, 0:PAD] = gain_grad[0:2, :]
+
+    def dm_copy(p):
+        return rcopy(dsend.at[p], dbuf.at[me], dm_s.at[p], dm_r.at[me], dev_flat(p))
+
+    loop(1, 32, lambda k: dm_copy(lax.rem(me + k, 32)).start())
+    dbuf[me] = dsend[me]
+
+    for slot in range(3):
+        group = 3 * b + slot
+        src = lax.rem(group, 16)
+
+        @pl.when(src != b)
+        def _():
+            rcopy(
+                pc_send.at[0], pc_in.at[slot], pc_s.at[0], pc_r.at[slot], dev_tile(src)
+            ).wait_recv()
+
+    qkv_grad[...] = jnp.concatenate(
+        [pc_in[slot].astype(F32)[:, 0:HEAD] for slot in range(3)], axis=1
+    )
+    for p in range(3):
+        to, copy = pc_copy(p)
+
+        @pl.when(to != b)
+        def _():
+            copy.wait_send()
+
+    def dm_wait(k):
+        p = lax.rem(me + k, 32)
+        rcopy(dsend.at[p], dbuf.at[p], dm_s.at[p], dm_r.at[p], dev_flat(p)).wait()
+
+    loop(1, 32, dm_wait)
+    sums = [
+        lax.fori_loop(1, 16, lambda s, a, i=i: a + dbuf[16 * i + s], dbuf[16 * i])
+        for i in range(2)
+    ]
+    gain_grad[...] = jnp.where(
+        lax.broadcasted_iota(jnp.int32, (8, PAD), 0) < 2,
+        pltpu.roll(sums[0] + sums[1], 7, 0)[:, 0:PAD],
+        0.0,
+    )
+    row = lax.broadcasted_iota(jnp.int32, (8, 2 * PAD), 0)
+    d_two = jnp.where(row == 0, sums[0][0:1, :], jnp.where(row == 1, sums[1][0:1, :], 0.0))
+    row = lax.broadcasted_iota(jnp.int32, (8, width), 0)
+    a_two = jnp.where(row == 0, actbuf[0], jnp.where(row == 1, actbuf[1], 0.0))
+    ada_grad[...] = dot_tn(d_two, a_two, HIGH)[0:part, :]
+    act_copy.wait_send()
+
+
+def rope_table():
+    table = np.zeros((PAD, 2 * PAD), np.float64)
+    angle = np.arange(64)[:, None] * 10000.0 ** (-np.arange(18) / 18)
+    for axis in range(2):
+        rows = slice(64 * axis, 64 * axis + 64)
+        for quarter in range(2):
+            at = 36 * axis + 18 * quarter
+            table[rows, at : at + 18] = np.cos(angle)
+            table[rows, PAD + at : PAD + at + 18] = np.sin(angle)
+    return table.astype(np.float32)
+
+
+def run_block(tokens, cotangent, act, ada, wh, wout, wup, wdown, wqkv, q_gain, k_gain, hw):
+    width, hidden = tokens.shape[1], wup.shape[1] // 2
+    half, part = width // 2, ada.shape[0]
+    vmem, any_ = pl.BlockSpec(memory_space=pltpu.VMEM), pl.BlockSpec(memory_space=pl.ANY)
+    smem = pl.BlockSpec(memory_space=pltpu.SMEM)
+    sds = jax.ShapeDtypeStruct
+    v, dma = pltpu.VMEM, pltpu.SemaphoreType.DMA
+    n_chunks = len(weight_chunks(width, hidden))
+    tile16 = (16, TILE, PAD)
+    out_shape = (
+        sds((TILE, width), BF16),
+        sds((TILE, width), BF16),
+        sds((TILE, width), BF16),
+        sds((TILE, width), BF16),
+        sds((TILE, hidden), BF16),
+        sds((TILE, width), BF16),
+        sds((TILE, width), BF16),
+        sds((TILE, 2 * hidden), BF16),
+        sds((half, 3 * HEAD), F32),
+        sds((part, width), F32),
+        sds((8, PAD), F32),
+        sds((width, 3 * width), BF16),
+    )
+    scratch = [
+        v((16, TILE, width), BF16),
+        v((width, 3 * PAD), BF16),
+        v((width, width), BF16),
+        v((width, 2 * hidden), BF16),
+        v((hidden, width), BF16),
+        v((2, 8, width), F32),
+        v((2, 8, 2 * PAD), F32),
+        v((32, 8, 2 * PAD), F32),
+        v((8, 6 * width), F32),
+        v(tile16, F32),
+        v(tile16, F32),
+        v(tile16, F32),
+        v(tile16, F32),
+        v(tile16, BF16),
+        v(tile16, BF16),
+        v(tile16, BF16),
+        v((PAD, 16 * TILE), BF16),
+        v((PAD, 16 * TILE), BF16),
+        v(tile16, F32),
+        v(tile16, BF16),
+        v(tile16, BF16),
+        v(tile16, BF16),
+        v((PAD, 16 * TILE), BF16),
+        v((PAD, 16 * TILE), F32),
+        v(tile16, F32),
+        v(tile16, F32),
+        v((16, TILE, 2 * PAD), BF16),
+        v((16, TILE, 2 * PAD), BF16),
+        v((2, half, 3 * PAD), BF16),
+        v((half, 3 * PAD), BF16),
+        v((3, half, PAD), BF16),
+        v((3, half, PAD), BF16),
+        v((TILE, width), F32),
+        v((TILE, width), F32),
+        v((TILE, width), F32),
+        v((TILE, width), F32),
+        v((TILE, width), F32),
+        v((3 * PAD, width), F32),
+        v((8, 6 * width), F32),
+        v((32, 8, 2 * PAD), F32),
+        v((32, 8, 2 * PAD), F32),
+        dma((16, 4)),
+        dma((16,)),
+        dma,
+        dma((n_chunks, 4)),
+        dma((n_chunks, 4)),
+        dma((4,)),
+        dma((2,)),
+        dma((2,)),
+        dma((32,)),
+        dma((32,)),
+        dma((16,)),
+        dma((16,)),
+        dma((16,)),
+        dma((16,)),
+        dma((16,)),
+        dma((16,)),
+        dma((2,)),
+        dma((3,)),
+        dma((3,)),
+        dma((32,)),
+        dma((32,)),
+        dma,
+    ]
+    return pl.pallas_call(
+        block_kernel,
+        out_shape=out_shape,
+        in_specs=[vmem] * 5 + [any_] * 4 + [vmem] * 3 + [smem],
+        out_specs=[vmem] * 11 + [any_],
+        scratch_shapes=scratch,
+        compiler_params=pltpu.CompilerParams(
+            collective_id=0, has_side_effects=True, vmem_limit_bytes=VMEM_LIMIT
+        ),
+    )(tokens, cotangent, act, ada, wh, wout, wup, wdown, wqkv, q_gain, k_gain, rope_table(), hw)
+
+
+def swap(value, axis, bit):
+    n = lax.axis_size(axis)
+    return lax.ppermute(value, axis, [(i, i ^ bit) for i in range(n)])
+
+
+def pick(value, index, axis):
+    return lax.dynamic_index_in_dim(value, index, axis, keepdims=False)
+
+
+def plane_grad(left, right):
+    img, ty, z = lax.axis_index("img"), lax.axis_index("ty"), lax.axis_index("tx")
+    rows, kl = left.shape
+    n = right.shape[1]
+    halves = left.reshape(rows, 2, kl // 2)
+    l2 = jnp.concatenate([pick(halves, img, 1), swap(pick(halves, 1 - img, 1), "img", 1)])
+    l4 = jnp.concatenate([l2, swap(l2, "ty", 2)])
+    l8 = jnp.concatenate([l4, swap(l4, "ty", 1)])
+    quarters = right.reshape(rows, 2, 2, n // 4)
+    y, c = ty // 2, ty % 2
+    mine = pick(quarters, y, 1)
+    theirs = swap(pick(quarters, 1 - y, 1), "ty", 2)
+    across = swap(jnp.stack([mine, theirs]), "img", 1)
+    r4 = jnp.concatenate([mine, across[0], theirs, across[1]])
+    r8 = jnp.concatenate([pick(r4, c, 1), swap(pick(r4, 1 - c, 1), "ty", 1)])
+    part = outer_sum(l8, r8).reshape(kl // 2, 2, 2, n // 16)
+    high, low = z // 2, z % 2
+    sent = swap(pick(part, 1 - low, 2).astype(jnp.bfloat16), "tx", 1)
+    part = pick(part, low, 2) + sent.astype(jnp.float32)
+    sent = swap(pick(part, 1 - high, 1).astype(jnp.bfloat16), "tx", 2)
+    return pick(part, high, 1) + sent.astype(jnp.float32)
+
+
+def head_weight(weight):
+    at = lax.axis_index(("ty", "tx")) * HEAD
+    width = weight.shape[1] // 3
+    parts = [
+        lax.dynamic_slice_in_dim(weight, p * width + at, HEAD, axis=1) for p in range(3)
+    ]
+    return jnp.concatenate([jnp.pad(p, ((0, 0), (0, PAD - HEAD))) for p in parts], axis=1)
+
+
+def fast_body(
+    tokens,
+    cotangent,
+    class_embed,
+    timestep,
+    grid_height,
+    grid_width,
+    qkv_weight,
+    out_weight,
+    up_weight,
+    down_weight,
+    ada_weight,
+    q_gain,
+    k_gain,
+):
+    width = tokens.shape[2]
+    act = jax.nn.silu(class_embed + time_embed(timestep, width)).astype(BF16).astype(F32)
+    pad = lambda g: jnp.broadcast_to(jnp.pad(g, (0, PAD - HEAD))[None], (8, PAD))
+    (mixed, tgrad, l_attn, l_h2, l_mid, r_ffn, r_branch, r_gu, qkv_grad, ada_grad, gains, _) = (
+        run_block(
+            tokens[0],
+            cotangent[0],
+            jnp.broadcast_to(act, (8, width)),
+            ada_weight,
+            head_weight(qkv_weight),
+            out_weight,
+            up_weight,
+            down_weight,
+            qkv_weight,
+            pad(q_gain),
+            pad(k_gain),
+            jnp.concatenate([grid_height, grid_width]),
+        )
+    )
+    down_grad = plane_grad(l_mid, r_ffn)
+    up_grad = plane_grad(l_h2, r_gu)
+    out_grad = plane_grad(l_attn, r_branch)
+    return (
+        mixed[None],
+        tgrad[None],
+        qkv_grad,
+        out_grad,
+        up_grad,
+        down_grad,
+        ada_grad,
+        gains[0, :HEAD],
+        gains[1, :HEAD],
+    )
+
+
 def solution(mesh):
     in_specs = (
         P("img", ("ty", "tx"), None),
@@ -318,4 +1173,7 @@
         P(),
         P(),
     )
+    shape = dict(mesh.shape)
+    fast = (shape["img"], shape["ty"], shape["tx"]) == (2, 4, 4)
+    body = fast_body if fast else general_body
     return jax.shard_map(body, mesh=mesh, in_specs=in_specs, out_specs=out_specs, check_vma=False)

time: 1690 us -> 411 us (0.24)
  waiting for transfers between devices: 1340 us -> 97.3 us
  Pallas kernels: 0 us -> 236 us
  matrix products: 131 us -> 7.4 us
  local copies, waits for them, and re-layouts: 108 us -> 34.5 us
  blocking collectives: 39.4 us -> 0 us
  other arithmetic: 48 us -> 13.8 us
  starting transfers between devices: 1.19 us -> 19.1 us
    unnamed x26 -> x0, waiting for transfers between devices: 666 us -> none
    all_gather x7 -> x0, waiting for transfers between devices: 574 us -> none  [the longest x1 168 us: body(): lax.all_gather(up_weight, 'img', axis=0, tiled=True)]
    pallas_call x0 -> x1, Pallas kernels: none -> 236 us  [run_block(): pl.pallas_call(block_kernel, out_shape=out_shape, in_specs=[vmem] * 5 + [...]
    dot_general x15 -> x0, matrix products: 109 us -> none  [the longest x4 26.3 us: times_transposed(): lax.dot_general(left, weight, (((left.ndim - 1,), (1,)), ((), ())), prefe...]
    reduce_scatter x3 -> x0, waiting for transfers between devices: 101 us -> none  [the longest x1 91.6 us: body(): lax.psum_scatter(term_down.astype(jnp.bfloat16), ('ty', 'tx'), scatter_di...]
    ppermute x0 -> x24, waiting for transfers between devices: none -> 97.3 us  [swap(): return lax.ppermute(value, axis, [(i, i ^ bit) for i in range(n)])]
    unnamed x143 -> x41, local copies, waits for them, and re-layouts: 94.2 us -> 6.15 us
    psum x1 -> x0, blocking collectives: 39.4 us -> none  [body(): lax.psum((d_q_gain, d_k_gain), ('img', 'ty', 'tx'))]
  transfers between devices with their start and end apart: 18 -> 24, of which waited for: 15 -> 9; matrix products, arithmetic and copies ran while one was open for 12% -> 11% of each run, Pallas kernels for 0% -> 0%
where the time goes in v1:
time: 411 us
  Pallas kernels  236 us (57%)
  waiting for transfers between devices  97.3 us (24%)
  local copies, waits for them, and re-layouts  34.5 us (8%)
  starting transfers between devices  19.1 us (5%)
  other arithmetic  13.8 us (3%)
  matrix products  7.4 us (2%)
    pallas_call x1, Pallas kernels, run_block(): pl.pallas_call(block_kernel, out_shape=out_shape, in_specs=[vmem] * 5 + [...  236 us
    ppermute x24, waiting for transfers between devices, swap(): return lax.ppermute(value, axis, [(i, i ^ bit) for i in range(n)])  97.3 us
    ppermute x24, starting transfers between devices, swap(): return lax.ppermute(value, axis, [(i, i ^ bit) for i in range(n)])  19.1 us
  transfers between devices with their start and end apart: 24, of which 9 were waited for; matrix products, arithmetic and copies ran while one was open for 11% of the time, Pallas kernels for 0%

profile of v1, /device:TPU:0, one launch (start us, length us, event | category | flops | bytes accessed | tf_op | source)
XLA Modules:
  0.0 410.8 jit_solution(15506064423979603150)
XLA Ops:
  4.6 1.3 constant_dynamic-slice_fusion.8
  8.7 235.5 %shard_map.205 = (bf16[128,1152]{1,0:T(8,128)(2,1)}, bf16[128,1152]{1,0:T(8,128)(2,1)}, bf16[128,1152]{1,0:T(8,128)(2,1)}, bf16[128,1152]{1,0:T(8,128)(2,1)}, bf...) custom-call(bf16[128,1152]{1,0:T(8,128)(2,1)} %bitcast.126, ...), custom_call_target="tpu_custom_call" | custom-call | tf_op jit(solution)/shard_map/pallas_call | solution.py:1046
  246.4 1.7 collective-permute-start.19
  248.7 1.6 constant_dynamic-slice_fusion.1
  254.1 4.3 %reshape.86 = bf16[128,2,2,1536]{3,2,1,0:T(2,128)(2,1)S(1)} reshape(bf16[128,6144]{1,0:T(8,128)(2,1)} %get-tuple-element.26) | data formatting | bytes 3145728 | tf_op jit(solution)/shard_map/reshape | solution.py:1075
  261.8 1.7 collective-permute-start.3
  265.9 2.2 copy.41
  270.1 12.6 %collective-permute-done.3 = bf16[128,2,288]{0,2,1:T(8,128)(2,1)} collective-permute-done((bf16[128,2,288]{0,2,1:T(8,128)(2,1)}, bf16[128,2,288]{0,2,1:T(8,128)(2,1)}, u32[]{:S(2)}, u32[]{:S(2)}) %collective-permute-start.3) | collective-permute-done | bytes 147488 | tf_op jit(solution)/shard_map/ppermute | solution.py:1060
  288.9 4.2 %collective-permute-done.1 = bf16[256,576]{0,1:T(8,128)(2,1)S(1)} collective-permute-done((bf16[256,576]{0,1:T(8,128)(2,1)S(1)}, bf16[256,576]{0,1:T(8,128)(2,1)S(1)}, u32[]{:S(2)}, u32[]{:S(2)}) %collective-permute-start.1) | collective-permute-done | bytes 294944 | tf_op jit(solution)/shard_map/ppermute | solution.py:1060
  293.9 5.1 %collective-permute-done.4 = bf16[2,128,2,288]{1,3,2,0:T(8,128)(2,1)S(1)} collective-permute-done((bf16[2,128,2,288]{1,3,2,0:T(8,128)(2,1)S(1)}, bf16[2,128,2,288]{1,3,2,0:T(8,128)(2,1)S(1)}, u32[]{:S(2)}, u32[]{:S(2)}) %collective-permute-start.4) | collective-permute-done | bytes 294944 | tf_op jit(solution)/shard_map/ppermute | solution.py:1060
  303.1 9.5 %collective-permute-done.17 = bf16[256,1536]{1,0:T(8,128)(2,1)S(1)} collective-permute-done((bf16[256,1536]{1,0:T(8,128)(2,1)S(1)}, bf16[256,1536]{1,0:T(8,128)(2,1)S(1)}, u32[]{:S(2)}, u32[]{:S(2)}) %collective-permute-start.17) | collective-permute-done | bytes 786464 | tf_op jit(solution)/shard_map/ppermute | solution.py:1060
  313.8 16.2 %collective-permute-done.12 = bf16[2,128,2,1536]{3,1,2,0:T(8,128)(2,1)S(1)} collective-permute-done((bf16[2,128,2,1536]{3,1,2,0:T(8,128)(2,1)S(1)}, bf16[2,128,2,1536]{3,1,2,0:T(8,128)(2,1)S(1)}, u32[]{:S(2)}, u32[]{:S(2)}) %collective-permute-start.12) | collective-permute-done | bytes 1572896 | tf_op jit(solution)/shard_map/ppermute | solution.py:1060
  332.7 5.1 %collective-permute-done.6 = bf16[576,2,72]{0,2,1:T(8,128)(2,1)S(1)} collective-permute-done((bf16[576,2,72]{0,2,1:T(8,128)(2,1)S(1)}, bf16[576,2,72]{0,2,1:T(8,128)(2,1)S(1)}, u32[]{:S(2)}, u32[]{:S(2)}) %collective-permute-start.6) | collective-permute-done | bytes 165920 | tf_op jit(solution)/shard_map/ppermute | solution.py:1060
  337.8 1.3 collective-permute-start.7
  340.2 4.9 %collective-permute-done.7 = bf16[576,72]{0,1:T(8,128)(2,1)S(1)} collective-permute-done((bf16[576,72]{0,1:T(8,128)(2,1)S(1)}, bf16[576,72]{0,1:T(8,128)(2,1)S(1)}, u32[]{:S(2)}, u32[]{:S(2)}) %collective-permute-start.7) | collective-permute-done | bytes 82976 | tf_op jit(solution)/shard_map/ppermute | solution.py:1060
  345.7 2.1 fusion.4
  349.2 4.7 %fusion = f32[576,1536]{1,0:T(8,128)} fusion(bf16[512,1536]{1,0:T(8,128)(2,1)S(1)} %collective-permute-done.13, bf16[512,1536]{1,0:T(8,128)(2,1)S(1)} %get-tuple-element.52, bf16[512,576]{0,1:T(8,128)(2,1)S(1)} %collective-permute-done.10, bf16[256,576]{0,1:T(8,128)(2,1)S(1)} %collective-permute-done.9, bf16[128,576]{0,1:T(8,128)(2,1)} %collective-permute-done.8, ...), kind=kOutput, calls=%fused_computation.1 | convolution fusion | flops 1822949376 | bytes 7864320 | tf_op jit(solution)/shard_map/dot_general | solution.py:73
  353.9 4.4 %reshape.87 = f32[576,2,2,384]{3,2,1,0:T(2,128)S(1)} reshape(f32[576,1536]{1,0:T(8,128)} %fusion) | data formatting | bytes 7077888 | tf_op jit(solution)/shard_map/reshape | solution.py:1082
  358.3 1.6 constant_dynamic-slice_fusion.2
  360.0 1.6 collective-permute-start.14
  362.8 2.0 collective-permute-start.23
  364.8 1.5 constant_dynamic-slice_fusion.3
  366.3 19.9 %collective-permute-done.14 = bf16[576,2,384]{2,0,1:T(8,128)(2,1)S(1)} collective-permute-done((bf16[576,2,384]{2,0,1:T(8,128)(2,1)S(1)}, bf16[576,2,384]{2,0,1:T(8,128)(2,1)S(1)}, u32[]{:S(2)}, u32[]{:S(2)}) %collective-permute-start.14) | collective-permute-done | bytes 884768 | tf_op jit(solution)/shard_map/ppermute | solution.py:1060
  387.5 19.9 %collective-permute-done.15 = bf16[576,384]{1,0:T(8,128)(2,1)S(1)} collective-permute-done((bf16[576,384]{1,0:T(8,128)(2,1)S(1)}, bf16[576,384]{1,0:T(8,128)(2,1)S(1)}, u32[]{:S(2)}, u32[]{:S(2)}) %collective-permute-start.15) | collective-permute-done | bytes 442400 | tf_op jit(solution)/shard_map/ppermute | solution.py:1060
  (126 shorter events, 42.9 us)
Async XLA Ops:
  246.4 21.8 %collective-permute-start.19 = (bf16[128,2,288]{0,2,1:T(8,128)(2,1)}, bf16[128,2,288]{0,2,1:T(8,128)(2,1)}, u32[]{:S(2)}, u32[]{:S(2)}) collective-permute-start(bf16[128,2,288]{0,2,1:T(8,128)(2,1)} %get-tuple-element.68), channel_id=1, source_target_pairs={{0,8},{4,12},{8,0},{12,4},{1,9},{5,13},{9,1},{13,5},{2,10},{6,14},... | collective-permute-start | bytes 442376 | tf_op jit(solution)/shard_map/ppermute | solution.py:1060
  251.1 35.6 %collective-permute-start.16 = (bf16[128,1536]{1,0:T(8,128)(2,1)}, bf16[128,1536]{1,0:T(8,128)(2,1)}, u32[]{:S(2)}, u32[]{:S(2)}) collective-permute-start(bf16[128,1536]{1,0:T(8,128)(2,1)} %bitcast.107), channel_id=1, source_target_pairs={{0,16},{16,0},{1,17},{17,1},{2,18},{18,2},{3,19},{19,3},{4,20},{20... | collective-permute-start | bytes 1179656 | tf_op jit(solution)/shard_map/ppermute | solution.py:1060
  253.1 47.0 %collective-permute-start.8 = (bf16[128,576]{0,1:T(8,128)(2,1)}, bf16[128,576]{0,1:T(8,128)(2,1)}, u32[]{:S(2)}, u32[]{:S(2)}) collective-permute-start(bf16[128,576]{0,1:T(8,128)(2,1)} %get-tuple-element.72), channel_id=1, source_target_pairs={{0,16},{16,0},{1,17},{17,1},{2,18},{18,2},{3,19},{19,3},{4,20},{20... | collective-permute-start | bytes 442376 | tf_op jit(solution)/shard_map/ppermute | solution.py:1060
  260.4 25.3 %collective-permute-start.11 = (bf16[128,2,1536]{2,0,1:T(8,128)(2,1)}, bf16[128,2,1536]{2,0,1:T(8,128)(2,1)S(1)}, u32[]{:S(2)}, u32[]{:S(2)}) collective-permute-start(bf16[128,2,1536]{2,0,1:T(8,128)(2,1)} %bitcast.105), channel_id=1, source_target_pairs={{0,8},{4,12},{8,0},{12,4},{1,9},{5,13},{9,1},{13,5},{2,10},{6,14},... | collective-permute-start | bytes 2359304 | tf_op jit(solution)/shard_map/ppermute | solution.py:1060
  261.8 20.9 %collective-permute-start.3 = (bf16[128,2,288]{0,2,1:T(8,128)(2,1)}, bf16[128,2,288]{0,2,1:T(8,128)(2,1)}, u32[]{:S(2)}, u32[]{:S(2)}) collective-permute-start(bf16[128,2,288]{0,2,1:T(8,128)(2,1)} %get-tuple-element.75), channel_id=1, source_target_pairs={{0,8},{4,12},{8,0},{12,4},{1,9},{5,13},{9,1},{13,5},{2,10},{6,14},... | collective-permute-start | bytes 442376 | tf_op jit(solution)/shard_map/ppermute | solution.py:1060
  268.1 16.5 %collective-permute-start = (bf16[128,576]{0,1:T(8,128)(2,1)S(1)}, bf16[128,576]{0,1:T(8,128)(2,1)S(1)}, u32[]{:S(2)}, u32[]{:S(2)}) collective-permute-start(bf16[128,576]{0,1:T(8,128)(2,1)S(1)} %copy-done.15), channel_id=1, source_target_pairs={{0,16},{16,0},{1,17},{17,1},{2,18},{18,2},{3,19},{19,3},{4,20},{20... | collective-permute-start | bytes 442376 | tf_op jit(solution)/shard_map/ppermute | solution.py:1060
  282.7 18.9 %collective-permute-start.20 = (bf16[2,128,2,288]{1,3,2,0:T(8,128)(2,1)S(1)}, bf16[2,128,2,288]{1,3,2,0:T(8,128)(2,1)S(1)}, u32[]{:S(2)}, u32[]{:S(2)}) collective-permute-start(bf16[2,128,2,288]{1,3,2,0:T(8,128)(2,1)S(1)} %pad_maximum_fusion.11), channel_id=1, source_target_pairs={{0,16},{16,0},{1,17},{17,1},{2,18},{18,2},{3,19},{19,3},{4,20},{20... | collective-permute-start | bytes 884744 | tf_op jit(solution)/shard_map/ppermute | solution.py:1060
  284.7 14.3 %collective-permute-start.4 = (bf16[2,128,2,288]{1,3,2,0:T(8,128)(2,1)S(1)}, bf16[2,128,2,288]{1,3,2,0:T(8,128)(2,1)S(1)}, u32[]{:S(2)}, u32[]{:S(2)}) collective-permute-start(bf16[2,128,2,288]{1,3,2,0:T(8,128)(2,1)S(1)} %pad_maximum_fusion.9), channel_id=1, source_target_pairs={{0,16},{16,0},{1,17},{17,1},{2,18},{18,2},{3,19},{19,3},{4,20},{20... | collective-permute-start | bytes 884744 | tf_op jit(solution)/shard_map/ppermute | solution.py:1060
  285.8 7.2 %collective-permute-start.1 = (bf16[256,576]{0,1:T(8,128)(2,1)S(1)}, bf16[256,576]{0,1:T(8,128)(2,1)S(1)}, u32[]{:S(2)}, u32[]{:S(2)}) collective-permute-start(bf16[256,576]{0,1:T(8,128)(2,1)S(1)} %pad_maximum_fusion.8), channel_id=1, source_target_pairs={{0,8},{4,12},{8,0},{12,4},{1,9},{5,13},{9,1},{13,5},{2,10},{6,14},... | collective-permute-start | bytes 884744 | tf_op jit(solution)/shard_map/ppermute | solution.py:1060
  286.8 43.2 %collective-permute-start.12 = (bf16[2,128,2,1536]{3,1,2,0:T(8,128)(2,1)S(1)}, bf16[2,128,2,1536]{3,1,2,0:T(8,128)(2,1)S(1)}, u32[]{:S(2)}, u32[]{:S(2)}) collective-permute-start(bf16[2,128,2,1536]{3,1,2,0:T(8,128)(2,1)S(1)} %pad_maximum_fusion.1), channel_id=1, source_target_pairs={{0,16},{16,0},{1,17},{17,1},{2,18},{18,2},{3,19},{19,3},{4,20},{20... | collective-permute-start | bytes 4718600 | tf_op jit(solution)/shard_map/ppermute | solution.py:1060
  293.0 19.6 %collective-permute-start.17 = (bf16[256,1536]{1,0:T(8,128)(2,1)S(1)}, bf16[256,1536]{1,0:T(8,128)(2,1)S(1)}, u32[]{:S(2)}, u32[]{:S(2)}) collective-permute-start(bf16[256,1536]{1,0:T(8,128)(2,1)S(1)} %pad_maximum_fusion.3), channel_id=1, source_target_pairs={{0,8},{4,12},{8,0},{12,4},{1,9},{5,13},{9,1},{13,5},{2,10},{6,14},... | collective-permute-start | bytes 2359304 | tf_op jit(solution)/shard_map/ppermute | solution.py:1060
  299.0 3.5 collective-permute-start.2
  300.1 2.3 collective-permute-start.5
  301.6 37.5 %collective-permute-start.9 = (bf16[256,576]{0,1:T(8,128)(2,1)S(1)}, bf16[256,576]{0,1:T(8,128)(2,1)S(1)}, u32[]{:S(2)}, u32[]{:S(2)}) collective-permute-start(bf16[256,576]{0,1:T(8,128)(2,1)S(1)} %pad_maximum_fusion.10), channel_id=1, source_target_pairs={{0,8},{4,12},{8,0},{12,4},{1,9},{5,13},{9,1},{13,5},{2,10},{6,14},... | collective-permute-start | bytes 884744 | tf_op jit(solution)/shard_map/ppermute | solution.py:1060
  313.7 32.0 %collective-permute-start.18 = (bf16[512,1536]{1,0:T(8,128)(2,1)S(1)}, bf16[512,1536]{1,0:T(8,128)(2,1)S(1)}, u32[]{:S(2)}, u32[]{:S(2)}) collective-permute-start(bf16[512,1536]{1,0:T(8,128)(2,1)S(1)} %pad_maximum_fusion.2), channel_id=1, source_target_pairs={{0,4},{4,0},{8,12},{12,8},{1,5},{5,1},{9,13},{13,9},{2,6},{6,2},{1... | collective-permute-start | bytes 4718600 | tf_op jit(solution)/shard_map/ppermute | solution.py:1060
  330.6 18.2 %collective-permute-start.13 = (bf16[512,1536]{1,0:T(8,128)(2,1)S(1)}, bf16[512,1536]{1,0:T(8,128)(2,1)S(1)}, u32[]{:S(2)}, u32[]{:S(2)}) collective-permute-start(bf16[512,1536]{1,0:T(8,128)(2,1)S(1)} %get-tuple-element.53), channel_id=1, source_target_pairs={{0,4},{4,0},{8,12},{12,8},{1,5},{5,1},{9,13},{13,9},{2,6},{6,2},{1... | collective-permute-start | bytes 4718600 | tf_op jit(solution)/shard_map/ppermute | solution.py:1060
  330.7 7.1 %collective-permute-start.6 = (bf16[576,2,72]{0,2,1:T(8,128)(2,1)S(1)}, bf16[576,2,72]{0,2,1:T(8,128)(2,1)S(1)}, u32[]{:S(2)}, u32[]{:S(2)}) collective-permute-start(bf16[576,2,72]{0,2,1:T(8,128)(2,1)S(1)} %fusion.43), channel_id=1, source_target_pairs={{0,1},{1,0},{2,3},{3,2},{4,5},{5,4},{6,7},{7,6},{8,9},{9,8},{10,11... | collective-permute-start | bytes 497672 | tf_op jit(solution)/shard_map/ppermute | solution.py:1060
  332.4 13.3 %collective-permute-start.21 = (bf16[512,288]{0,1:T(8,128)(2,1)S(1)}, bf16[512,288]{0,1:T(8,128)(2,1)S(1)}, u32[]{:S(2)}, u32[]{:S(2)}) collective-permute-start(bf16[512,288]{0,1:T(8,128)(2,1)S(1)} %get-tuple-element.63), channel_id=1, source_target_pairs={{0,4},{4,0},{8,12},{12,8},{1,5},{5,1},{9,13},{13,9},{2,6},{6,2},{1... | collective-permute-start | bytes 884744 | tf_op jit(solution)/shard_map/ppermute | solution.py:1060
  337.8 7.2 %collective-permute-start.7 = (bf16[576,72]{0,1:T(8,128)(2,1)S(1)}, bf16[576,72]{0,1:T(8,128)(2,1)S(1)}, u32[]{:S(2)}, u32[]{:S(2)}) collective-permute-start(bf16[576,72]{0,1:T(8,128)(2,1)S(1)} %fusion.44), channel_id=1, source_target_pairs={{0,2},{1,3},{2,0},{3,1},{4,6},{5,7},{6,4},{7,5},{8,10},{9,11},{10,... | collective-permute-start | bytes 248840 | tf_op jit(solution)/shard_map/ppermute | solution.py:1060
  340.1 8.7 %collective-permute-start.10 = (bf16[512,576]{0,1:T(8,128)(2,1)S(1)}, bf16[512,576]{0,1:T(8,128)(2,1)S(1)}, u32[]{:S(2)}, u32[]{:S(2)}) collective-permute-start(bf16[512,576]{0,1:T(8,128)(2,1)S(1)} %pad_maximum_fusion.6), channel_id=1, source_target_pairs={{0,4},{4,0},{8,12},{12,8},{1,5},{5,1},{9,13},{13,9},{2,6},{6,2},{1... | collective-permute-start | bytes 1769480 | tf_op jit(solution)/shard_map/ppermute | solution.py:1060
  348.7 12.9 %collective-permute-start.22 = (bf16[1536,2,72]{0,2,1:T(8,128)(2,1)}, bf16[1536,2,72]{0,2,1:T(8,128)(2,1)}, u32[]{:S(2)}, u32[]{:S(2)}) collective-permute-start(bf16[1536,2,72]{0,2,1:T(8,128)(2,1)} %fusion.41), channel_id=1, source_target_pairs={{0,1},{1,0},{2,3},{3,2},{4,5},{5,4},{6,7},{7,6},{8,9},{9,8},{10,11... | collective-permute-start | bytes 1327112 | tf_op jit(solution)/shard_map/ppermute | solution.py:1060
  360.0 26.2 %collective-permute-start.14 = (bf16[576,2,384]{2,0,1:T(8,128)(2,1)S(1)}, bf16[576,2,384]{2,0,1:T(8,128)(2,1)S(1)}, u32[]{:S(2)}, u32[]{:S(2)}) collective-permute-start(bf16[576,2,384]{2,0,1:T(8,128)(2,1)S(1)} %bitcast.121), channel_id=1, source_target_pairs={{0,1},{1,0},{2,3},{3,2},{4,5},{5,4},{6,7},{7,6},{8,9},{9,8},{10,11... | collective-permute-start | bytes 2654216 | tf_op jit(solution)/shard_map/ppermute | solution.py:1060
  362.8 23.9 %collective-permute-start.23 = (bf16[1536,72]{0,1:T(8,128)(2,1)S(1)}, bf16[1536,72]{0,1:T(8,128)(2,1)S(1)}, u32[]{:S(2)}, u32[]{:S(2)}) collective-permute-start(bf16[1536,72]{0,1:T(8,128)(2,1)S(1)} %fusion.42), channel_id=1, source_target_pairs={{0,2},{1,3},{2,0},{3,1},{4,6},{5,7},{6,4},{7,5},{8,10},{9,11},{10,... | collective-permute-start | bytes 663560 | tf_op jit(solution)/shard_map/ppermute | solution.py:1060
  386.5 20.9 %collective-permute-start.15 = (bf16[576,384]{1,0:T(8,128)(2,1)S(1)}, bf16[576,384]{1,0:T(8,128)(2,1)S(1)}, u32[]{:S(2)}, u32[]{:S(2)}) collective-permute-start(bf16[576,384]{1,0:T(8,128)(2,1)S(1)} %fusion.40), channel_id=1, source_target_pairs={{0,2},{1,3},{2,0},{3,1},{4,6},{5,7},{6,4},{7,5},{8,10},{9,11},{10,... | collective-permute-start | bytes 1327112 | tf_op jit(solution)/shard_map/ppermute | solution.py:1060
  (17 other events, 153.9 us)

commit v2 on v1

--- a/solution.py
+++ b/solution.py
@@ -350,11 +350,15 @@
 
 def block_kernel(
     tok, cot, act, ada, wh, wout, wup, wdown, wqkv, q_gain, k_gain, tab, hw,
-    mixed, tgrad, l_attn, l_h2, l_mid, r_ffn, r_branch, r_gu, qkv_grad, ada_grad, gain_grad, qkv_hbm,
+    mixed, tgrad, qkv_grad, ada_grad, gain_grad, down_grad, up_grad, out_grad, qkv_hbm,
+    lb_down, lb_up, lb_out, rb_down, rb_up, rb_out,
     tok_all, whv, woutv, wupv, wdownv, actbuf, modsend, modbuf, modv,
     cosv, sinv, qraw, kraw, qa, ka, va, kt, qt, onorm, attn_send, attn_in,
-    do_in, dot_t, dqt, dkv, dvv, dqkv_send, dqkv_in, dw_send, dw_in, pc_send, pc_in,
-    x1v, branchv, ffnv, dh2v, dx1v, dwv, dmod, dsend, dbuf,
+    do_in, dot_t, dqt, dkv, dvv, dqkv_in, dw_in, pc_in,
+    x1v, branchv, ffnv, dh2v, dmod, dsend, dbuf,
+    l_attn, l_h2, l_mid, r_ffn, r_branch, r_gu, l_h2s, l_attns, r_branchs,
+    za_down, za_up, za_out, zb_down, zb_up, zb_out, z_out,
+    gl_s, gl_r, gr_s, gr_r, g_loc, za_s, za_r, zb_s, zb_r, z_loc,
     tok_send, tok_recv, tok_loc, w_send, w_recv, w_loc, wh_sem, act_sem, mod_s, mod_r,
     at_s, at_r, do_s, do_r, dq_s, dq_r, dw_sem, pc_s, pc_r, dm_s, dm_r, loc,
 ):
@@ -456,13 +460,16 @@
     wh_copy.start()
     whv[pl.ds(pl.multiple_of(img * half, 64), half), :] = wh[...]
 
+    def tok_at(chunk):
+        return tok_all.at[pl.ds(pl.multiple_of(chunk * TILE, TILE), TILE)]
+
     def t_send(src, chunk, way, d):
-        return rcopy(src, tok_all.at[chunk], tok_send.at[chunk, way], tok_recv.at[chunk], d)
+        return rcopy(src, tok_at(chunk), tok_send.at[chunk, way], tok_recv.at[chunk], d)
 
     def t_wait(chunk):
         t_send(tok, chunk, 0, dev(t=ty ^ 1)).wait_recv()
 
-    tok_own = pltpu.make_async_copy(tok, tok_all.at[b], tok_loc)
+    tok_own = pltpu.make_async_copy(tok, tok_at(b), tok_loc)
     tok_own.start()
 
     def t_forward(src, chunk, up, down):
@@ -482,7 +489,7 @@
         t_send(src, chunk, 3, dev(t=ty ^ 1)).start()
 
     t_forward(tok, b, True, True)
-    for m in range(4):
+    for m in range(3):
         own(m).start()
     for i in range(9):
         w_x(i).start()
@@ -502,17 +509,17 @@
         @pl.when(z - s >= 0)
         def _():
             t_wait(b - s)
-            t_forward(tok_all.at[b - s], b - s, True, False)
+            t_forward(tok_at(b - s), b - s, True, False)
 
         @pl.when(z + s <= 3)
         def _():
             t_wait(b + s)
-            t_forward(tok_all.at[b + s], b + s, False, True)
+            t_forward(tok_at(b + s), b + s, False, True)
 
     def t_y(zz):
         chunk = (ty ^ 2) * 4 + zz
         t_wait(chunk)
-        t_send(tok_all.at[chunk], chunk, 3, dev(t=ty ^ 1)).start()
+        t_send(tok_at(chunk), chunk, 3, dev(t=ty ^ 1)).start()
 
     loop(0, 4, t_y)
     x_arrived(0)
@@ -524,7 +531,7 @@
 
     def t_drain(zz):
         chunk = ty * 4 + zz
-        ref = tok_all.at[chunk]
+        ref = tok_at(chunk)
 
         @pl.when((zz <= z) & (z < 3))
         def _():
@@ -537,7 +544,7 @@
         t_send(ref, chunk, 2, dev(t=ty ^ 1)).wait_send()
         t_send(ref, chunk, 3, dev(t=ty ^ 1)).wait_send()
         away = (ty ^ 2) * 4 + zz
-        t_send(tok_all.at[away], away, 3, dev(t=ty ^ 1)).wait_send()
+        t_send(tok_at(away), away, 3, dev(t=ty ^ 1)).wait_send()
 
     loop(0, 4, t_drain)
     tok_own.wait()
@@ -594,10 +601,11 @@
         cosv[t] = c
         sinv[t] = sine
         s1, s2 = split_sin(sine)
-        x = tok_all[t].astype(F32)
+        at = pl.ds(pl.multiple_of(t * TILE, TILE), TILE)
+        x = tok_all[at, :].astype(F32)
         r = lax.rsqrt(jnp.mean(x * x, axis=1, keepdims=True) + EPS)
         h1 = ((x * r) * (1.0 + scale1()) + shift1()).astype(BF16)
-        tok_all[t] = h1
+        tok_all[at, :] = h1
         qkv = dot(h1, whv[...])
         q_r, k_r, v_r = qkv[:, 0:PAD], qkv[:, PAD : 2 * PAD], qkv[:, 2 * PAD : 3 * PAD]
         qraw[t] = q_r
@@ -621,8 +629,11 @@
         x_arrived(i)
     y_arrived(0)
 
+    def head_lanes(h):
+        return attn_in.at[:, pl.ds(pl.multiple_of(h * PAD, PAD), PAD)]
+
     def at_copy(t):
-        return rcopy(attn_send.at[t], attn_in.at[b], at_s.at[t], at_r.at[b], dev_tile(t))
+        return rcopy(attn_send.at[t], head_lanes(b), at_s.at[t], at_r.at[b], dev_tile(t))
 
     def attend(k):
         q2 = qa[pl.ds(2 * k, 2)].reshape(2 * TILE, PAD)
@@ -646,7 +657,7 @@
                 at_copy(t).start()
 
     loop(0, 8, attend)
-    attn_in[b] = attn_send[b]
+    head_lanes(b)[...] = attn_send[b]
     for i in range(1, 5):
         y_arrived(i)
     x_arrived(9)
@@ -656,14 +667,118 @@
 
     def at_wait(k):
         p = lax.rem(b + k, 16)
-        rcopy(attn_send.at[p], attn_in.at[p], at_s.at[p], at_r.at[p], dev_tile(p)).wait()
+        rcopy(attn_send.at[p], head_lanes(p), at_s.at[p], at_r.at[p], dev_tile(p)).wait()
 
     loop(1, 16, at_wait)
 
+    def put_halves(ref, value):
+        pad = jnp.zeros((TILE, 5 * PAD - half), F32)
+        for k in range(2):
+            piece = jnp.concatenate([value[:, k * half : (k + 1) * half], pad], axis=1)
+            ref[:, k * 5 * PAD : (k + 1) * 5 * PAD] = piece.astype(BF16)
+
+    def put_blocks(ref, value):
+        pad = jnp.zeros((TILE, PAD - HEAD), F32)
+        for k in range(16):
+            zz = k % 4
+            to = 4 * (k // 4) + 2 * (zz % 2) + zz // 2
+            piece = jnp.concatenate([value[:, k * HEAD : (k + 1) * HEAD], pad], axis=1)
+            ref[:, to * PAD : (to + 1) * PAD] = piece.astype(BF16)
+
+    l_src, l_all = (l_mid, l_h2s, l_attns), (lb_down, lb_up, lb_out)
+    r_src, r_all = (attn_in, r_gu, r_branchs), (rb_down, rb_up, rb_out)
+    y, c = ty // 2, lax.rem(ty, 2)
+
+    def slot_rows(i, t):
+        return pl.ds(pl.multiple_of((i * 4 + t) * TILE, TILE), TILE)
+
+    def lanes_at(k, n):
+        return pl.ds(pl.multiple_of(k * n, PAD), n)
+
+    def g_left(m, k, src, i, t, d):
+        dst = l_all[m].at[slot_rows(i, t)]
+        return rcopy(dst if src is None else src, dst, gl_s.at[m, k], gl_r.at[m, i * 4 + t], d)
+
+    def g_right(m, k, src, i, t, d):
+        n = r_src[m].shape[1] // 4
+        dst = r_all[m].at[slot_rows(i, t)]
+        if k in (2, 4, 5, 6):
+            dst = r_all[m].at[slot_rows(i, t), lanes_at(1 - c, n)]
+        return rcopy(dst if src is None else src, dst, gr_s.at[m, k], gr_r.at[m, i * 4 + t], d)
+
+    to_x, to_y, to_c = dev(i=other), dev(t=ty ^ 2), dev(t=ty ^ 1)
+
+    def l_part(m, k):
+        return l_src[m].at[:, lanes_at(k, l_src[m].shape[1] // 2)]
+
+    def r_part(m, k, n):
+        return r_src[m].at[:, lanes_at(k, n * (r_src[m].shape[1] // 4))]
+
+    def g_first(m):
+        return [
+            g_left(m, 0, l_part(m, other), img, ty, to_x),
+            g_right(m, 0, r_part(m, 1 - y, 2), img, ty, to_y),
+            g_left(m, 1, l_part(m, img), img, ty, to_y),
+            g_right(m, 1, r_part(m, y, 2), img, ty, to_x),
+            g_left(m, 2, l_part(m, img), img, ty, to_c),
+            g_right(m, 2, r_part(m, ty ^ 1, 1), img, ty, to_c),
+        ]
+
+    def g_own(m):
+        n = r_src[m].shape[1] // 4
+        rows = slot_rows(img, ty)
+        return [
+            pltpu.make_async_copy(l_part(m, img), l_all[m].at[rows], g_loc.at[m, 0]),
+            pltpu.make_async_copy(
+                r_part(m, ty, 1), r_all[m].at[rows, lanes_at(c, n)], g_loc.at[m, 1]
+            ),
+        ]
+
+    def g_start(m):
+        for copy in g_first(m) + g_own(m):
+            copy.start()
+
+    def g_hop(m):
+        g_left(m, 0, None, other, ty, to_x).wait_recv()
+        g_left(m, 3, None, other, ty, to_y).start()
+        g_left(m, 4, None, other, ty, to_c).start()
+        g_right(m, 0, None, img, ty ^ 2, to_y).wait_recv()
+        g_right(m, 3, None, img, ty ^ 2, to_x).start()
+        g_right(m, 4, None, img, ty ^ 2, to_c).start()
+        g_left(m, 1, None, img, ty ^ 2, to_y).wait_recv()
+        g_left(m, 5, None, img, ty ^ 2, to_c).start()
+        g_right(m, 1, None, other, ty, to_x).wait_recv()
+        g_right(m, 5, None, other, ty, to_c).start()
+
+    def g_hop2(m):
+        g_left(m, 3, None, other, ty ^ 2, to_y).wait_recv()
+        g_left(m, 6, None, other, ty ^ 2, to_c).start()
+        g_right(m, 3, None, other, ty ^ 2, to_x).wait_recv()
+        g_right(m, 6, None, other, ty ^ 2, to_c).start()
+
+    def g_done(m):
+        n = r_src[m].shape[1] // 4
+        for i in range(2):
+            for t in (ty ^ 1, ty ^ 3):
+                g_left(m, 2, None, i, t, to_c).wait_recv()
+                ref = r_all[m].at[slot_rows(i, t), lanes_at(c, n)]
+                rcopy(ref, ref, gr_s.at[m, 2], gr_r.at[m, i * 4 + t], to_c).wait_recv()
+        for copy in g_own(m):
+            copy.wait()
+
+    def g_drain(m):
+        for copy in g_first(m):
+            copy.wait_send()
+        for k, i, t in ((3, other, ty), (4, other, ty), (5, img, ty ^ 2), (6, other, ty ^ 2)):
+            g_left(m, k, None, i, t, to_c).wait_send()
+        for k, i, t in ((3, img, ty ^ 2), (4, img, ty ^ 2), (5, other, ty), (6, other, ty ^ 2)):
+            g_right(m, k, None, i, t, to_c).wait_send()
+
     attn = jnp.concatenate(
-        [attn_in[h].astype(F32)[:, 0:HEAD] for h in range(16)], axis=1
-    ).astype(BF16)
-    l_attn[...] = attn
+        [attn_in[:, h * PAD : h * PAD + HEAD].astype(F32) for h in range(16)], axis=1
+    )
+    l_attn[...] = attn.astype(BF16)
+    put_halves(l_attns, attn)
     own(OUT).wait()
     w_done(0)
     own_valid = tile_layout(b)[0]
@@ -679,8 +794,12 @@
     x1 = x + keep * gate1() * branchv[...]
     x1v[...] = x1
     r = lax.rsqrt(jnp.mean(x1 * x1, axis=1, keepdims=True) + EPS)
-    l_h2[...] = ((x1 * r) * (1.0 + scale2()) + shift2()).astype(BF16)
-    r_ffn[...] = (cot[...].astype(F32) * keep * gate2()).astype(BF16)
+    h2_rows = (x1 * r) * (1.0 + scale2()) + shift2()
+    l_h2[...] = h2_rows.astype(BF16)
+    put_halves(l_h2s, h2_rows)
+    d_ffn = cot[...].astype(F32) * keep * gate2()
+    r_ffn[...] = d_ffn.astype(BF16)
+    put_blocks(attn_in, d_ffn)
     ffnv[...] = jnp.zeros_like(ffnv)
     dh2v[...] = jnp.zeros_like(dh2v)
     y_arrived(9)
@@ -710,6 +829,8 @@
         dh2v[...] += dot_nt(d_gate, wupv[:, g_at]) + dot_nt(d_up, wupv[:, u_at])
 
     loop(0, hidden // step, mlp)
+    g_start(0)
+    g_start(1)
     x_arrived(10)
     ffn = ffnv[...]
     g = cot[...].astype(F32)
@@ -729,9 +850,11 @@
     dmod_put(3, colsum(d_h2))
     d_n2 = d_h2 * (1.0 + scale2())
     d_x1 = g + r * (d_n2 - norm2 * jnp.mean(d_n2 * norm2, axis=1, keepdims=True))
-    dx1v[...] = d_x1
     dmod_put(2, colsum(d_x1 * keep * branchv[...]))
-    r_branch[...] = (d_x1 * keep * gate1()).astype(BF16)
+    x1v[...] = d_x1
+    d_branch = d_x1 * keep * gate1()
+    r_branch[...] = d_branch.astype(BF16)
+    put_blocks(r_branchs, d_branch)
 
     def unproject(k):
         at = pl.ds(pl.multiple_of(k * cols, PAD), cols)
@@ -751,14 +874,15 @@
 
     loop(1, 16, lambda k: do_copy(lax.rem(b + k, 16)).start())
     do_in[b] = attn_send[b]
+    g_start(2)
     y_arrived(10)
-    own(QKV).wait()
 
     def do_wait(k):
         p = lax.rem(b + k, 16)
         rcopy(attn_send.at[p], do_in.at[p], do_s.at[p], do_r.at[p], dev_tile(p)).wait()
 
     loop(1, 16, do_wait)
+    g_hop(0)
 
     def delta(t):
         d = do_in[t].astype(F32)
@@ -779,14 +903,19 @@
         at = pl.ds(pl.multiple_of(k * 2 * TILE, 2 * TILE), 2 * TILE)
         dqt[...] += dot(kt[:, at], ds)
 
-    loop(0, 8, attend_back)
+    loop(0, 4, attend_back)
+    g_hop(1)
+    loop(4, 8, attend_back)
 
     for i in range(11):
         w_drain(i)
     gain_grad[...] = jnp.zeros_like(gain_grad)
 
+    def dq_rows(t):
+        return wdownv.at[pl.ds(pl.multiple_of(t * TILE, TILE), TILE), pl.ds(3 * PAD, 2 * PAD)]
+
     def dq_copy(t):
-        return rcopy(dqkv_send.at[t], dqkv_in.at[b], dq_s.at[t], dq_r.at[b], dev_tile(t))
+        return rcopy(dq_rows(t), dqkv_in.at[b], dq_s.at[t], dq_r.at[b], dev_tile(t))
 
     def heads_back(t):
         c = cosv[t]
@@ -805,7 +934,7 @@
         d_v = jnp.where(lane < HEAD, dvv[t], 0.0)
         at = pl.ds(pl.multiple_of(t * TILE, TILE), TILE)
         wdownv[at, 0 : 3 * PAD] = jnp.concatenate([d_q, d_k, d_v], axis=1).astype(BF16)
-        dqkv_send[t] = jnp.concatenate(
+        wdownv[at, 3 * PAD : 5 * PAD] = jnp.concatenate(
             [d_q[:, 0:HEAD], d_k[:, 0:HEAD], d_v[:, 0:HEAD], zeros[:, 0:40]], axis=1
         ).astype(BF16)
 
@@ -814,41 +943,63 @@
             dq_copy(t).start()
 
     loop(0, 16, heads_back)
-    dqkv_in[b] = dqkv_send[b]
-
-    dwv[...] = jnp.zeros_like(dwv)
+    dqkv_in[b] = dq_rows(b)[...]
+    g_hop(2)
+    g_hop2(0)
+
+    sums_t = (branchv, ffnv, dqt.at[:, pl.ds(0, width)])
+    for ref in sums_t:
+        ref[...] = jnp.zeros((PAD, width), F32)
 
     def dw_rows(k):
-        two = pl.ds(2 * k, 2)
         at = pl.ds(pl.multiple_of(k * 2 * TILE, TILE), 2 * TILE)
-        dwv[...] += dot_tn(wdownv[at, 0 : 3 * PAD], tok_all[two].reshape(2 * TILE, width))
+        term = dot_tn(wdownv[at, 0 : 3 * PAD], tok_all[at, :])
+        for p in range(3):
+            sums_t[p][...] += term[p * PAD : (p + 1) * PAD]
 
     loop(0, 8, dw_rows)
-    dw = dwv[...].T
-    dw_send[0] = dw[0:half].astype(BF16)
-    dw_send[1] = dw[half : 2 * half].astype(BF16)
-    dw_copy = rcopy(dw_send.at[other], dw_in, dw_sem.at[0], dw_sem.at[1], dev(i=other))
+    for p in range(3):
+        wdownv[0:width, (5 + p) * PAD : (6 + p) * PAD] = sums_t[p][...].T.astype(BF16)
+
+    def dw_half(i):
+        return wdownv.at[pl.ds(pl.multiple_of(i * half, 64), half), pl.ds(5 * PAD, 3 * PAD)]
+
+    dw_copy = rcopy(dw_half(other), dw_in, dw_sem.at[0], dw_sem.at[1], dev(i=other))
     dw_copy.start()
+    g_hop2(1)
+    g_hop2(2)
     w_done(10)
 
-    load = pltpu.make_async_copy(qkv_hbm, wupv.at[:, pl.ds(0, 3 * width)], loc)
-    load.start()
+    loads = [
+        pltpu.make_async_copy(
+            src, wupv.at[pl.ds(owner * half, half), pl.ds(0, 3 * width)], loc.at[k]
+        )
+        for k, (src, owner) in enumerate(
+            ((wqkv, img), (qkv_hbm.at[pl.ds(other * half, half)], other))
+        )
+    ]
+    for load in loads:
+        load.start()
 
     def dq_wait(k):
         p = lax.rem(b + k, 16)
-        rcopy(dqkv_send.at[p], dqkv_in.at[p], dq_s.at[p], dq_r.at[p], dev_tile(p)).wait()
+        rcopy(dq_rows(p), dqkv_in.at[p], dq_s.at[p], dq_r.at[p], dev_tile(p)).wait()
 
     loop(1, 16, dq_wait)
     dw_copy.wait()
-    dw_sum = dw_send[img].astype(F32) + dw_in[...].astype(F32)
+    dw_sum = dw_half(img)[...].astype(F32) + dw_in[...].astype(F32)
+
+    def pc_send(p):
+        return wdownv.at[pl.ds(width, half), pl.ds((5 + p) * PAD, PAD)]
+
     for p in range(3):
-        pc_send[p] = dw_sum[:, p * PAD : (p + 1) * PAD].astype(BF16)
+        pc_send(p)[...] = dw_sum[:, p * PAD : (p + 1) * PAD].astype(BF16)
 
     def pc_copy(p):
         group = 16 * p + b
         to, slot = group // 3, lax.rem(group, 3)
         return to, rcopy(
-            pc_send.at[p], pc_in.at[slot], pc_s.at[p], pc_r.at[slot], dev_tile(to)
+            pc_send(p), pc_in.at[slot], pc_s.at[p], pc_r.at[slot], dev_tile(to)
         )
 
     for p in range(3):
@@ -860,9 +1011,10 @@
 
         @pl.when(to == b)
         def _():
-            pc_in[lax.rem(16 * p + b, 3)] = pc_send[p]
-
-    load.wait()
+            pc_in[lax.rem(16 * p + b, 3)] = pc_send(p)[...]
+
+    for load in loads:
+        load.wait()
     dqkv = [dqkv_in[h].astype(F32) for h in range(16)]
     def own_part(p):
         return slice(16 * TILE + p * TILE, 16 * TILE + (p + 1) * TILE)
@@ -888,7 +1040,112 @@
     dmod_put(0, colsum(d_h1))
     d_n1 = d_h1 * (1.0 + scale1())
     back = r1 * (d_n1 - norm1 * jnp.mean(d_n1 * norm1, axis=1, keepdims=True))
-    tgrad[...] = (dx1v[...] + back).astype(BF16)
+    tgrad[...] = (x1v[...] + back).astype(BF16)
+
+    high, low = z // 2, lax.rem(z, 2)
+    l0 = 3 * width
+
+    def z_load(m):
+        kl, n = l_all[m].shape[1], r_src[m].shape[1] // 4
+        copies = [
+            pltpu.make_async_copy(
+                l_all[m], wupv.at[pl.ds(0, 8 * TILE), pl.ds(l0, kl)], z_loc.at[0]
+            ),
+            pltpu.make_async_copy(
+                r_all[m].at[:, lanes_at(c, n)],
+                wupv.at[pl.ds(0, 8 * TILE), pl.ds(l0 + kl, n)],
+                z_loc.at[1],
+            ),
+        ]
+        for copy in copies:
+            copy.start()
+        for copy in copies:
+            copy.wait()
+
+    def z_copies(m):
+        if m == 0:
+            sent = [kt.at[pl.ds(0, 80), pl.ds(0, 12 * PAD)], qt.at[pl.ds(0, 80), pl.ds(0, 12 * PAD)]]
+        elif m == 1:
+            sent = [tok_all.at[pl.ds(0, half), pl.ds(k * 3 * PAD, 3 * PAD)] for k in range(2)]
+        else:
+            sent = [tok_all.at[pl.ds(640 + 128 * k, 80), pl.ds(0, 5 * PAD)] for k in range(2)]
+        return [
+            rcopy(sent[k], za[m].at[k], za_s.at[m, k], za_r.at[m, k], dev(k=z ^ 1))
+            for k in range(2)
+        ]
+
+    za, zb = (za_down, za_up, za_out), (zb_down, zb_up, zb_out)
+    z_rest = (
+        dot_t.at[pl.ds(0, 80), pl.ds(0, 12 * PAD)],
+        tok_all.at[pl.ds(0, half), pl.ds(6 * PAD, 3 * PAD)],
+        tok_all.at[pl.ds(896, 80), pl.ds(0, 5 * PAD)],
+    )
+    z_own = (dqt.at[pl.ds(0, 80), pl.ds(0, 12 * PAD)], up_grad, z_out)
+
+    def z_copy2(m):
+        return rcopy(z_rest[m], zb[m], zb_s.at[m], zb_r.at[m], dev(k=z ^ 2))
+
+    def z_product(m):
+        kl = l_all[m].shape[1]
+        sent = [copy.src_ref for copy in z_copies(m)]
+        if m == 1:
+
+            def turn(k):
+                at = pl.ds(pl.multiple_of(k * TILE, TILE), TILE)
+                woutv[0 : 5 * PAD, at] = wupv[at, l0 : l0 + kl].astype(F32).T.astype(BF16)
+
+            loop(0, 8, turn)
+
+            def block(zz):
+                at = pl.ds(pl.multiple_of(l0 + kl + zz * 3 * PAD, PAD), 3 * PAD)
+                return dot(woutv[0:half, 0 : 8 * TILE], wupv[0 : 8 * TILE, at])
+
+            for k in range(2):
+                sent[k][...] = block(2 * k + 1 - low).astype(BF16)
+            for copy in z_copies(m):
+                copy.start()
+            z_rest[m][...] = block(2 * (1 - high) + low).astype(BF16)
+            z_own[m][...] = block(z)
+            return
+
+        def pair(k):
+            at = pl.ds(pl.multiple_of(l0 + kl + k * 2 * PAD, PAD), 2 * PAD)
+            return dot_tn(wupv[0 : 8 * TILE, at], wupv[0 : 8 * TILE, l0 : l0 + kl])
+
+        both = pair(1 - low)
+        for k in range(2):
+            sent[k][...] = both[k * PAD : k * PAD + 80].astype(BF16)
+        for copy in z_copies(m):
+            copy.start()
+        both = pair(low)
+        first, second = both[0:80], both[PAD : PAD + 80]
+        z_rest[m][...] = jnp.where(high == 0, second, first).astype(BF16)
+        z_own[m][...] = jnp.where(high == 0, first, second)
+
+    def z_second(m):
+        for copy in z_copies(m):
+            copy.wait()
+        rest = z_rest[m][...].astype(F32) + za[m][1 - high].astype(F32)
+        z_rest[m][...] = rest.astype(BF16)
+        z_copy2(m).start()
+        z_own[m][...] += za[m][high].astype(F32)
+
+    def z_last(m):
+        z_copy2(m).wait()
+        z_own[m][...] += zb[m][...].astype(F32)
+
+    for m in range(3):
+        g_done(m)
+        z_load(m)
+        z_product(m)
+    for m in range(3):
+        z_second(m)
+    for m in range(3):
+        z_last(m)
+    for m in range(3):
+        g_drain(m)
+    down_grad[...] = z_own[0][...].T[:, 0:HEAD]
+    out_grad[...] = z_own[2][...].T[0:half, 0:HEAD]
 
     dsend[...] = jnp.zeros_like(dsend)
     for s in range(32):
@@ -908,7 +1165,7 @@
         @pl.when(src != b)
         def _():
             rcopy(
-                pc_send.at[0], pc_in.at[slot], pc_s.at[0], pc_r.at[slot], dev_tile(src)
+                pc_send(0), pc_in.at[slot], pc_s.at[0], pc_r.at[slot], dev_tile(src)
             ).wait_recv()
 
     qkv_grad[...] = jnp.concatenate(
@@ -967,19 +1224,22 @@
     out_shape = (
         sds((TILE, width), BF16),
         sds((TILE, width), BF16),
-        sds((TILE, width), BF16),
-        sds((TILE, width), BF16),
-        sds((TILE, hidden), BF16),
-        sds((TILE, width), BF16),
-        sds((TILE, width), BF16),
-        sds((TILE, 2 * hidden), BF16),
         sds((half, 3 * HEAD), F32),
         sds((part, width), F32),
         sds((8, PAD), F32),
+        sds((hidden // 2, HEAD), F32),
+        sds((half, 3 * PAD), F32),
+        sds((half, HEAD), F32),
         sds((width, 3 * width), BF16),
+        sds((8 * TILE, hidden // 2), BF16),
+        sds((8 * TILE, 5 * PAD), BF16),
+        sds((8 * TILE, 5 * PAD), BF16),
+        sds((8 * TILE, 8 * PAD), BF16),
+        sds((8 * TILE, hidden), BF16),
+        sds((8 * TILE, 8 * PAD), BF16),
     )
     scratch = [
-        v((16, TILE, width), BF16),
+        v((16 * TILE, width), BF16),
         v((width, 3 * PAD), BF16),
         v((width, width), BF16),
         v((width, 2 * hidden), BF16),
@@ -999,27 +1259,48 @@
         v((PAD, 16 * TILE), BF16),
         v(tile16, F32),
         v(tile16, BF16),
-        v(tile16, BF16),
+        v((TILE, 16 * PAD), BF16),
         v(tile16, BF16),
         v((PAD, 16 * TILE), BF16),
         v((PAD, 16 * TILE), F32),
         v(tile16, F32),
         v(tile16, F32),
         v((16, TILE, 2 * PAD), BF16),
-        v((16, TILE, 2 * PAD), BF16),
-        v((2, half, 3 * PAD), BF16),
         v((half, 3 * PAD), BF16),
-        v((3, half, PAD), BF16),
         v((3, half, PAD), BF16),
         v((TILE, width), F32),
         v((TILE, width), F32),
         v((TILE, width), F32),
         v((TILE, width), F32),
-        v((TILE, width), F32),
-        v((3 * PAD, width), F32),
         v((8, 6 * width), F32),
         v((32, 8, 2 * PAD), F32),
         v((32, 8, 2 * PAD), F32),
+        v((TILE, width), BF16),
+        v((TILE, width), BF16),
+        v((TILE, hidden), BF16),
+        v((TILE, width), BF16),
+        v((TILE, width), BF16),
+        v((TILE, 2 * hidden), BF16),
+        v((TILE, 10 * PAD), BF16),
+        v((TILE, 10 * PAD), BF16),
+        v((TILE, 16 * PAD), BF16),
+        v((2, 80, hidden // 2), BF16),
+        v((2, half, 3 * PAD), BF16),
+        v((2, 80, 5 * PAD), BF16),
+        v((80, hidden // 2), BF16),
+        v((half, 3 * PAD), BF16),
+        v((80, 5 * PAD), BF16),
+        v((80, 5 * PAD), F32),
+        dma((3, 8)),
+        dma((3, 8)),
+        dma((3, 8)),
+        dma((3, 8)),
+        dma((3, 2)),
+        dma((3, 2)),
+        dma((3, 2)),
+        dma((3,)),
+        dma((3,)),
+        dma((2,)),
         dma((16, 4)),
         dma((16,)),
         dma,
@@ -1041,50 +1322,18 @@
         dma((3,)),
         dma((32,)),
         dma((32,)),
-        dma,
+        dma((2,)),
     ]
     return pl.pallas_call(
         block_kernel,
         out_shape=out_shape,
         in_specs=[vmem] * 5 + [any_] * 4 + [vmem] * 3 + [smem],
-        out_specs=[vmem] * 11 + [any_],
+        out_specs=[vmem] * 8 + [any_] * 7,
         scratch_shapes=scratch,
         compiler_params=pltpu.CompilerParams(
             collective_id=0, has_side_effects=True, vmem_limit_bytes=VMEM_LIMIT
         ),
     )(tokens, cotangent, act, ada, wh, wout, wup, wdown, wqkv, q_gain, k_gain, rope_table(), hw)
-
-
-def swap(value, axis, bit):
-    n = lax.axis_size(axis)
-    return lax.ppermute(value, axis, [(i, i ^ bit) for i in range(n)])
-
-
-def pick(value, index, axis):
-    return lax.dynamic_index_in_dim(value, index, axis, keepdims=False)
-
-
-def plane_grad(left, right):
-    img, ty, z = lax.axis_index("img"), lax.axis_index("ty"), lax.axis_index("tx")
-    rows, kl = left.shape
-    n = right.shape[1]
-    halves = left.reshape(rows, 2, kl // 2)
-    l2 = jnp.concatenate([pick(halves, img, 1), swap(pick(halves, 1 - img, 1), "img", 1)])
-    l4 = jnp.concatenate([l2, swap(l2, "ty", 2)])
-    l8 = jnp.concatenate([l4, swap(l4, "ty", 1)])
-    quarters = right.reshape(rows, 2, 2, n // 4)
-    y, c = ty // 2, ty % 2
-    mine = pick(quarters, y, 1)
-    theirs = swap(pick(quarters, 1 - y, 1), "ty", 2)
-    across = swap(jnp.stack([mine, theirs]), "img", 1)
-    r4 = jnp.concatenate([mine, across[0], theirs, across[1]])
-    r8 = jnp.concatenate([pick(r4, c, 1), swap(pick(r4, 1 - c, 1), "ty", 1)])
-    part = outer_sum(l8, r8).reshape(kl // 2, 2, 2, n // 16)
-    high, low = z // 2, z % 2
-    sent = swap(pick(part, 1 - low, 2).astype(jnp.bfloat16), "tx", 1)
-    part = pick(part, low, 2) + sent.astype(jnp.float32)
-    sent = swap(pick(part, 1 - high, 1).astype(jnp.bfloat16), "tx", 2)
-    return pick(part, high, 1) + sent.astype(jnp.float32)
 
 
 def head_weight(weight):
@@ -1114,7 +1363,7 @@
     width = tokens.shape[2]
     act = jax.nn.silu(class_embed + time_embed(timestep, width)).astype(BF16).astype(F32)
     pad = lambda g: jnp.broadcast_to(jnp.pad(g, (0, PAD - HEAD))[None], (8, PAD))
-    (mixed, tgrad, l_attn, l_h2, l_mid, r_ffn, r_branch, r_gu, qkv_grad, ada_grad, gains, _) = (
+    (mixed, tgrad, qkv_grad, ada_grad, gains, down_grad, up_grad, out_grad) = (
         run_block(
             tokens[0],
             cotangent[0],
@@ -1128,11 +1377,8 @@
             pad(q_gain),
             pad(k_gain),
             jnp.concatenate([grid_height, grid_width]),
-        )
-    )
-    down_grad = plane_grad(l_mid, r_ffn)
-    up_grad = plane_grad(l_h2, r_gu)
-    out_grad = plane_grad(l_attn, r_branch)
+        )[:8]
+    )
     return (
         mixed[None],
         tgrad[None],

time: 411 us -> 362 us (0.88)
  Pallas kernels: 236 us -> 340 us
  waiting for transfers between devices: 97.3 us -> 0 us
  starting transfers between devices: 19.1 us -> 0 us
  local copies, waits for them, and re-layouts: 34.5 us -> 16.1 us
  other arithmetic: 13.8 us -> 2.33 us
  matrix products: 7.4 us -> 0 us
    pallas_call x1, Pallas kernels: 236 us -> 340 us  [run_block(): pl.pallas_call(block_kernel, out_shape=out_shape, in_specs=[vmem] * 5 + [...]
    ppermute x24 -> x0, waiting for transfers between devices: 97.3 us -> none  [swap(): return lax.ppermute(value, axis, [(i, i ^ bit) for i in range(n)])]
    ppermute x24 -> x0, starting transfers between devices: 19.1 us -> none  [swap(): return lax.ppermute(value, axis, [(i, i ^ bit) for i in range(n)])]
    reshape x3 -> x0, local copies, waits for them, and re-layouts: 9.23 us -> none  [the longest x1 4.38 us: plane_grad(): part = outer_sum(l8, r8).reshape(kl // 2, 2, 2, n // 16)]
    dot_general x3 -> x0, matrix products: 7.4 us -> none  [outer_sum(): lax.dot_general(flat_rows(left), flat_rows(right), (((0,), (0,)), ((), ()...]
    dynamic_slice x6 -> x0, local copies, waits for them, and re-layouts: 6.87 us -> none  [pick(): return lax.dynamic_index_in_dim(value, index, axis, keepdims=False)]
    concatenate x9 -> x0, other arithmetic: 6.37 us -> none  [the longest x3 2.24 us: plane_grad(): r4 = jnp.concatenate([mine, across[0], theirs, across[1]])]
    unnamed x41 -> x13, local copies, waits for them, and re-layouts: 6.15 us -> 10.3 us
  transfers between devices with their start and end apart: 24 -> 0, of which waited for: 9 -> 0; matrix products, arithmetic and copies ran while one was open for 11% -> 0% of each run, Pallas kernels for 0% -> 0%
where the time goes in v2:
time: 362 us; the launch traced here: 361 us
  Pallas kernels  340 us (94%)
  local copies, waits for them, and re-layouts  16.1 us (4%)
    pallas_call x1, Pallas kernels, run_block(): pl.pallas_call(block_kernel, out_shape=out_shape, in_specs=[vmem] * 5 + [...  340 us
    unnamed x13, local copies, waits for them, and re-layouts  10.3 us

profile of v2, /device:TPU:0, one launch (start us, length us, event | category | flops | bytes accessed | tf_op | source)
XLA Modules:
  0.0 361.4 jit_solution(5817775545714612455)
XLA Ops:
  2.6 0.6 pad_add_fusion.hw
  3.2 0.7 pad.20
  3.8 0.7 pad.21
  4.5 0.6 broadcast_in_dim.34.k_gain
  5.1 0.6 broadcast_in_dim.33.q_gain
  5.7 0.1 fusion.6
  5.8 0.8 convert_reduce_fusion
  6.6 0.6 broadcast_in_dim.32.act
  7.2 1.3 constant_dynamic-slice_fusion.2
  8.5 0.9 fusion.5.wh
  9.4 340.3 %shard_map.205 = (bf16[128,1152]{1,0:T(8,128)(2,1)}, bf16[128,1152]{1,0:T(8,128)(2,1)}, f32[576,216]{1,0:T(8,128)}, f32[216,1152]{1,0:T(8,128)}, f32[8,128]{1,0:...) custom-call(bf16[128,1152]{1,0:T(8,128)(2,1)} %bitcast.11, ...), custom_call_target="tpu_custom_call" | custom-call | tf_op jit(solution)/shard_map/pallas_call | solution.py:1327
  349.7 0.0 copy-start.2
  349.7 0.0 copy-start.1
  349.7 0.0 copy-start
  349.7 1.3 slice_bitcast_fusion
  351.1 1.8 copy.24
  352.9 2.1 copy.25
  355.0 2.1 copy.23
  357.1 1.7 copy.33
  358.8 0.0 copy-done.2
  358.8 0.7 copy.34
  359.5 0.0 copy-done.1
  359.5 0.9 copy.35
  360.4 0.9 copy.36
  (1 shorter events, 0.0 us)
Async XLA Ops:
  349.7 9.1 %copy-start.2 = (bf16[128,1152]{1,0:T(8,128)(2,1)S(1)}, bf16[128,1152]{1,0:T(8,128)(2,1)}, u32[]{:S(2)}) copy-start(bf16[128,1152]{1,0:T(8,128)(2,1)} %get-tuple-element.18) | copy-start | bytes 884740
  349.7 9.8 %copy-start.1 = (f32[576,384]{1,0:T(8,128)S(1)}, f32[576,384]{1,0:T(8,128)}, u32[]{:S(2)}) copy-start(f32[576,384]{1,0:T(8,128)} %get-tuple-element.54) | copy-start | bytes 2654212
  349.7 10.7 %copy-start = (f32[216,1152]{1,0:T(8,128)S(1)}, f32[216,1152]{1,0:T(8,128)}, u32[]{:S(2)}) copy-start(f32[216,1152]{1,0:T(8,128)} %get-tuple-element.56) | copy-start | bytes 2985988

commit v3 on v2

--- a/solution.py
+++ b/solution.py
@@ -341,11 +341,23 @@
 
 
 def weight_chunks(width, hidden):
-    up = []
-    step = hidden // 4
-    for k in range(4):
-        up += [(UP, k * step, step), (UP, hidden + k * step, step)]
-    return [(OUT, 0, width)] + up + [(DOWN, 0, width), (QKV, 0, 3 * width)]
+    half = width // 2
+    quarter = hidden // 4
+    rows = hidden // 4
+
+    def up(k, along_z):
+        return [(UP, 2 * k + u, 0, half, quarter, along_z) for u in range(2)]
+
+    return (
+        [(OUT, 0, 0, half, width, True)]
+        + up(0, True)
+        + up(1, False)
+        + up(2, True)
+        + [(DOWN, 0, 0, rows, width, False)]
+        + up(3, True)
+        + [(DOWN, 0, rows, rows, width, False)]
+        + [(QKV, 0, 0, half, 14 * PAD, True), (QKV, 1, 0, half, 13 * PAD, False)]
+    )
 
 
 def block_kernel(
@@ -405,49 +417,74 @@
     vm = (woutv, wupv, wdownv, qkv_hbm)
     chunks = weight_chunks(width, hidden)
 
-    def wregion(i, owner, p):
-        m, c0, cn = chunks[i]
-        rows = hbm[m].shape[0]
-        return vm[m].at[pl.ds(owner * rows + p * (rows // 4), rows // 4), pl.ds(c0, cn)]
+    z_bit = lax.rem(z, 2)
+
+    def w_col(i, im):
+        m, k = chunks[i][:2]
+        if m == UP:
+            return (k % 2) * hidden + lax.rem(2 * im + k // 2, 4) * (hidden // 4)
+        return k * 14 * PAD
+
+    def w_own(i):
+        return 2 * z_bit + lax.rem(ty, 2) if chunks[i][5] else ty
+
+    def w_hop(i):
+        return dev(k=z ^ 1) if chunks[i][5] else dev(t=ty ^ 2)
+
+    def w_piece(ref, i, row0, im, p):
+        _, _, r0, rows, cols, _ = chunks[i]
+        n = rows // 4
+        return ref.at[
+            pl.ds(pl.multiple_of(row0 + r0 + p * n, 16), n),
+            pl.ds(pl.multiple_of(w_col(i, im), PAD), cols),
+        ]
+
+    def wregion(i, owner, im, p):
+        m = chunks[i][0]
+        return w_piece(vm[m], i, owner * hbm[m].shape[0], im, p)
 
     def w_x(i):
-        m, c0, cn = chunks[i]
-        piece = hbm[m].shape[0] // 4
-        return rcopy(
-            hbm[m].at[pl.ds(ty * piece, piece), pl.ds(c0, cn)],
-            wregion(i, img, ty), w_send.at[i, 0], w_recv.at[i, ty], dev(i=other),
-        )
+        p = w_own(i)
+        src = w_piece(hbm[chunks[i][0]], i, 0, other, p)
+        dst = wregion(i, img, other, p)
+        return rcopy(src, dst, w_send.at[i, 0], w_recv.at[i, p], dev(i=other))
+
+    def w_mine(i, p):
+        return wregion(i, other, img, p)
 
     def w_y(i):
-        ref = wregion(i, other, ty)
-        return rcopy(ref, ref, w_send.at[i, 1], w_recv.at[i, ty], dev(t=ty ^ 2))
+        ref = w_mine(i, w_own(i))
+        return rcopy(ref, ref, w_send.at[i, 1], w_recv.at[i, w_own(i)], w_hop(i))
 
     def w_c(i, p, slot):
-        ref = wregion(i, other, p)
+        ref = w_mine(i, p)
         return rcopy(ref, ref, w_send.at[i, slot], w_recv.at[i, p], dev(t=ty ^ 1))
 
     def w_wait(i, p):
-        ref = wregion(i, other, p)
+        ref = w_mine(i, p)
         rcopy(ref, ref, w_send.at[i, 0], w_recv.at[i, p], dev(t=ty ^ 1)).wait_recv()
 
-    def x_arrived(i):
-        w_wait(i, ty)
-        w_y(i).start()
-        w_c(i, ty, 2).start()
-
-    def y_arrived(i):
-        w_wait(i, ty ^ 2)
-        w_c(i, ty ^ 2, 3).start()
-
-    def w_done(i):
-        w_wait(i, ty ^ 1)
-        w_wait(i, ty ^ 3)
+    def x_arrived(*which):
+        for i in which:
+            w_wait(i, w_own(i))
+            w_y(i).start()
+            w_c(i, w_own(i), 2).start()
+
+    def hop_arrived(*which):
+        for i in which:
+            w_wait(i, w_own(i) ^ 2)
+            w_c(i, w_own(i) ^ 2, 3).start()
+
+    def w_done(*which):
+        for i in which:
+            w_wait(i, w_own(i) ^ 1)
+            w_wait(i, w_own(i) ^ 3)
 
     def w_drain(i):
         w_x(i).wait_send()
         w_y(i).wait_send()
-        w_c(i, ty, 2).wait_send()
-        w_c(i, ty ^ 2, 3).wait_send()
+        w_c(i, w_own(i), 2).wait_send()
+        w_c(i, w_own(i) ^ 2, 3).wait_send()
 
     def own(m):
         rows = hbm[m].shape[0]
@@ -457,7 +494,7 @@
     act_copy.start()
     actbuf[img] = act[...]
     wh_copy = rcopy(wh, whv.at[pl.ds(img * half, half)], wh_sem.at[0], wh_sem.at[1], dev(i=other))
-    wh_copy.start()
+    w_x(0).start()
     whv[pl.ds(pl.multiple_of(img * half, 64), half), :] = wh[...]
 
     def tok_at(chunk):
@@ -491,8 +528,6 @@
     t_forward(tok, b, True, True)
     for m in range(3):
         own(m).start()
-    for i in range(9):
-        w_x(i).start()
 
     act_copy.wait_recv()
     for i in range(2):
@@ -503,6 +538,9 @@
 
     loop(1, 32, lambda k: mod_copy(lax.rem(me + k, 32)).start())
     modbuf[me] = modsend[img]
+    wh_copy.start()
+    for i in range(1, len(chunks)):
+        w_x(i).start()
 
     for s in (1, 2, 3):
 
@@ -516,16 +554,15 @@
             t_wait(b + s)
             t_forward(tok_at(b + s), b + s, False, True)
 
+    x_arrived(0)
+
     def t_y(zz):
         chunk = (ty ^ 2) * 4 + zz
         t_wait(chunk)
         t_send(tok_at(chunk), chunk, 3, dev(t=ty ^ 1)).start()
 
     loop(0, 4, t_y)
-    x_arrived(0)
-    for i in range(1, 5):
-        x_arrived(i)
-    w_x(9).start()
+    x_arrived(1, 2)
     loop(0, 4, lambda zz: t_wait((ty ^ 1) * 4 + zz))
     loop(0, 4, lambda zz: t_wait((ty ^ 3) * 4 + zz))
 
@@ -624,10 +661,12 @@
         kt[:, pl.ds(pl.multiple_of(t * TILE, TILE), TILE)] = k_f.T.astype(BF16)
         va[t] = jnp.where((lane >= HEAD) & (lane < HEAD + 3), 1.0, v_r).astype(BF16)
 
-    loop(0, 16, head_rows)
-    for i in range(5, 9):
-        x_arrived(i)
-    y_arrived(0)
+    hop_arrived(0)
+    loop(0, 8, head_rows)
+    x_arrived(3, 4)
+    loop(8, 16, head_rows)
+    hop_arrived(1, 2)
+    x_arrived(5, 6)
 
     def head_lanes(h):
         return attn_in.at[:, pl.ds(pl.multiple_of(h * PAD, PAD), PAD)]
@@ -656,14 +695,12 @@
             def _():
                 at_copy(t).start()
 
-    loop(0, 8, attend)
+    loop(0, 4, attend)
+    x_arrived(7)
+    hop_arrived(3, 4)
+    loop(4, 8, attend)
     head_lanes(b)[...] = attn_send[b]
-    for i in range(1, 5):
-        y_arrived(i)
-    x_arrived(9)
-    w_x(10).start()
-    for i in range(5, 9):
-        y_arrived(i)
+    x_arrived(8, 9)
 
     def at_wait(k):
         p = lax.rem(b + k, 16)
@@ -734,8 +771,14 @@
             ),
         ]
 
-    def g_start(m):
-        for copy in g_first(m) + g_own(m):
+    def g_x(m):
+        for k in (0, 3):
+            g_first(m)[k].start()
+
+    def g_yc(m):
+        for k in (1, 2, 4, 5):
+            g_first(m)[k].start()
+        for copy in g_own(m):
             copy.start()
 
     def g_hop(m):
@@ -779,6 +822,7 @@
     )
     l_attn[...] = attn.astype(BF16)
     put_halves(l_attns, attn)
+    hop_arrived(5, 6)
     own(OUT).wait()
     w_done(0)
     own_valid = tile_layout(b)[0]
@@ -790,6 +834,7 @@
         branchv[:, at] = dot(l_attn[...], woutv[:, at])
 
     loop(0, 3, project)
+    x_arrived(10)
     x = tok[...].astype(F32)
     x1 = x + keep * gate1() * branchv[...]
     x1v[...] = x1
@@ -802,16 +847,13 @@
     put_blocks(attn_in, d_ffn)
     ffnv[...] = jnp.zeros_like(ffnv)
     dh2v[...] = jnp.zeros_like(dh2v)
-    y_arrived(9)
-    for i in range(1, 10):
-        w_done(i)
     own(UP).wait()
     own(DOWN).wait()
     step = 256
 
     def mlp(j):
-        g_at = pl.ds(pl.multiple_of(j * step, step), step)
-        u_at = pl.ds(pl.multiple_of(hidden + j * step, step), step)
+        g_at = pl.ds(pl.multiple_of(j, step), step)
+        u_at = pl.ds(pl.multiple_of(hidden + j, step), step)
         h2 = l_h2[...]
         gate = dot(h2, wupv[:, g_at])
         up = dot(h2, wupv[:, u_at])
@@ -828,10 +870,21 @@
         r_gu[:, u_at] = d_up
         dh2v[...] += dot_nt(d_gate, wupv[:, g_at]) + dot_nt(d_up, wupv[:, u_at])
 
-    loop(0, hidden // step, mlp)
-    g_start(0)
-    g_start(1)
-    x_arrived(10)
+    def mlp_quarter(k):
+        first = lax.rem(2 * img + k, 4) * (hidden // 4)
+        loop(0, hidden // 4 // step, lambda j: mlp(first + j * step))
+
+    w_done(1, 2)
+    mlp_quarter(0)
+    hop_arrived(7, 8, 9)
+    w_done(3, 4)
+    mlp_quarter(1)
+    hop_arrived(10)
+    w_done(5, 6, 7)
+    mlp_quarter(2)
+    w_done(8, 9, 10)
+    mlp_quarter(3)
+    g_x(1)
     ffn = ffnv[...]
     g = cot[...].astype(F32)
     x1 = x1v[...]
@@ -874,15 +927,15 @@
 
     loop(1, 16, lambda k: do_copy(lax.rem(b + k, 16)).start())
     do_in[b] = attn_send[b]
-    g_start(2)
-    y_arrived(10)
+    g_yc(1)
+    x_arrived(11, 12)
 
     def do_wait(k):
         p = lax.rem(b + k, 16)
         rcopy(attn_send.at[p], do_in.at[p], do_s.at[p], do_r.at[p], dev_tile(p)).wait()
 
     loop(1, 16, do_wait)
-    g_hop(0)
+    hop_arrived(11, 12)
 
     def delta(t):
         d = do_in[t].astype(F32)
@@ -905,9 +958,12 @@
 
     loop(0, 4, attend_back)
     g_hop(1)
+    g_x(0)
+    g_x(2)
     loop(4, 8, attend_back)
 
-    for i in range(11):
+    w_done(11, 12)
+    for i in range(len(chunks)):
         w_drain(i)
     gain_grad[...] = jnp.zeros_like(gain_grad)
 
@@ -944,103 +1000,8 @@
 
     loop(0, 16, heads_back)
     dqkv_in[b] = dq_rows(b)[...]
-    g_hop(2)
-    g_hop2(0)
-
-    sums_t = (branchv, ffnv, dqt.at[:, pl.ds(0, width)])
-    for ref in sums_t:
-        ref[...] = jnp.zeros((PAD, width), F32)
-
-    def dw_rows(k):
-        at = pl.ds(pl.multiple_of(k * 2 * TILE, TILE), 2 * TILE)
-        term = dot_tn(wdownv[at, 0 : 3 * PAD], tok_all[at, :])
-        for p in range(3):
-            sums_t[p][...] += term[p * PAD : (p + 1) * PAD]
-
-    loop(0, 8, dw_rows)
-    for p in range(3):
-        wdownv[0:width, (5 + p) * PAD : (6 + p) * PAD] = sums_t[p][...].T.astype(BF16)
-
-    def dw_half(i):
-        return wdownv.at[pl.ds(pl.multiple_of(i * half, 64), half), pl.ds(5 * PAD, 3 * PAD)]
-
-    dw_copy = rcopy(dw_half(other), dw_in, dw_sem.at[0], dw_sem.at[1], dev(i=other))
-    dw_copy.start()
-    g_hop2(1)
-    g_hop2(2)
-    w_done(10)
-
-    loads = [
-        pltpu.make_async_copy(
-            src, wupv.at[pl.ds(owner * half, half), pl.ds(0, 3 * width)], loc.at[k]
-        )
-        for k, (src, owner) in enumerate(
-            ((wqkv, img), (qkv_hbm.at[pl.ds(other * half, half)], other))
-        )
-    ]
-    for load in loads:
-        load.start()
-
-    def dq_wait(k):
-        p = lax.rem(b + k, 16)
-        rcopy(dq_rows(p), dqkv_in.at[p], dq_s.at[p], dq_r.at[p], dev_tile(p)).wait()
-
-    loop(1, 16, dq_wait)
-    dw_copy.wait()
-    dw_sum = dw_half(img)[...].astype(F32) + dw_in[...].astype(F32)
-
-    def pc_send(p):
-        return wdownv.at[pl.ds(width, half), pl.ds((5 + p) * PAD, PAD)]
-
-    for p in range(3):
-        pc_send(p)[...] = dw_sum[:, p * PAD : (p + 1) * PAD].astype(BF16)
-
-    def pc_copy(p):
-        group = 16 * p + b
-        to, slot = group // 3, lax.rem(group, 3)
-        return to, rcopy(
-            pc_send(p), pc_in.at[slot], pc_s.at[p], pc_r.at[slot], dev_tile(to)
-        )
-
-    for p in range(3):
-        to, copy = pc_copy(p)
-
-        @pl.when(to != b)
-        def _():
-            copy.start()
-
-        @pl.when(to == b)
-        def _():
-            pc_in[lax.rem(16 * p + b, 3)] = pc_send(p)[...]
-
-    for load in loads:
-        load.wait()
-    dqkv = [dqkv_in[h].astype(F32) for h in range(16)]
-    def own_part(p):
-        return slice(16 * TILE + p * TILE, 16 * TILE + (p + 1) * TILE)
-
-    for p in range(3):
-        wdownv[own_part(p), :] = jnp.concatenate(
-            [dqkv[h][:, p * HEAD : (p + 1) * HEAD] for h in range(16)], axis=1
-        ).astype(BF16)
-
-    def h1_back(k):
-        at = pl.ds(pl.multiple_of(k * cols, PAD), cols)
-        dh2v[:, at] = sum(
-            dot_nt(wdownv[own_part(p), :], wupv[at, p * width : (p + 1) * width])
-            for p in range(3)
-        )
-
-    loop(0, 3, h1_back)
-    d_h1 = dh2v[...]
-    x = tok[...].astype(F32)
-    r1 = lax.rsqrt(jnp.mean(x * x, axis=1, keepdims=True) + EPS)
-    norm1 = x * r1
-    dmod_put(1, colsum(d_h1 * norm1))
-    dmod_put(0, colsum(d_h1))
-    d_n1 = d_h1 * (1.0 + scale1())
-    back = r1 * (d_n1 - norm1 * jnp.mean(d_n1 * norm1, axis=1, keepdims=True))
-    tgrad[...] = (x1v[...] + back).astype(BF16)
+    g_yc(0)
+    g_yc(2)
 
     high, low = z // 2, lax.rem(z, 2)
     l0 = 3 * width
@@ -1134,18 +1095,76 @@
         z_copy2(m).wait()
         z_own[m][...] += zb[m][...].astype(F32)
 
-    for m in range(3):
-        g_done(m)
-        z_load(m)
-        z_product(m)
-    for m in range(3):
-        z_second(m)
-    for m in range(3):
-        z_last(m)
-    for m in range(3):
-        g_drain(m)
-    down_grad[...] = z_own[0][...].T[:, 0:HEAD]
-    out_grad[...] = z_own[2][...].T[0:half, 0:HEAD]
+    sums_t = (branchv, ffnv, dh2v)
+    for ref in sums_t:
+        ref[...] = jnp.zeros((PAD, width), F32)
+
+    def dw_rows(k):
+        at = pl.ds(pl.multiple_of(k * 2 * TILE, TILE), 2 * TILE)
+        term = dot_tn(wdownv[at, 0 : 3 * PAD], tok_all[at, :])
+        for p in range(3):
+            sums_t[p][...] += term[p * PAD : (p + 1) * PAD]
+
+    loop(0, 8, dw_rows)
+    for p in range(3):
+        wdownv[0:width, (5 + p) * PAD : (6 + p) * PAD] = sums_t[p][...].T.astype(BF16)
+
+    def dw_half(i):
+        return wdownv.at[pl.ds(pl.multiple_of(i * half, 64), half), pl.ds(5 * PAD, 3 * PAD)]
+
+    dw_copy = rcopy(dw_half(other), dw_in, dw_sem.at[0], dw_sem.at[1], dev(i=other))
+    dw_copy.start()
+    g_hop2(1)
+    g_done(1)
+    z_load(1)
+    z_product(1)
+    g_hop(0)
+    g_hop(2)
+
+    loads = [
+        pltpu.make_async_copy(
+            src, wupv.at[pl.ds(owner * half, half), pl.ds(0, 3 * width)], loc.at[k]
+        )
+        for k, (src, owner) in enumerate(
+            ((wqkv, img), (qkv_hbm.at[pl.ds(other * half, half)], other))
+        )
+    ]
+    for load in loads:
+        load.start()
+
+    def dq_wait(k):
+        p = lax.rem(b + k, 16)
+        rcopy(dq_rows(p), dqkv_in.at[p], dq_s.at[p], dq_r.at[p], dev_tile(p)).wait()
+
+    loop(1, 16, dq_wait)
+    for load in loads:
+        load.wait()
+    dqkv = [dqkv_in[h].astype(F32) for h in range(16)]
+    def own_part(p):
+        return slice(16 * TILE + p * TILE, 16 * TILE + (p + 1) * TILE)
+
+    for p in range(3):
+        wdownv[own_part(p), :] = jnp.concatenate(
+            [dqkv[h][:, p * HEAD : (p + 1) * HEAD] for h in range(16)], axis=1
+        ).astype(BF16)
+
+    def h1_back(k):
+        at = pl.ds(pl.multiple_of(k * cols, PAD), cols)
+        dh2v[:, at] = sum(
+            dot_nt(wdownv[own_part(p), :], wupv[at, p * width : (p + 1) * width])
+            for p in range(3)
+        )
+
+    loop(0, 3, h1_back)
+    d_h1 = dh2v[...]
+    x = tok[...].astype(F32)
+    r1 = lax.rsqrt(jnp.mean(x * x, axis=1, keepdims=True) + EPS)
+    norm1 = x * r1
+    dmod_put(1, colsum(d_h1 * norm1))
+    dmod_put(0, colsum(d_h1))
+    d_n1 = d_h1 * (1.0 + scale1())
+    back = r1 * (d_n1 - norm1 * jnp.mean(d_n1 * norm1, axis=1, keepdims=True))
+    tgrad[...] = (x1v[...] + back).astype(BF16)
 
     dsend[...] = jnp.zeros_like(dsend)
     for s in range(32):
@@ -1158,6 +1177,47 @@
     loop(1, 32, lambda k: dm_copy(lax.rem(me + k, 32)).start())
     dbuf[me] = dsend[me]
 
+    z_second(1)
+    for m in (0, 2):
+        g_hop2(m)
+        g_done(m)
+        z_load(m)
+        z_product(m)
+    dw_copy.wait()
+    dw_sum = dw_half(img)[...].astype(F32) + dw_in[...].astype(F32)
+
+    def pc_send(p):
+        return wdownv.at[pl.ds(width, half), pl.ds((5 + p) * PAD, PAD)]
+
+    for p in range(3):
+        pc_send(p)[...] = dw_sum[:, p * PAD : (p + 1) * PAD].astype(BF16)
+
+    def pc_copy(p):
+        group = 16 * p + b
+        to, slot = group // 3, lax.rem(group, 3)
+        return to, rcopy(
+            pc_send(p), pc_in.at[slot], pc_s.at[p], pc_r.at[slot], dev_tile(to)
+        )
+
+    for p in range(3):
+        to, copy = pc_copy(p)
+
+        @pl.when(to != b)
+        def _():
+            copy.start()
+
+        @pl.when(to == b)
+        def _():
+            pc_in[lax.rem(16 * p + b, 3)] = pc_send(p)[...]
+
+    for m in (0, 2):
+        z_second(m)
+    for m in (1, 0, 2):
+        z_last(m)
+    for m in range(3):
+        g_drain(m)
+    down_grad[...] = z_own[0][0:HEAD, :]
+    out_grad[...] = z_own[2][0:HEAD, 0:half]
     for slot in range(3):
         group = 3 * b + slot
         src = lax.rem(group, 16)
@@ -1168,9 +1228,9 @@
                 pc_send(0), pc_in.at[slot], pc_s.at[0], pc_r.at[slot], dev_tile(src)
             ).wait_recv()
 
-    qkv_grad[...] = jnp.concatenate(
-        [pc_in[slot].astype(F32)[:, 0:HEAD] for slot in range(3)], axis=1
-    )
+    for slot in range(3):
+        at = slice(slot * HEAD, (slot + 1) * HEAD)
+        qkv_grad[at, :] = pc_in[slot].astype(F32).T[0:HEAD, :]
     for p in range(3):
         to, copy = pc_copy(p)
 
@@ -1224,12 +1284,12 @@
     out_shape = (
         sds((TILE, width), BF16),
         sds((TILE, width), BF16),
-        sds((half, 3 * HEAD), F32),
+        sds((3 * HEAD, half), F32),
         sds((part, width), F32),
         sds((8, PAD), F32),
-        sds((hidden // 2, HEAD), F32),
+        sds((HEAD, hidden // 2), F32),
         sds((half, 3 * PAD), F32),
-        sds((half, HEAD), F32),
+        sds((HEAD, half), F32),
         sds((width, 3 * width), BF16),
         sds((8 * TILE, hidden // 2), BF16),
         sds((8 * TILE, 5 * PAD), BF16),
@@ -1382,10 +1442,10 @@
     return (
         mixed[None],
         tgrad[None],
-        qkv_grad,
-        out_grad,
+        qkv_grad.T,
+        out_grad.T,
         up_grad,
-        down_grad,
+        down_grad.T,
         ada_grad,
         gains[0, :HEAD],
         gains[1, :HEAD],

time: 362 us -> 290 us (0.80)
  Pallas kernels: 340 us -> 268 us
    pallas_call x1, Pallas kernels: 340 us -> 268 us  [run_block(): pl.pallas_call(block_kernel, out_shape=out_shape, in_specs=[vmem] * 5 + [...]
    unnamed x13 -> x11, local copies, waits for them, and re-layouts: 10.3 us -> 10.7 us
where the time goes in v3:
time: 290 us; the launch traced here: 289 us
  Pallas kernels  268 us (92%)
  local copies, waits for them, and re-layouts  16.5 us (6%)
    pallas_call x1, Pallas kernels, run_block(): pl.pallas_call(block_kernel, out_shape=out_shape, in_specs=[vmem] * 5 + [...  268 us
    unnamed x11, local copies, waits for them, and re-layouts  10.7 us

profile of v3, /device:TPU:0, one launch (start us, length us, event | category | flops | bytes accessed | tf_op | source)
XLA Modules:
  0.0 289.3 jit_solution(3061000438590720847)
XLA Ops:
  2.6 0.6 pad_add_fusion.hw
  3.2 0.7 pad.20
  3.8 0.7 pad.21
  4.5 0.6 broadcast_in_dim.34.k_gain
  5.1 0.6 broadcast_in_dim.33.q_gain
  5.7 0.1 fusion.6
  5.8 0.8 convert_reduce_fusion
  6.6 0.6 broadcast_in_dim.32.act
  7.2 1.3 constant_dynamic-slice_fusion.2
  8.5 0.9 fusion.5.wh
  9.4 267.8 %shard_map.205 = (bf16[128,1152]{1,0:T(8,128)(2,1)}, bf16[128,1152]{1,0:T(8,128)(2,1)}, f32[216,576]{1,0:T(8,128)}, f32[216,1152]{1,0:T(8,128)}, f32[8,128]{1,0:...) custom-call(bf16[128,1152]{1,0:T(8,128)(2,1)} %bitcast.16, ...), custom_call_target="tpu_custom_call" | custom-call | tf_op jit(solution)/shard_map/pallas_call | solution.py:1387
  277.2 0.0 copy-start.1
  277.2 0.0 copy-start
  277.2 1.3 slice_bitcast_fusion
  278.5 1.7 copy.33
  280.2 1.7 copy.34
  281.9 1.9 copy.35
  283.8 1.6 copy.36
  285.4 2.1 copy.37
  287.5 0.0 copy-done.1
  287.6 0.8 copy.38
  288.3 0.0 copy-done
  288.3 0.9 copy.39
Async XLA Ops:
  277.2 10.4 %copy-start.1 = (f32[72,1536]{1,0:T(8,128)S(1)}, f32[72,1536]{1,0:T(8,128)}, u32[]{:S(2)}) copy-start(f32[72,1536]{1,0:T(8,128)} %get-tuple-element.22) | copy-start | bytes 1327108
  277.2 11.1 %copy-start = (f32[216,1152]{1,0:T(8,128)S(1)}, f32[216,1152]{1,0:T(8,128)}, u32[]{:S(2)}) copy-start(f32[216,1152]{1,0:T(8,128)} %get-tuple-element.47) | copy-start | bytes 2985988

commit v4 on v3

--- a/solution.py
+++ b/solution.py
@@ -343,20 +343,19 @@
 def weight_chunks(width, hidden):
     half = width // 2
     quarter = hidden // 4
-    rows = hidden // 4
-
-    def up(k, along_z):
-        return [(UP, 2 * k + u, 0, half, quarter, along_z) for u in range(2)]
+
+    def up(k):
+        return [(UP, 2 * k + u, 0, half, quarter, "yz") for u in range(2)]
 
     return (
-        [(OUT, 0, 0, half, width, True)]
-        + up(0, True)
-        + up(1, False)
-        + up(2, True)
-        + [(DOWN, 0, 0, rows, width, False)]
-        + up(3, True)
-        + [(DOWN, 0, rows, rows, width, False)]
-        + [(QKV, 0, 0, half, 14 * PAD, True), (QKV, 1, 0, half, 13 * PAD, False)]
+        [(OUT, 0, 0, half, width, "z")]
+        + up(0)
+        + up(1)
+        + up(2)
+        + [(DOWN, 0, 0, quarter, width, "yz")]
+        + up(3)
+        + [(DOWN, 0, quarter, quarter, width, "yz")]
+        + [(QKV, 0, 0, half, 14 * PAD, "z"), (QKV, 1, 0, half, 13 * PAD, "")]
     )
 
 
@@ -366,13 +365,13 @@
     lb_down, lb_up, lb_out, rb_down, rb_up, rb_out,
     tok_all, whv, woutv, wupv, wdownv, actbuf, modsend, modbuf, modv,
     cosv, sinv, qraw, kraw, qa, ka, va, kt, qt, onorm, attn_send, attn_in,
-    do_in, dot_t, dqt, dkv, dvv, dqkv_in, dw_in, pc_in,
+    do_in, dot_t, dqt, dkv_in, dq_in, dw_in, pc_in,
     x1v, branchv, ffnv, dh2v, dmod, dsend, dbuf,
     l_attn, l_h2, l_mid, r_ffn, r_branch, r_gu, l_h2s, l_attns, r_branchs,
     za_down, za_up, za_out, zb_down, zb_up, zb_out, z_out,
-    gl_s, gl_r, gr_s, gr_r, g_loc, za_s, za_r, zb_s, zb_r, z_loc,
+    gl_s, gl_r, gr_s, gr_r, gu_s, gu_r, g_loc, za_s, za_r, zb_s, zb_r, z_loc,
     tok_send, tok_recv, tok_loc, w_send, w_recv, w_loc, wh_sem, act_sem, mod_s, mod_r,
-    at_s, at_r, do_s, do_r, dq_s, dq_r, dw_sem, pc_s, pc_r, dm_s, dm_r, loc,
+    at_s, at_r, do_s, do_r, dq_s, dq_r, dkv_s, dkv_r, dw_sem, pc_s, pc_r, dm_s, dm_r, loc,
 ):
     img, ty, z = lax.axis_index("img"), lax.axis_index("ty"), lax.axis_index("tx")
     b = ty * 4 + z
@@ -417,74 +416,115 @@
     vm = (woutv, wupv, wdownv, qkv_hbm)
     chunks = weight_chunks(width, hidden)
 
-    z_bit = lax.rem(z, 2)
-
-    def w_col(i, im):
-        m, k = chunks[i][:2]
+    y, c, z_bit = ty // 2, lax.rem(ty, 2), lax.rem(z, 2)
+    to_x, to_y, to_z, to_c = dev(i=other), dev(t=ty ^ 2), dev(k=z ^ 1), dev(t=ty ^ 1)
+    OWN, FROM_Y, FROM_Z, FAR_A, FAR_B, SIBLING = range(6)
+
+    def w_ref(ref, i, row0, im, rel, sib=False):
+        m, k, r0, rows, cols, ways = chunks[i]
+        yy = 1 - y if rel in (FROM_Y, FAR_A, FAR_B) else y
+        zz = 1 - z_bit if rel in (FROM_Z, FAR_A, FAR_B) else z_bit
+        cc = 1 - c if sib else c
+        col = k * 14 * PAD if m == QKV else 0
         if m == UP:
-            return (k % 2) * hidden + lax.rem(2 * im + k // 2, 4) * (hidden // 4)
-        return k * 14 * PAD
-
-    def w_own(i):
-        return 2 * z_bit + lax.rem(ty, 2) if chunks[i][5] else ty
-
-    def w_hop(i):
-        return dev(k=z ^ 1) if chunks[i][5] else dev(t=ty ^ 2)
-
-    def w_piece(ref, i, row0, im, p):
-        _, _, r0, rows, cols, _ = chunks[i]
-        n = rows // 4
+            col = (k % 2) * hidden + lax.rem(2 * im + k // 2, 4) * (hidden // 4)
+        if ways == "yz" and m == UP:
+            n, p = rows // 4, 2 * yy + zz
+            cols = cols // 2
+            col = col + cc * cols
+        elif ways == "yz":
+            n, p = rows // 8, 4 * yy + 2 * zz + cc
+        elif ways == "":
+            n, p = rows // 2, cc
+        else:
+            n, p = rows // 4, 2 * (yy if ways == "y" else zz) + cc
+        row, size, first = row0 + r0 + p * n, n, (n // 32 + (n // 16) % 2) * 16
+        if rel == FAR_A:
+            size = first
+        if rel == FAR_B:
+            row, size = row + first, n - first
         return ref.at[
-            pl.ds(pl.multiple_of(row0 + r0 + p * n, 16), n),
-            pl.ds(pl.multiple_of(w_col(i, im), PAD), cols),
+            pl.ds(pl.multiple_of(row, 16), size), pl.ds(pl.multiple_of(col, PAD), cols)
         ]
 
-    def wregion(i, owner, im, p):
+    def w_mine(i, rel, sib=False):
         m = chunks[i][0]
-        return w_piece(vm[m], i, owner * hbm[m].shape[0], im, p)
+        return w_ref(vm[m], i, other * hbm[m].shape[0], img, rel, sib)
 
     def w_x(i):
-        p = w_own(i)
-        src = w_piece(hbm[chunks[i][0]], i, 0, other, p)
-        dst = wregion(i, img, other, p)
-        return rcopy(src, dst, w_send.at[i, 0], w_recv.at[i, p], dev(i=other))
-
-    def w_mine(i, p):
-        return wregion(i, other, img, p)
-
-    def w_y(i):
-        ref = w_mine(i, w_own(i))
-        return rcopy(ref, ref, w_send.at[i, 1], w_recv.at[i, w_own(i)], w_hop(i))
-
-    def w_c(i, p, slot):
-        ref = w_mine(i, p)
-        return rcopy(ref, ref, w_send.at[i, slot], w_recv.at[i, p], dev(t=ty ^ 1))
-
-    def w_wait(i, p):
-        ref = w_mine(i, p)
-        rcopy(ref, ref, w_send.at[i, 0], w_recv.at[i, p], dev(t=ty ^ 1)).wait_recv()
+        m = chunks[i][0]
+        src = w_ref(hbm[m], i, 0, other, OWN)
+        dst = w_ref(vm[m], i, img * hbm[m].shape[0], other, OWN)
+        return rcopy(src, dst, w_send.at[i, 0], w_recv.at[i, 0], to_x)
+
+    def w_copy(i, slot, held, rel, to):
+        ref = w_mine(i, held)
+        return rcopy(ref, ref, w_send.at[i, slot], w_recv.at[i, rel], to)
+
+    def w_wait(i, rel, sib=False):
+        ref = w_mine(i, rel, sib)
+        at = rel + SIBLING if sib else rel
+        rcopy(ref, ref, w_send.at[i, 0], w_recv.at[i, at], to_c).wait_recv()
+
+    def w_sends(i):
+        ways = chunks[i][5]
+        first = [w_copy(i, 1, OWN, SIBLING + OWN, to_c)]
+        if "y" in ways:
+            first.append(w_copy(i, 2, OWN, FROM_Y, to_y))
+        if "z" in ways:
+            first.append(w_copy(i, 3, OWN, FROM_Z, to_z))
+        sends = {OWN: first}
+        if "z" in ways:
+            sends[FROM_Z] = [w_copy(i, 4, FROM_Z, SIBLING + FROM_Z, to_c)]
+        if "y" in ways:
+            sends[FROM_Y] = [w_copy(i, 5, FROM_Y, SIBLING + FROM_Y, to_c)]
+        if ways == "yz":
+            far_a, far_b = w_far(i)
+            sends[FROM_Z].insert(0, far_a)
+            sends[FROM_Y].insert(0, far_b)
+            sends[FAR_A] = [w_copy(i, 8, FAR_A, SIBLING + FAR_A, to_c)]
+            sends[FAR_B] = [w_copy(i, 9, FAR_B, SIBLING + FAR_B, to_c)]
+        return sends
+
+    def w_far(i):
+        m, _, _, rows, _, _ = chunks[i]
+        n = rows // (4 if m == UP else 8)
+        first = (n // 32 + (n // 16) % 2) * 16
+        a = w_mine(i, FROM_Z).at[pl.ds(0, first)]
+        b_ = w_mine(i, FROM_Y).at[pl.ds(first, n - first)]
+        return (
+            rcopy(a, a, w_send.at[i, 6], w_recv.at[i, FAR_A], to_y),
+            rcopy(b_, b_, w_send.at[i, 7], w_recv.at[i, FAR_B], to_z),
+        )
+
+    def w_pass(which, rels):
+        for i in which:
+            sends = w_sends(i)
+            for rel in rels:
+                if rel in sends:
+                    w_wait(i, rel)
+                    for copy in sends[rel]:
+                        copy.start()
 
     def x_arrived(*which):
-        for i in which:
-            w_wait(i, w_own(i))
-            w_y(i).start()
-            w_c(i, w_own(i), 2).start()
+        w_pass(which, (OWN,))
 
     def hop_arrived(*which):
-        for i in which:
-            w_wait(i, w_own(i) ^ 2)
-            w_c(i, w_own(i) ^ 2, 3).start()
+        w_pass(which, (FROM_Z, FROM_Y))
+
+    def far_arrived(*which):
+        w_pass(which, (FAR_A, FAR_B))
 
     def w_done(*which):
         for i in which:
-            w_wait(i, w_own(i) ^ 1)
-            w_wait(i, w_own(i) ^ 3)
+            for rel in w_sends(i):
+                w_wait(i, rel, True)
 
     def w_drain(i):
         w_x(i).wait_send()
-        w_y(i).wait_send()
-        w_c(i, w_own(i), 2).wait_send()
-        w_c(i, w_own(i) ^ 2, 3).wait_send()
+        for copies in w_sends(i).values():
+            for copy in copies:
+                copy.wait_send()
 
     def own(m):
         rows = hbm[m].shape[0]
@@ -494,7 +534,8 @@
     act_copy.start()
     actbuf[img] = act[...]
     wh_copy = rcopy(wh, whv.at[pl.ds(img * half, half)], wh_sem.at[0], wh_sem.at[1], dev(i=other))
-    w_x(0).start()
+    for i in range(3):
+        w_x(i).start()
     whv[pl.ds(pl.multiple_of(img * half, 64), half), :] = wh[...]
 
     def tok_at(chunk):
@@ -539,7 +580,7 @@
     loop(1, 32, lambda k: mod_copy(lax.rem(me + k, 32)).start())
     modbuf[me] = modsend[img]
     wh_copy.start()
-    for i in range(1, len(chunks)):
+    for i in range(3, len(chunks)):
         w_x(i).start()
 
     for s in (1, 2, 3):
@@ -554,7 +595,7 @@
             t_wait(b + s)
             t_forward(tok_at(b + s), b + s, False, True)
 
-    x_arrived(0)
+    x_arrived(0, 1, 2)
 
     def t_y(zz):
         chunk = (ty ^ 2) * 4 + zz
@@ -562,7 +603,7 @@
         t_send(tok_at(chunk), chunk, 3, dev(t=ty ^ 1)).start()
 
     loop(0, 4, t_y)
-    x_arrived(1, 2)
+    hop_arrived(0)
     loop(0, 4, lambda zz: t_wait((ty ^ 1) * 4 + zz))
     loop(0, 4, lambda zz: t_wait((ty ^ 3) * 4 + zz))
 
@@ -661,12 +702,16 @@
         kt[:, pl.ds(pl.multiple_of(t * TILE, TILE), TILE)] = k_f.T.astype(BF16)
         va[t] = jnp.where((lane >= HEAD) & (lane < HEAD + 3), 1.0, v_r).astype(BF16)
 
-    hop_arrived(0)
+    x_arrived(3, 4)
+    hop_arrived(1, 2)
     loop(0, 8, head_rows)
-    x_arrived(3, 4)
+    x_arrived(5, 6)
+    hop_arrived(3, 4)
+    far_arrived(1, 2)
     loop(8, 16, head_rows)
-    hop_arrived(1, 2)
-    x_arrived(5, 6)
+    x_arrived(7)
+    hop_arrived(5, 6)
+    far_arrived(3, 4)
 
     def head_lanes(h):
         return attn_in.at[:, pl.ds(pl.multiple_of(h * PAD, PAD), PAD)]
@@ -695,12 +740,11 @@
             def _():
                 at_copy(t).start()
 
-    loop(0, 4, attend)
-    x_arrived(7)
-    hop_arrived(3, 4)
-    loop(4, 8, attend)
+    loop(0, 8, attend)
     head_lanes(b)[...] = attn_send[b]
-    x_arrived(8, 9)
+    x_arrived(8, 9, 10)
+    hop_arrived(7)
+    far_arrived(5, 6)
 
     def at_wait(k):
         p = lax.rem(b + k, 16)
@@ -724,7 +768,6 @@
 
     l_src, l_all = (l_mid, l_h2s, l_attns), (lb_down, lb_up, lb_out)
     r_src, r_all = (attn_in, r_gu, r_branchs), (rb_down, rb_up, rb_out)
-    y, c = ty // 2, lax.rem(ty, 2)
 
     def slot_rows(i, t):
         return pl.ds(pl.multiple_of((i * 4 + t) * TILE, TILE), TILE)
@@ -742,8 +785,6 @@
         if k in (2, 4, 5, 6):
             dst = r_all[m].at[slot_rows(i, t), lanes_at(1 - c, n)]
         return rcopy(dst if src is None else src, dst, gr_s.at[m, k], gr_r.at[m, i * 4 + t], d)
-
-    to_x, to_y, to_c = dev(i=other), dev(t=ty ^ 2), dev(t=ty ^ 1)
 
     def l_part(m, k):
         return l_src[m].at[:, lanes_at(k, l_src[m].shape[1] // 2)]
@@ -771,32 +812,74 @@
             ),
         ]
 
-    def g_x(m):
-        for k in (0, 3):
-            g_first(m)[k].start()
-
-    def g_yc(m):
-        for k in (1, 2, 4, 5):
-            g_first(m)[k].start()
-        for copy in g_own(m):
-            copy.start()
-
-    def g_hop(m):
+    def gl_x(m):
+        g_first(m)[0].start()
+
+    def gl_yc(m):
+        g_first(m)[2].start()
+        g_first(m)[4].start()
+        g_own(m)[0].start()
+
+    def gr_x(m):
+        g_first(m)[3].start()
+
+    def gr_yc(m):
+        if m != 1:
+            g_first(m)[1].start()
+        g_first(m)[5].start()
+        g_own(m)[1].start()
+
+    def gu_lanes(i, k, base=0):
+        n = hidden // 4
+        return pl.ds(pl.multiple_of(base + lax.rem(2 * i + k, 4) * n, PAD), n)
+
+    def gu_copy(w, k):
+        dst = rb_up.at[slot_rows(img, ty ^ 2 if w == 2 else ty), gu_lanes(img, k)]
+        src = dst
+        if w < 2:
+            src = r_gu.at[:, gu_lanes(img, k, (1 - y if w == 0 else y) * hidden)]
+        return rcopy(src, dst, gu_s.at[w, k], gu_r.at[w, k], to_y if w == 0 else to_x)
+
+    def gu_wait(w, k):
+        i, t = (img, ty ^ 2) if w == 0 else (other, ty if w == 1 else ty ^ 2)
+        ref = rb_up.at[slot_rows(i, t), gu_lanes(i, k)]
+        rcopy(ref, ref, gu_s.at[w, k], gu_r.at[w, k], to_x).wait_recv()
+
+    def gu_hop(k):
+        gu_wait(0, k)
+        gu_copy(2, k).start()
+
+    def gl_hop(m):
         g_left(m, 0, None, other, ty, to_x).wait_recv()
         g_left(m, 3, None, other, ty, to_y).start()
         g_left(m, 4, None, other, ty, to_c).start()
-        g_right(m, 0, None, img, ty ^ 2, to_y).wait_recv()
-        g_right(m, 3, None, img, ty ^ 2, to_x).start()
-        g_right(m, 4, None, img, ty ^ 2, to_c).start()
+
+    def gl_across(m):
         g_left(m, 1, None, img, ty ^ 2, to_y).wait_recv()
         g_left(m, 5, None, img, ty ^ 2, to_c).start()
-        g_right(m, 1, None, other, ty, to_x).wait_recv()
+
+    def gr_hop(m):
+        if m != 1:
+            g_right(m, 0, None, img, ty ^ 2, to_y).wait_recv()
+            g_right(m, 3, None, img, ty ^ 2, to_x).start()
+        g_right(m, 4, None, img, ty ^ 2, to_c).start()
+        if m != 1:
+            g_right(m, 1, None, other, ty, to_x).wait_recv()
+        else:
+            for k in range(4):
+                gu_wait(1, k)
         g_right(m, 5, None, other, ty, to_c).start()
 
-    def g_hop2(m):
+    def gl_hop2(m):
         g_left(m, 3, None, other, ty ^ 2, to_y).wait_recv()
         g_left(m, 6, None, other, ty ^ 2, to_c).start()
-        g_right(m, 3, None, other, ty ^ 2, to_x).wait_recv()
+
+    def gr_hop2(m):
+        if m != 1:
+            g_right(m, 3, None, other, ty ^ 2, to_x).wait_recv()
+        else:
+            for k in range(4):
+                gu_wait(2, k)
         g_right(m, 6, None, other, ty ^ 2, to_c).start()
 
     def g_done(m):
@@ -810,19 +893,24 @@
             copy.wait()
 
     def g_drain(m):
-        for copy in g_first(m):
-            copy.wait_send()
+        for k, copy in enumerate(g_first(m)):
+            if m != 1 or k not in (1, 3):
+                copy.wait_send()
         for k, i, t in ((3, other, ty), (4, other, ty), (5, img, ty ^ 2), (6, other, ty ^ 2)):
             g_left(m, k, None, i, t, to_c).wait_send()
         for k, i, t in ((3, img, ty ^ 2), (4, img, ty ^ 2), (5, other, ty), (6, other, ty ^ 2)):
-            g_right(m, k, None, i, t, to_c).wait_send()
+            if m != 1 or k != 3:
+                g_right(m, k, None, i, t, to_c).wait_send()
+        if m == 1:
+            for w in range(3):
+                for k in range(4):
+                    gu_copy(w, k).wait_send()
 
     attn = jnp.concatenate(
         [attn_in[:, h * PAD : h * PAD + HEAD].astype(F32) for h in range(16)], axis=1
     )
     l_attn[...] = attn.astype(BF16)
     put_halves(l_attns, attn)
-    hop_arrived(5, 6)
     own(OUT).wait()
     w_done(0)
     own_valid = tile_layout(b)[0]
@@ -834,7 +922,6 @@
         branchv[:, at] = dot(l_attn[...], woutv[:, at])
 
     loop(0, 3, project)
-    x_arrived(10)
     x = tok[...].astype(F32)
     x1 = x + keep * gate1() * branchv[...]
     x1v[...] = x1
@@ -874,17 +961,26 @@
         first = lax.rem(2 * img + k, 4) * (hidden // 4)
         loop(0, hidden // 4 // step, lambda j: mlp(first + j * step))
 
+    gl_x(1)
     w_done(1, 2)
     mlp_quarter(0)
-    hop_arrived(7, 8, 9)
+    gu_copy(1, 0).start()
+    far_arrived(7)
+    hop_arrived(8, 9)
     w_done(3, 4)
     mlp_quarter(1)
+    gu_copy(1, 1).start()
     hop_arrived(10)
+    far_arrived(8, 9)
     w_done(5, 6, 7)
     mlp_quarter(2)
+    gu_copy(1, 2).start()
+    gu_copy(0, 0).start()
+    far_arrived(10)
     w_done(8, 9, 10)
     mlp_quarter(3)
-    g_x(1)
+    gu_copy(1, 3).start()
+    gu_copy(0, 1).start()
     ffn = ffnv[...]
     g = cot[...].astype(F32)
     x1 = x1v[...]
@@ -927,15 +1023,27 @@
 
     loop(1, 16, lambda k: do_copy(lax.rem(b + k, 16)).start())
     do_in[b] = attn_send[b]
-    g_yc(1)
-    x_arrived(11, 12)
+    gu_copy(0, 2).start()
+    gu_copy(0, 3).start()
+    x_arrived(11)
+    gl_yc(1)
+    gl_hop(1)
+    gr_yc(1)
+    gu_hop(0)
+    gu_hop(1)
+    gl_x(2)
+    gl_yc(2)
+    gr_yc(0)
+    gr_yc(2)
+    gl_yc(0)
 
     def do_wait(k):
         p = lax.rem(b + k, 16)
         rcopy(attn_send.at[p], do_in.at[p], do_s.at[p], do_r.at[p], dev_tile(p)).wait()
 
     loop(1, 16, do_wait)
-    hop_arrived(11, 12)
+    gu_hop(2)
+    x_arrived(12)
 
     def delta(t):
         d = do_in[t].astype(F32)
@@ -945,63 +1053,12 @@
         dot_t[:, pl.ds(pl.multiple_of(t * TILE, TILE), TILE)] = d.T.astype(BF16)
 
     loop(0, 16, delta)
+    gu_hop(3)
+    gr_x(0)
+    gl_x(0)
+    gr_x(2)
+    gl_hop(2)
     dqt[...] = jnp.zeros_like(dqt)
-
-    def attend_back(k):
-        two = pl.ds(2 * k, 2)
-        p = jnp.exp(dot(ka[two].reshape(2 * TILE, PAD), qt[...]))
-        ds = (p * dot(va[two].reshape(2 * TILE, PAD), dot_t[...])).astype(BF16)
-        dkv[two] = dot(ds, qa[...].reshape(16 * TILE, PAD)).reshape(2, TILE, PAD)
-        dvv[two] = dot(p.astype(BF16), do_in[...].reshape(16 * TILE, PAD)).reshape(2, TILE, PAD)
-        at = pl.ds(pl.multiple_of(k * 2 * TILE, 2 * TILE), 2 * TILE)
-        dqt[...] += dot(kt[:, at], ds)
-
-    loop(0, 4, attend_back)
-    g_hop(1)
-    g_x(0)
-    g_x(2)
-    loop(4, 8, attend_back)
-
-    w_done(11, 12)
-    for i in range(len(chunks)):
-        w_drain(i)
-    gain_grad[...] = jnp.zeros_like(gain_grad)
-
-    def dq_rows(t):
-        return wdownv.at[pl.ds(pl.multiple_of(t * TILE, TILE), TILE), pl.ds(3 * PAD, 2 * PAD)]
-
-    def dq_copy(t):
-        return rcopy(dq_rows(t), dqkv_in.at[b], dq_s.at[t], dq_r.at[b], dev_tile(t))
-
-    def heads_back(t):
-        c = cosv[t]
-        s1, s2 = split_sin(sinv[t])
-
-        def norm_back(d, v, gain, row):
-            rr = lax.rsqrt(jnp.sum(v * v, axis=1, keepdims=True) * (1.0 / HEAD) + EPS)
-            n = v * rr
-            gain_grad[row : row + 1, :] += colsum(d * n)
-            dn = d * gain[0:1, :]
-            return rr * (dn - n * (jnp.sum(dn * n, axis=1, keepdims=True) * (1.0 / HEAD)))
-
-        d_q = dqt[:, pl.ds(pl.multiple_of(t * TILE, TILE), TILE)].T * HEAD ** (-0.5)
-        d_q = norm_back(unrope(d_q, c, s1, s2), qraw[t], q_gain, 0)
-        d_k = norm_back(unrope(dkv[t], c, s1, s2), kraw[t], k_gain, 1)
-        d_v = jnp.where(lane < HEAD, dvv[t], 0.0)
-        at = pl.ds(pl.multiple_of(t * TILE, TILE), TILE)
-        wdownv[at, 0 : 3 * PAD] = jnp.concatenate([d_q, d_k, d_v], axis=1).astype(BF16)
-        wdownv[at, 3 * PAD : 5 * PAD] = jnp.concatenate(
-            [d_q[:, 0:HEAD], d_k[:, 0:HEAD], d_v[:, 0:HEAD], zeros[:, 0:40]], axis=1
-        ).astype(BF16)
-
-        @pl.when(t != b)
-        def _():
-            dq_copy(t).start()
-
-    loop(0, 16, heads_back)
-    dqkv_in[b] = dq_rows(b)[...]
-    g_yc(0)
-    g_yc(2)
 
     high, low = z // 2, lax.rem(z, 2)
     l0 = 3 * width
@@ -1027,7 +1084,7 @@
         if m == 0:
             sent = [kt.at[pl.ds(0, 80), pl.ds(0, 12 * PAD)], qt.at[pl.ds(0, 80), pl.ds(0, 12 * PAD)]]
         elif m == 1:
-            sent = [tok_all.at[pl.ds(0, half), pl.ds(k * 3 * PAD, 3 * PAD)] for k in range(2)]
+            sent = [wupv.at[pl.ds(k * half, half), pl.ds(44 * PAD, 3 * PAD)] for k in range(2)]
         else:
             sent = [tok_all.at[pl.ds(640 + 128 * k, 80), pl.ds(0, 5 * PAD)] for k in range(2)]
         return [
@@ -1038,7 +1095,7 @@
     za, zb = (za_down, za_up, za_out), (zb_down, zb_up, zb_out)
     z_rest = (
         dot_t.at[pl.ds(0, 80), pl.ds(0, 12 * PAD)],
-        tok_all.at[pl.ds(0, half), pl.ds(6 * PAD, 3 * PAD)],
+        wdownv.at[pl.ds(19 * TILE, half), pl.ds(0, 3 * PAD)],
         tok_all.at[pl.ds(896, 80), pl.ds(0, 5 * PAD)],
     )
     z_own = (dqt.at[pl.ds(0, 80), pl.ds(0, 12 * PAD)], up_grad, z_out)
@@ -1095,6 +1152,95 @@
         z_copy2(m).wait()
         z_own[m][...] += zb[m][...].astype(F32)
 
+    gain_grad[...] = jnp.zeros_like(gain_grad)
+    for i in range(11):
+        w_drain(i)
+
+    def kv_send(k, u):
+        at = pl.ds(pl.multiple_of(k * 2 * HEAD, 16), 2 * HEAD)
+        return wdownv.at[at, pl.ds((3 + u) * PAD, PAD)]
+
+    def q_send(k, u):
+        at = pl.ds(pl.multiple_of(width + k * 80, 16), 80)
+        return wdownv.at[at, pl.ds((3 + u) * PAD, PAD)]
+
+    def kv_copy(k, u):
+        t = 2 * k + u
+        return rcopy(kv_send(k, u), dkv_in.at[b], dkv_s.at[t], dkv_r.at[b], dev_tile(t))
+
+    def q_copy(k, u):
+        t = 2 * k + u
+        return rcopy(q_send(k, u), dq_in.at[b], dq_s.at[t], dq_r.at[b], dev_tile(t))
+
+    def head_back(d, v, gain, row, t):
+        c_, (s1, s2) = cosv[t], split_sin(sinv[t])
+        d = unrope(d, c_, s1, s2)
+        rr = lax.rsqrt(jnp.sum(v * v, axis=1, keepdims=True) * (1.0 / HEAD) + EPS)
+        n = v * rr
+        gain_grad[row : row + 1, :] += colsum(d * n)
+        dn = d * gain[0:1, :]
+        return rr * (dn - n * (jnp.sum(dn * n, axis=1, keepdims=True) * (1.0 / HEAD)))
+
+    def send_tile(k, u, copy, keep_own):
+        copy_ = copy(k, u)
+
+        @pl.when(2 * k + u != b)
+        def _():
+            copy_.start()
+
+        @pl.when(2 * k + u == b)
+        def _():
+            keep_own[b] = copy_.src_ref[...]
+
+    def attend_back(k):
+        two = pl.ds(2 * k, 2)
+        p = jnp.exp(dot(ka[two].reshape(2 * TILE, PAD), qt[...]))
+        ds = (p * dot(va[two].reshape(2 * TILE, PAD), dot_t[...])).astype(BF16)
+        d_k2 = dot(ds, qa[...].reshape(16 * TILE, PAD))
+        d_v2 = dot(p.astype(BF16), do_in[...].reshape(16 * TILE, PAD))
+        at = pl.ds(pl.multiple_of(k * 2 * TILE, 2 * TILE), 2 * TILE)
+        dqt[...] += dot(kt[:, at], ds)
+        for u in range(2):
+            t = 2 * k + u
+            rows = slice(u * TILE, (u + 1) * TILE)
+            d_k = head_back(d_k2[rows], kraw[t], k_gain, 1, t)
+            d_v = jnp.where(lane < HEAD, d_v2[rows], 0.0)
+            at = pl.ds(pl.multiple_of(t * TILE, TILE), TILE)
+            wdownv[at, PAD : 3 * PAD] = jnp.concatenate([d_k, d_v], axis=1).astype(BF16)
+            turned = jnp.concatenate([d_k.T[0:HEAD], d_v.T[0:HEAD]], axis=0)
+            kv_send(k, u)[...] = turned.astype(BF16)
+            send_tile(k, u, kv_copy, dkv_in)
+
+    loop(0, 4, attend_back)
+    gl_across(1)
+    gr_hop(1)
+    hop_arrived(11)
+    loop(4, 8, attend_back)
+    gl_hop2(1)
+    gr_hop2(1)
+    g_done(1)
+    z_load(1)
+    z_product(1)
+    gl_hop(0)
+    gr_hop(0)
+
+    def heads_back(k):
+        for u in range(2):
+            t = 2 * k + u
+            at = pl.ds(pl.multiple_of(t * TILE, TILE), TILE)
+            d_q = dqt[:, at].T * HEAD ** (-0.5)
+            d_q = head_back(d_q, qraw[t], q_gain, 0, t)
+            wdownv[at, 0:PAD] = d_q.astype(BF16)
+            q_send(k, u)[...] = d_q.T[0:80].astype(BF16)
+            send_tile(k, u, q_copy, dq_in)
+
+    loop(0, 8, heads_back)
+    gr_hop(2)
+    w_done(11, 12)
+    w_drain(11)
+    w_drain(12)
+
+
     sums_t = (branchv, ffnv, dh2v)
     for ref in sums_t:
         ref[...] = jnp.zeros((PAD, width), F32)
@@ -1106,20 +1252,18 @@
             sums_t[p][...] += term[p * PAD : (p + 1) * PAD]
 
     loop(0, 8, dw_rows)
+    half_pad = jnp.zeros((80, 5 * PAD - half), F32)
     for p in range(3):
-        wdownv[0:width, (5 + p) * PAD : (6 + p) * PAD] = sums_t[p][...].T.astype(BF16)
+        for i in range(2):
+            piece = sums_t[p][0:80, i * half : (i + 1) * half]
+            at = slice((3 * i + p) * 80, (3 * i + p + 1) * 80)
+            tok_all[at, 0 : 5 * PAD] = jnp.concatenate([piece, half_pad], axis=1).astype(BF16)
 
     def dw_half(i):
-        return wdownv.at[pl.ds(pl.multiple_of(i * half, 64), half), pl.ds(5 * PAD, 3 * PAD)]
+        return tok_all.at[pl.ds(pl.multiple_of(i * 240, 16), 240), pl.ds(0, 5 * PAD)]
 
     dw_copy = rcopy(dw_half(other), dw_in, dw_sem.at[0], dw_sem.at[1], dev(i=other))
     dw_copy.start()
-    g_hop2(1)
-    g_done(1)
-    z_load(1)
-    z_product(1)
-    g_hop(0)
-    g_hop(2)
 
     loads = [
         pltpu.make_async_copy(
@@ -1134,19 +1278,31 @@
 
     def dq_wait(k):
         p = lax.rem(b + k, 16)
-        rcopy(dq_rows(p), dqkv_in.at[p], dq_s.at[p], dq_r.at[p], dev_tile(p)).wait()
-
+        kv, q_ = dkv_in.at[p], dq_in.at[p]
+        rcopy(kv, kv, dkv_s.at[p], dkv_r.at[p], dev_tile(p)).wait()
+        rcopy(q_, q_, dq_s.at[p], dq_r.at[p], dev_tile(p)).wait()
+
+    z_second(1)
     loop(1, 16, dq_wait)
+    for m in (0, 2):
+        gl_across(m)
+        gl_hop2(m)
+        gr_hop2(m)
+    g_done(0)
+    z_load(0)
+    z_product(0)
     for load in loads:
         load.wait()
-    dqkv = [dqkv_in[h].astype(F32) for h in range(16)]
+
     def own_part(p):
         return slice(16 * TILE + p * TILE, 16 * TILE + (p + 1) * TILE)
 
     for p in range(3):
-        wdownv[own_part(p), :] = jnp.concatenate(
-            [dqkv[h][:, p * HEAD : (p + 1) * HEAD] for h in range(16)], axis=1
-        ).astype(BF16)
+        got, r0 = (dq_in, 0) if p == 0 else (dkv_in, (p - 1) * HEAD)
+        turned = jnp.concatenate(
+            [got[h].astype(F32)[r0 : r0 + HEAD] for h in range(16)], axis=0
+        )
+        wdownv[own_part(p), :] = turned.T.astype(BF16)
 
     def h1_back(k):
         at = pl.ds(pl.multiple_of(k * cols, PAD), cols)
@@ -1177,20 +1333,17 @@
     loop(1, 32, lambda k: dm_copy(lax.rem(me + k, 32)).start())
     dbuf[me] = dsend[me]
 
-    z_second(1)
-    for m in (0, 2):
-        g_hop2(m)
-        g_done(m)
-        z_load(m)
-        z_product(m)
+    g_done(2)
+    z_load(2)
+    z_product(2)
     dw_copy.wait()
     dw_sum = dw_half(img)[...].astype(F32) + dw_in[...].astype(F32)
 
     def pc_send(p):
-        return wdownv.at[pl.ds(width, half), pl.ds((5 + p) * PAD, PAD)]
+        return tok_all.at[pl.ds(1024 + 80 * p, 80), pl.ds(0, 5 * PAD)]
 
     for p in range(3):
-        pc_send(p)[...] = dw_sum[:, p * PAD : (p + 1) * PAD].astype(BF16)
+        pc_send(p)[...] = dw_sum[80 * p : 80 * (p + 1)].astype(BF16)
 
     def pc_copy(p):
         group = 16 * p + b
@@ -1210,12 +1363,14 @@
         def _():
             pc_in[lax.rem(16 * p + b, 3)] = pc_send(p)[...]
 
-    for m in (0, 2):
-        z_second(m)
-    for m in (1, 0, 2):
-        z_last(m)
-    for m in range(3):
-        g_drain(m)
+    z_second(0)
+    z_second(2)
+    z_last(1)
+    z_last(0)
+    z_last(2)
+    g_drain(0)
+    g_drain(1)
+    g_drain(2)
     down_grad[...] = z_own[0][0:HEAD, :]
     out_grad[...] = z_own[2][0:HEAD, 0:half]
     for slot in range(3):
@@ -1230,7 +1385,7 @@
 
     for slot in range(3):
         at = slice(slot * HEAD, (slot + 1) * HEAD)
-        qkv_grad[at, :] = pc_in[slot].astype(F32).T[0:HEAD, :]
+        qkv_grad[at, :] = pc_in[slot].astype(F32)[0:HEAD, 0:half]
     for p in range(3):
         to, copy = pc_copy(p)
 
@@ -1323,11 +1478,10 @@
         v(tile16, BF16),
         v((PAD, 16 * TILE), BF16),
         v((PAD, 16 * TILE), F32),
-        v(tile16, F32),
-        v(tile16, F32),
-        v((16, TILE, 2 * PAD), BF16),
-        v((half, 3 * PAD), BF16),
-        v((3, half, PAD), BF16),
+        v((16, 2 * HEAD, PAD), BF16),
+        v((16, 80, PAD), BF16),
+        v((240, 5 * PAD), BF16),
+        v((3, 80, 5 * PAD), BF16),
         v((TILE, width), F32),
         v((TILE, width), F32),
         v((TILE, width), F32),
@@ -1355,6 +1509,8 @@
         dma((3, 8)),
         dma((3, 8)),
         dma((3, 8)),
+        dma((3, 4)),
+        dma((3, 4)),
         dma((3, 2)),
         dma((3, 2)),
         dma((3, 2)),
@@ -1364,13 +1520,15 @@
         dma((16, 4)),
         dma((16,)),
         dma,
-        dma((n_chunks, 4)),
-        dma((n_chunks, 4)),
+        dma((n_chunks, 10)),
+        dma((n_chunks, 10)),
         dma((4,)),
         dma((2,)),
         dma((2,)),
         dma((32,)),
         dma((32,)),
+        dma((16,)),
+        dma((16,)),
         dma((16,)),
         dma((16,)),
         dma((16,)),

time: 290 us -> 258 us (0.89)
  Pallas kernels: 268 us -> 236 us
    pallas_call x1, Pallas kernels: 268 us -> 236 us  [run_block(): pl.pallas_call(block_kernel, out_shape=out_shape, in_specs=[vmem] * 5 + [...]
where the time goes in v4:
time: 258 us; the launch traced here: 257 us
  Pallas kernels  236 us (91%)
  local copies, waits for them, and re-layouts  16.5 us (6%)
  between operations  2.63 us (1%)
    pallas_call x1, Pallas kernels, run_block(): pl.pallas_call(block_kernel, out_shape=out_shape, in_specs=[vmem] * 5 + [...  236 us
    unnamed x11, local copies, waits for them, and re-layouts  10.7 us

profile of v4, /device:TPU:0, one launch (start us, length us, event | category | flops | bytes accessed | tf_op | source)
XLA Modules:
  0.0 257.1 jit_solution(5718191575169649933)
XLA Ops:
  2.6 0.6 pad_add_fusion.hw
  3.2 0.7 pad.20
  3.8 0.7 pad.21
  4.5 0.6 broadcast_in_dim.34.k_gain
  5.1 0.6 broadcast_in_dim.33.q_gain
  5.7 0.1 fusion.6
  5.8 0.8 convert_reduce_fusion
  6.6 0.6 broadcast_in_dim.32.act
  7.2 1.3 constant_dynamic-slice_fusion.2
  8.5 0.9 fusion.5.wh
  9.4 235.7 %shard_map.205 = (bf16[128,1152]{1,0:T(8,128)(2,1)}, bf16[128,1152]{1,0:T(8,128)(2,1)}, f32[216,576]{1,0:T(8,128)}, f32[216,1152]{1,0:T(8,128)}, f32[8,128]{1,0:...) custom-call(bf16[128,1152]{1,0:T(8,128)(2,1)} %bitcast.16, ...), custom_call_target="tpu_custom_call" | custom-call | tf_op jit(solution)/shard_map/pallas_call | solution.py:1545
  245.1 0.0 copy-start.1
  245.1 0.0 copy-start
  245.1 1.3 slice_bitcast_fusion
  246.4 1.7 copy.33
  248.1 1.7 copy.34
  249.8 1.9 copy.35
  251.7 1.6 copy.36
  253.3 2.1 copy.37
  255.4 0.0 copy-done.1
  255.4 0.8 copy.38
  256.2 0.0 copy-done
  256.2 0.9 copy.39
Async XLA Ops:
  245.1 10.4 %copy-start.1 = (f32[72,1536]{1,0:T(8,128)S(1)}, f32[72,1536]{1,0:T(8,128)}, u32[]{:S(2)}) copy-start(f32[72,1536]{1,0:T(8,128)} %get-tuple-element.22) | copy-start | bytes 1327108
  245.1 11.1 %copy-start = (f32[216,1152]{1,0:T(8,128)S(1)}, f32[216,1152]{1,0:T(8,128)}, u32[]{:S(2)}) copy-start(f32[216,1152]{1,0:T(8,128)} %get-tuple-element.47) | copy-start | bytes 2985988

commit v5 on v4

--- a/solution.py
+++ b/solution.py
@@ -360,10 +360,10 @@
 
 
 def block_kernel(
-    tok, cot, act, ada, wh, wout, wup, wdown, wqkv, q_gain, k_gain, tab, hw,
+    tok, cot, act_row, ada, wout, wup, wdown, wqkv, q_gain_row, k_gain_row, tab, grid_h, grid_w,
     mixed, tgrad, qkv_grad, ada_grad, gain_grad, down_grad, up_grad, out_grad, qkv_hbm,
     lb_down, lb_up, lb_out, rb_down, rb_up, rb_out,
-    tok_all, whv, woutv, wupv, wdownv, actbuf, modsend, modbuf, modv,
+    act, q_gain, k_gain, win, win_sem, tok_all, whv, woutv, wupv, wdownv, actbuf, modsend, modbuf, modv,
     cosv, sinv, qraw, kraw, qa, ka, va, kt, qt, onorm, attn_send, attn_in,
     do_in, dot_t, dqt, dkv_in, dq_in, dw_in, pc_in,
     x1v, branchv, ffnv, dh2v, dmod, dsend, dbuf,
@@ -530,22 +530,43 @@
         rows = hbm[m].shape[0]
         return pltpu.make_async_copy(hbm[m], vm[m].at[pl.ds(img * rows, rows)], w_loc.at[m])
 
+    act[...] = jnp.broadcast_to(act_row[...], (8, width))
+    gain_pad = jnp.zeros((1, PAD - HEAD), F32)
+    q_gain[...] = jnp.concatenate([q_gain_row[...], gain_pad], axis=1)
+    k_gain[...] = jnp.concatenate([k_gain_row[...], gain_pad], axis=1)
+
+    def window(p):
+        first = p * width + b * HEAD
+        start = jnp.minimum(first // PAD * PAD, 3 * width - 2 * PAD)
+        return pl.multiple_of(start, PAD), first - start
+
+    wins = [
+        pltpu.make_async_copy(
+            wqkv.at[:, pl.ds(window(p)[0], 2 * PAD)], win.at[p], win_sem.at[p]
+        )
+        for p in range(3)
+    ]
+    for copy in wins:
+        copy.start()
     act_copy = rcopy(act, actbuf.at[img], act_sem.at[0], act_sem.at[1], dev(i=other))
     act_copy.start()
     actbuf[img] = act[...]
-    wh_copy = rcopy(wh, whv.at[pl.ds(img * half, half)], wh_sem.at[0], wh_sem.at[1], dev(i=other))
+    own_wh = whv.at[pl.ds(pl.multiple_of(img * half, 64), half)]
+    wh_copy = rcopy(own_wh, own_wh, wh_sem.at[0], wh_sem.at[1], dev(i=other))
     for i in range(3):
         w_x(i).start()
-    whv[pl.ds(pl.multiple_of(img * half, 64), half), :] = wh[...]
 
     def tok_at(chunk):
         return tok_all.at[pl.ds(pl.multiple_of(chunk * TILE, TILE), TILE)]
 
-    def t_send(src, chunk, way, d):
-        return rcopy(src, tok_at(chunk), tok_send.at[chunk, way], tok_recv.at[chunk], d)
-
-    def t_wait(chunk):
-        t_send(tok, chunk, 0, dev(t=ty ^ 1)).wait_recv()
+    def tok_half(q):
+        return tok_all.at[pl.ds(pl.multiple_of(q * 64, 64), 64)]
+
+    def t_send(src, q, way, d):
+        return rcopy(src, tok_half(q), tok_send.at[q, way], tok_recv.at[q], d)
+
+    def t_wait(q):
+        t_send(tok_half(q), q, 0, to_c).wait_recv()
 
     tok_own = pltpu.make_async_copy(tok, tok_at(b), tok_loc)
     tok_own.start()
@@ -566,7 +587,8 @@
         t_send(src, chunk, 2, dev(t=ty ^ 2)).start()
         t_send(src, chunk, 3, dev(t=ty ^ 1)).start()
 
-    t_forward(tok, b, True, True)
+    for h in range(2):
+        t_forward(tok.at[pl.ds(64 * h, 64)], 2 * b + h, True, True)
     for m in range(3):
         own(m).start()
 
@@ -579,52 +601,61 @@
 
     loop(1, 32, lambda k: mod_copy(lax.rem(me + k, 32)).start())
     modbuf[me] = modsend[img]
+    for p in range(3):
+        wins[p].wait()
+        shift = 2 * PAD - window(p)[1]
+        cols_p = pltpu.roll(win[p].astype(F32), shift, 1)[:, 0:PAD]
+        at_lane = lax.broadcasted_iota(jnp.int32, (half, PAD), 1)
+        own_wh[:, p * PAD : (p + 1) * PAD] = jnp.where(at_lane < HEAD, cols_p, 0.0).astype(BF16)
     wh_copy.start()
     for i in range(3, len(chunks)):
         w_x(i).start()
 
     for s in (1, 2, 3):
-
-        @pl.when(z - s >= 0)
-        def _():
-            t_wait(b - s)
-            t_forward(tok_at(b - s), b - s, True, False)
-
-        @pl.when(z + s <= 3)
-        def _():
-            t_wait(b + s)
-            t_forward(tok_at(b + s), b + s, False, True)
+        for h in range(2):
+
+            @pl.when(z - s >= 0)
+            def _():
+                q = 2 * (b - s) + h
+                t_wait(q)
+                t_forward(tok_half(q), q, True, False)
+
+            @pl.when(z + s <= 3)
+            def _():
+                q = 2 * (b + s) + h
+                t_wait(q)
+                t_forward(tok_half(q), q, False, True)
 
     x_arrived(0, 1, 2)
 
-    def t_y(zz):
-        chunk = (ty ^ 2) * 4 + zz
-        t_wait(chunk)
-        t_send(tok_at(chunk), chunk, 3, dev(t=ty ^ 1)).start()
-
-    loop(0, 4, t_y)
+    def t_y(k):
+        q = (ty ^ 2) * 8 + k
+        t_wait(q)
+        t_send(tok_half(q), q, 3, to_c).start()
+
+    loop(0, 8, t_y)
     hop_arrived(0)
-    loop(0, 4, lambda zz: t_wait((ty ^ 1) * 4 + zz))
-    loop(0, 4, lambda zz: t_wait((ty ^ 3) * 4 + zz))
-
-    def t_drain(zz):
-        chunk = ty * 4 + zz
-        ref = tok_at(chunk)
+    loop(0, 8, lambda k: t_wait((ty ^ 1) * 8 + k))
+    loop(0, 8, lambda k: t_wait((ty ^ 3) * 8 + k))
+
+    def t_drain(k):
+        q, zz = ty * 8 + k, k // 2
+        ref = tok_half(q)
 
         @pl.when((zz <= z) & (z < 3))
         def _():
-            t_send(ref, chunk, 0, dev(t=ty ^ 1)).wait_send()
+            t_send(ref, q, 0, to_c).wait_send()
 
         @pl.when((zz >= z) & (z > 0))
         def _():
-            t_send(ref, chunk, 1, dev(t=ty ^ 1)).wait_send()
-
-        t_send(ref, chunk, 2, dev(t=ty ^ 1)).wait_send()
-        t_send(ref, chunk, 3, dev(t=ty ^ 1)).wait_send()
-        away = (ty ^ 2) * 4 + zz
-        t_send(tok_at(away), away, 3, dev(t=ty ^ 1)).wait_send()
-
-    loop(0, 4, t_drain)
+            t_send(ref, q, 1, to_c).wait_send()
+
+        t_send(ref, q, 2, to_c).wait_send()
+        t_send(ref, q, 3, to_c).wait_send()
+        away = (ty ^ 2) * 8 + k
+        t_send(tok_half(away), away, 3, to_c).wait_send()
+
+    loop(0, 8, t_drain)
     tok_own.wait()
 
     def mod_wait(k):
@@ -641,7 +672,7 @@
     ]
     wh_copy.wait()
 
-    height, wide = hw[0], hw[1]
+    height, wide = grid_h[0], grid_w[0]
     local = lax.broadcasted_iota(jnp.int32, (TILE, PAD), 0)
     lane = lax.broadcasted_iota(jnp.int32, (TILE, PAD), 1)
 
@@ -707,11 +738,10 @@
     loop(0, 8, head_rows)
     x_arrived(5, 6)
     hop_arrived(3, 4)
-    far_arrived(1, 2)
     loop(8, 16, head_rows)
     x_arrived(7)
+    far_arrived(1, 2)
     hop_arrived(5, 6)
-    far_arrived(3, 4)
 
     def head_lanes(h):
         return attn_in.at[:, pl.ds(pl.multiple_of(h * PAD, PAD), PAD)]
@@ -743,8 +773,8 @@
     loop(0, 8, attend)
     head_lanes(b)[...] = attn_send[b]
     x_arrived(8, 9, 10)
+    far_arrived(3, 4)
     hop_arrived(7)
-    far_arrived(5, 6)
 
     def at_wait(k):
         p = lax.rem(b + k, 16)
@@ -922,6 +952,7 @@
         branchv[:, at] = dot(l_attn[...], woutv[:, at])
 
     loop(0, 3, project)
+    far_arrived(5, 6)
     x = tok[...].astype(F32)
     x1 = x + keep * gate1() * branchv[...]
     x1v[...] = x1
@@ -1215,12 +1246,13 @@
     gl_across(1)
     gr_hop(1)
     hop_arrived(11)
-    loop(4, 8, attend_back)
+    loop(4, 6, attend_back)
     gl_hop2(1)
     gr_hop2(1)
     g_done(1)
     z_load(1)
     z_product(1)
+    loop(6, 8, attend_back)
     gl_hop(0)
     gr_hop(0)
 
@@ -1427,7 +1459,7 @@
     return table.astype(np.float32)
 
 
-def run_block(tokens, cotangent, act, ada, wh, wout, wup, wdown, wqkv, q_gain, k_gain, hw):
+def run_block(tokens, cotangent, act, ada, wout, wup, wdown, wqkv, q_gain, k_gain, grid_h, grid_w):
     width, hidden = tokens.shape[1], wup.shape[1] // 2
     half, part = width // 2, ada.shape[0]
     vmem, any_ = pl.BlockSpec(memory_space=pltpu.VMEM), pl.BlockSpec(memory_space=pl.ANY)
@@ -1454,6 +1486,11 @@
         sds((8 * TILE, 8 * PAD), BF16),
     )
     scratch = [
+        v((8, width), F32),
+        v((1, PAD), F32),
+        v((1, PAD), F32),
+        v((3, half, 2 * PAD), BF16),
+        dma((3,)),
         v((16 * TILE, width), BF16),
         v((width, 3 * PAD), BF16),
         v((width, width), BF16),
@@ -1517,8 +1554,8 @@
         dma((3,)),
         dma((3,)),
         dma((2,)),
-        dma((16, 4)),
-        dma((16,)),
+        dma((32, 4)),
+        dma((32,)),
         dma,
         dma((n_chunks, 10)),
         dma((n_chunks, 10)),
@@ -1545,22 +1582,16 @@
     return pl.pallas_call(
         block_kernel,
         out_shape=out_shape,
-        in_specs=[vmem] * 5 + [any_] * 4 + [vmem] * 3 + [smem],
+        in_specs=[vmem] * 4 + [any_] * 4 + [vmem] * 3 + [smem] * 2,
         out_specs=[vmem] * 8 + [any_] * 7,
         scratch_shapes=scratch,
         compiler_params=pltpu.CompilerParams(
             collective_id=0, has_side_effects=True, vmem_limit_bytes=VMEM_LIMIT
         ),
-    )(tokens, cotangent, act, ada, wh, wout, wup, wdown, wqkv, q_gain, k_gain, rope_table(), hw)
-
-
-def head_weight(weight):
-    at = lax.axis_index(("ty", "tx")) * HEAD
-    width = weight.shape[1] // 3
-    parts = [
-        lax.dynamic_slice_in_dim(weight, p * width + at, HEAD, axis=1) for p in range(3)
-    ]
-    return jnp.concatenate([jnp.pad(p, ((0, 0), (0, PAD - HEAD))) for p in parts], axis=1)
+    )(
+        tokens, cotangent, act, ada, wout, wup, wdown, wqkv, q_gain, k_gain, rope_table(),
+        grid_h, grid_w,
+    )
 
 
 def fast_body(
@@ -1580,21 +1611,20 @@
 ):
     width = tokens.shape[2]
     act = jax.nn.silu(class_embed + time_embed(timestep, width)).astype(BF16).astype(F32)
-    pad = lambda g: jnp.broadcast_to(jnp.pad(g, (0, PAD - HEAD))[None], (8, PAD))
     (mixed, tgrad, qkv_grad, ada_grad, gains, down_grad, up_grad, out_grad) = (
         run_block(
             tokens[0],
             cotangent[0],
-            jnp.broadcast_to(act, (8, width)),
+            act,
             ada_weight,
-            head_weight(qkv_weight),
             out_weight,
             up_weight,
             down_weight,
             qkv_weight,
-            pad(q_gain),
-            pad(k_gain),
-            jnp.concatenate([grid_height, grid_width]),
+            q_gain[None],
+            k_gain[None],
+            grid_height,
+            grid_width,
         )[:8]
     )
     return (

time: 258 us -> 247 us (0.957)
  local copies, waits for them, and re-layouts: 16.5 us -> 10.9 us
  Pallas kernels: 236 us -> 232 us
    pallas_call x1, Pallas kernels: 236 us -> 232 us  [run_block(): pl.pallas_call(block_kernel, out_shape=out_shape, in_specs=[vmem] * 4 + [...]
    unnamed x11 -> x13, local copies, waits for them, and re-layouts: 10.7 us -> 9.52 us
where the time goes in v5:
time: 247 us
  Pallas kernels  232 us (94%)
  local copies, waits for them, and re-layouts  10.9 us (4%)
  between operations  2.62 us (1%)
    pallas_call x1, Pallas kernels, run_block(): pl.pallas_call(block_kernel, out_shape=out_shape, in_specs=[vmem] * 4 + [...  232 us
    unnamed x13, local copies, waits for them, and re-layouts  9.52 us

profile of v5, /device:TPU:0, one launch (start us, length us, event | category | flops | bytes accessed | tf_op | source)
XLA Modules:
  0.0 246.5 jit_solution(12541913881423374190)
XLA Ops:
  2.6 0.1 fusion
  2.7 1.4 convert_convert_fusion.act_row
  4.1 231.5 %shard_map.205 = (bf16[128,1152]{1,0:T(8,128)(2,1)}, bf16[128,1152]{1,0:T(8,128)(2,1)}, f32[216,576]{1,0:T(8,128)}, f32[216,1152]{1,0:T(8,128)}, f32[8,128]{1,0:...) custom-call(bf16[128,1152]{1,0:T(8,128)(2,1)} %bitcast.18, ...), custom_call_target="tpu_custom_call" | custom-call | tf_op jit(solution)/shard_map/pallas_call | solution.py:1582
  235.6 0.0 copy-start.1
  235.6 0.0 copy-start.2
  235.6 0.0 copy-start
  235.6 1.3 slice_bitcast_fusion
  237.0 1.7 copy.33
  238.7 1.7 copy.34
  240.4 1.9 copy.35
  242.3 1.6 copy.36
  243.9 0.0 copy-done.1
  243.9 0.9 copy.37
  244.8 0.0 copy-done.2
  244.8 0.8 copy.38
  245.6 0.0 copy-done
  245.6 0.9 copy.39
Async XLA Ops:
  235.6 8.3 %copy-start.1 = (f32[576,384]{1,0:T(8,128)S(1)}, f32[576,384]{1,0:T(8,128)}, u32[]{:S(2)}) copy-start(f32[576,384]{1,0:T(8,128)} %get-tuple-element.42) | copy-start | bytes 2654212
  235.6 9.2 %copy-start.2 = (f32[72,1536]{1,0:T(8,128)S(1)}, f32[72,1536]{1,0:T(8,128)}, u32[]{:S(2)}) copy-start(f32[72,1536]{1,0:T(8,128)} %get-tuple-element.22) | copy-start | bytes 1327108
  235.6 9.9 %copy-start = (f32[216,1152]{1,0:T(8,128)S(1)}, f32[216,1152]{1,0:T(8,128)}, u32[]{:S(2)}) copy-start(f32[216,1152]{1,0:T(8,128)} %get-tuple-element.44) | copy-start | bytes 2985988

commit v6 on v5

--- a/solution.py
+++ b/solution.py
@@ -603,7 +603,7 @@
     modbuf[me] = modsend[img]
     for p in range(3):
         wins[p].wait()
-        shift = 2 * PAD - window(p)[1]
+        shift = lax.rem(2 * PAD - window(p)[1], 2 * PAD)
         cols_p = pltpu.roll(win[p].astype(F32), shift, 1)[:, 0:PAD]
         at_lane = lax.broadcasted_iota(jnp.int32, (half, PAD), 1)
         own_wh[:, p * PAD : (p + 1) * PAD] = jnp.where(at_lane < HEAD, cols_p, 0.0).astype(BF16)
@@ -1131,8 +1131,12 @@
     )
     z_own = (dqt.at[pl.ds(0, 80), pl.ds(0, 12 * PAD)], up_grad, z_out)
 
-    def z_copy2(m):
-        return rcopy(z_rest[m], zb[m], zb_s.at[m], zb_r.at[m], dev(k=z ^ 2))
+    def z_copy2(m, part=0):
+        src, dst, k = z_rest[m], zb[m], m
+        if m == 1:
+            at = pl.ds(part * (half // 2), half // 2)
+            src, dst, k = src.at[at], dst.at[at], 1 + 2 * part
+        return rcopy(src, dst, zb_s.at[k], zb_r.at[k], dev(k=z ^ 2))
 
     def z_product(m):
         kl = l_all[m].shape[1]
@@ -1181,6 +1185,8 @@
 
     def z_last(m):
         z_copy2(m).wait()
+        if m == 1:
+            z_copy2(m, 1).wait()
         z_own[m][...] += zb[m][...].astype(F32)
 
     gain_grad[...] = jnp.zeros_like(gain_grad)
@@ -1323,6 +1329,7 @@
     g_done(0)
     z_load(0)
     z_product(0)
+    z_copy2(1, 1).start()
     for load in loads:
         load.wait()
 
@@ -1551,8 +1558,8 @@
         dma((3, 2)),
         dma((3, 2)),
         dma((3, 2)),
-        dma((3,)),
-        dma((3,)),
+        dma((4,)),
+        dma((4,)),
         dma((2,)),
         dma((32, 4)),
         dma((32,)),

time: 247 us -> 246 us (level)
  no operation moved by 1% of the time
where the time goes in v6:
time: 246 us; the launch traced here: 245 us
  Pallas kernels  230 us (93%)
  local copies, waits for them, and re-layouts  10.9 us (4%)
  between operations  2.62 us (1%)
    pallas_call x1, Pallas kernels, run_block(): pl.pallas_call(block_kernel, out_shape=out_shape, in_specs=[vmem] * 4 + [...  230 us
    unnamed x13, local copies, waits for them, and re-layouts  9.52 us

profile of v6, /device:TPU:0, one launch (start us, length us, event | category | flops | bytes accessed | tf_op | source)
XLA Modules:
  0.0 245.2 jit_solution(7308321509666755826)
XLA Ops:
  2.6 0.1 fusion
  2.7 1.4 convert_convert_fusion.act_row
  4.1 230.2 %shard_map.205 = (bf16[128,1152]{1,0:T(8,128)(2,1)}, bf16[128,1152]{1,0:T(8,128)(2,1)}, f32[216,576]{1,0:T(8,128)}, f32[216,1152]{1,0:T(8,128)}, f32[8,128]{1,0:...) custom-call(bf16[128,1152]{1,0:T(8,128)(2,1)} %bitcast.18, ...), custom_call_target="tpu_custom_call" | custom-call | tf_op jit(solution)/shard_map/pallas_call | solution.py:1589
  234.3 0.0 copy-start.1
  234.3 0.0 copy-start.2
  234.3 0.0 copy-start
  234.3 1.3 slice_bitcast_fusion
  235.7 1.7 copy.33
  237.4 1.7 copy.34
  239.1 1.9 copy.35
  241.0 1.6 copy.36
  242.6 0.0 copy-done.1
  242.6 0.9 copy.37
  243.5 0.0 copy-done.2
  243.5 0.8 copy.38
  244.2 0.0 copy-done
  244.3 0.9 copy.39
Async XLA Ops:
  234.3 8.3 %copy-start.1 = (f32[576,384]{1,0:T(8,128)S(1)}, f32[576,384]{1,0:T(8,128)}, u32[]{:S(2)}) copy-start(f32[576,384]{1,0:T(8,128)} %get-tuple-element.42) | copy-start | bytes 2654212
  234.3 9.2 %copy-start.2 = (f32[72,1536]{1,0:T(8,128)S(1)}, f32[72,1536]{1,0:T(8,128)}, u32[]{:S(2)}) copy-start(f32[72,1536]{1,0:T(8,128)} %get-tuple-element.22) | copy-start | bytes 1327108
  234.3 9.9 %copy-start = (f32[216,1152]{1,0:T(8,128)S(1)}, f32[216,1152]{1,0:T(8,128)}, u32[]{:S(2)}) copy-start(f32[216,1152]{1,0:T(8,128)} %get-tuple-element.44) | copy-start | bytes 2985988
